TPU v7x, 32 devices: a whole 2x2x4 slice. The times are simulated.
32 devices in a mesh: dp: 16 (over z, y, x), head: 2 (over core).
Axes of the slice: x: 2, y: 2, z: 4, core: 2. Of those that a mesh axis runs over, the one named last changes fastest.
Arguments:
- hidden_in: float32 [6144, 1536], P(('dp', 'head')), may hold values from -6 to 6
- row_lengths: int32 [16, 3], P('dp'), may hold values from 0 to 384, as said below
- norm_attn: bfloat16 [1536], P('dp'), may hold values from 0.099609375 to 1.8984375
- w_query: bfloat16 [1536, 1536], P('dp', 'head'), may hold values from -0.15625 to 0.15625
- b_query: bfloat16 [2, 768], P('head', 'dp'), may hold values from -3 to 3
- w_key: bfloat16 [1536, 256], P('dp', 'head'), may hold values from -0.15625 to 0.15625
- b_key: bfloat16 [2, 128], P('head', 'dp'), may hold values from -3 to 3
- w_value: bfloat16 [1536, 256], P('dp', 'head'), may hold values from -0.15625 to 0.15625
- b_value: bfloat16 [2, 128], P('head', 'dp'), may hold values from -0.59765625 to 0.59765625
- w_out: bfloat16 [1536, 1536], P('head', 'dp'), may hold values from -1.25 to 1.25
- norm_mlp: bfloat16 [1536], P('dp'), may hold values from 0.099609375 to 1.8984375
- w_gate: bfloat16 [1536, 8960], P('dp', 'head'), may hold values from -0.15625 to 0.15625
- w_up: bfloat16 [1536, 8960], P('dp', 'head'), may hold values from -0.15625 to 0.15625
- w_down: bfloat16 [8960, 1536], P('head', 'dp'), may hold values from -0.125 to 0.125
- out_grad: float32 [6144, 1536], P(('dp', 'head')), may hold values from -18 to 18
Outputs:
- block_out: float32 [6144, 1536], P(('dp', 'head'))
- grad_in: float32 [6144, 1536], P(('dp', 'head'))
- grad_norm_attn: float32 [1536], replicated
- grad_w_query: float32 [1536, 1536], P('dp', 'head')
- grad_b_query: float32 [2, 768], replicated
- grad_w_key: float32 [1536, 256], P('dp', 'head')
- grad_b_key: float32 [2, 128], replicated
- grad_w_value: float32 [1536, 256], P('dp', 'head')
- grad_b_value: float32 [2, 128], replicated
- grad_w_out: float32 [1536, 1536], P('head', 'dp')
- grad_norm_mlp: float32 [1536], replicated
- grad_w_gate: float32 [1536, 8960], P('dp', 'head')
- grad_w_up: float32 [1536, 8960], P('dp', 'head')
- grad_w_down: float32 [8960, 1536], P('head', 'dp')
Inputs may be any that keep to these rules, and one draw needn't show every extreme that they name: `row_lengths`: in every batch the nonzero lengths come first, are multiples of 96 and add up to 384, and the other slots are 0; some row of every batch holds both tokens 384 // 2 - 1 and 192 of the batch.
All inputs are finite; a program needn't handle non-finite values.
Results may differ from a plain program's by a relative error of at most 0.023.
Values may be sent and summed in bfloat16 or wider, within the bound.
A program may use at most 512 MiB of HBM per device.

v0:
```python
import math

import jax
import jax.numpy as jnp
from jax import lax
from jax.sharding import PartitionSpec as P

NORM_EPS = 1e-06
ROPE_BASE = 1000000.0
MASKED = -1e30


def rms_norm(value_rows, gain_vec):
    return (
        value_rows
        * lax.rsqrt(jnp.mean(value_rows * value_rows, axis=-1, keepdims=True) + NORM_EPS)
        * gain_vec
    )


def layout(lengths_row, token_count):
    row_ends = jnp.cumsum(lengths_row)
    places = jnp.arange(token_count, dtype=jnp.int32)
    passed = (places[:, None] >= row_ends[None, :]).astype(jnp.int32)
    segment = jnp.sum(passed, axis=1)
    offset = jnp.sum(passed * lengths_row[None, :], axis=1)
    return (segment, places - offset)


def rotary_tables(positions, head_dim):
    half_dim = head_dim // 2
    frequency = jnp.exp(
        jnp.arange(half_dim, dtype=jnp.float32) * (-2.0 * math.log(ROPE_BASE) / head_dim)
    )
    angles = positions.astype(jnp.float32)[:, None] * frequency[None, :]
    cosine = jnp.cos(angles)
    sine_tab = jnp.sin(angles)
    return (jnp.concatenate([cosine, cosine], -1), jnp.concatenate([sine_tab, sine_tab], -1))


def rotate(value_rows, cosine, sine_tab):
    half_dim = value_rows.shape[-1] // 2
    turned = jnp.concatenate([-value_rows[..., half_dim:], value_rows[..., :half_dim]], -1)
    return value_rows * cosine + turned * sine_tab


def unrotate(grads_in, cosine, sine_tab):
    half_dim = grads_in.shape[-1] // 2
    scaled = grads_in * sine_tab
    return grads_in * cosine + jnp.concatenate(
        [scaled[..., half_dim:], -scaled[..., :half_dim]], -1
    )


def product(left_side, right_side):
    return jnp.dot(left_side, right_side, preferred_element_type=jnp.float32)


def contract_last(left_side, right_side):
    return lax.dot_general(
        left_side, right_side, (((1,), (1,)), ((), ())), preferred_element_type=jnp.float32
    )


def contract_first(left_side, right_side):
    return lax.dot_general(
        left_side, right_side, (((0,), (0,)), ((), ())), preferred_element_type=jnp.float32
    )


def share_rows(normed_low):
    return lax.all_gather(normed_low, "head", axis=0, tiled=True)


def sum_rows(partial_out):
    return lax.psum_scatter(
        partial_out.astype(jnp.bfloat16), "head", scatter_dimension=0, tiled=True
    ).astype(jnp.float32)


def share_grads(grad_low):
    return lax.all_gather(grad_low, "head", axis=0, tiled=True)


def sum_grads(partial_grad):
    return lax.psum_scatter(
        partial_grad.astype(jnp.bfloat16), "head", scatter_dimension=0, tiled=True
    ).astype(jnp.float32)


def block_mask(segment, block_index, block_len):
    first_row = block_index * block_len
    query_place = first_row + jnp.arange(block_len, dtype=jnp.int32)
    key_place = jnp.arange(segment.shape[0], dtype=jnp.int32)
    return (segment[:, None] == segment[None, :]) & (key_place[None, :] <= query_place[:, None])


def attend_forward(query_rot, rotated_key_rows, value_low, segment, block_count):
    token_count, group_heads, head_dim = query_rot.shape
    block_len = token_count // block_count
    score_scale = 1.0 / math.sqrt(head_dim)
    query_blocks = query_rot.reshape(block_count, block_len, group_heads, head_dim)

    def one_block(pair_in):
        query_block, block_index = pair_in
        allowed = block_mask(segment, block_index, block_len)
        unscaled_scores = jnp.einsum(
            "qhd,kd->hqk", query_block, rotated_key_rows, preferred_element_type=jnp.float32
        )
        scores = jnp.where(allowed[None], unscaled_scores * score_scale, MASKED)
        row_max = jnp.max(scores, axis=-1, keepdims=True)
        exp_scores = jnp.exp(scores - row_max)
        row_total = jnp.sum(exp_scores, axis=-1, keepdims=True)
        probs_low = (exp_scores / row_total).astype(jnp.bfloat16)
        heads_block = jnp.einsum(
            "hqk,kd->qhd", probs_low, value_low, preferred_element_type=jnp.float32
        )
        return (heads_block, (row_max + jnp.log(row_total))[..., 0])

    heads_out, log_sums = lax.map(
        one_block, (query_blocks, jnp.arange(block_count, dtype=jnp.int32))
    )
    return (heads_out.reshape(token_count, group_heads, head_dim), log_sums)


def attend_backward(
    query_rot, rotated_key_rows, value_low, segment, block_count, log_sums, grad_heads
):
    token_count, group_heads, head_dim = query_rot.shape
    block_len = token_count // block_count
    score_scale = 1.0 / math.sqrt(head_dim)
    query_blocks = query_rot.reshape(block_count, block_len, group_heads, head_dim)
    grad_blocks = grad_heads.reshape(block_count, block_len, group_heads, head_dim)

    def one_block(running, pack_in):
        key_acc, value_acc = running
        query_block, grad_block, lse_block, block_index = pack_in
        allowed = block_mask(segment, block_index, block_len)
        unscaled_scores = jnp.einsum(
            "qhd,kd->hqk", query_block, rotated_key_rows, preferred_element_type=jnp.float32
        )
        scores = jnp.where(allowed[None], unscaled_scores * score_scale, MASKED)
        probs = jnp.exp(scores - lse_block[..., None])
        probs_low = probs.astype(jnp.bfloat16)
        value_acc = value_acc + jnp.einsum(
            "hqk,qhd->kd", probs_low, grad_block, preferred_element_type=jnp.float32
        )
        grad_probs = jnp.einsum(
            "qhd,kd->hqk", grad_block, value_low, preferred_element_type=jnp.float32
        )
        centre = jnp.sum(grad_probs * probs, axis=-1, keepdims=True)
        grad_scores = (probs * (grad_probs - centre) * score_scale).astype(jnp.bfloat16)
        query_grad = jnp.einsum(
            "hqk,kd->qhd", grad_scores, rotated_key_rows, preferred_element_type=jnp.float32
        )
        key_acc = key_acc + jnp.einsum(
            "hqk,qhd->kd", grad_scores, query_block, preferred_element_type=jnp.float32
        )
        return ((key_acc, value_acc), query_grad)

    zero_keys = jnp.zeros(rotated_key_rows.shape, jnp.float32)
    (key_grad, value_grad), query_grads = lax.scan(
        one_block,
        (zero_keys, zero_keys),
        (query_blocks, grad_blocks, log_sums, jnp.arange(block_count, dtype=jnp.int32)),
    )
    return (query_grads.reshape(token_count, group_heads, head_dim), key_grad, value_grad)


def mlp_terms(mlp_low, grad_gate, grad_up, grad_rows, hidden_low):
    return jnp.concatenate(
        [
            contract_first(mlp_low, grad_gate),
            contract_first(mlp_low, grad_up),
            contract_first(grad_rows, hidden_low),
        ],
        1,
    )


def attn_terms(normed_low, grad_query, grad_key, grad_value, grad_attn_rows, heads_low):
    return jnp.concatenate(
        [
            contract_first(normed_low, grad_query),
            contract_first(normed_low, grad_key),
            contract_first(normed_low, grad_value),
            contract_first(grad_attn_rows, heads_low),
        ],
        1,
    )


def local(
    hidden_in,
    row_lengths,
    norm_attn,
    w_query,
    b_query,
    w_key,
    b_key,
    w_value,
    b_value,
    w_out,
    norm_mlp,
    w_gate,
    w_up,
    w_down,
    out_grad,
):
    lanes = lax.axis_size("head")
    lane_index = lax.axis_index("head")
    local_rows = hidden_in.shape[0]
    token_count = local_rows * lanes
    head_dim = w_key.shape[1]
    query_width = w_query.shape[1]
    group_heads = query_width // head_dim
    hidden_width = w_gate.shape[1]
    block_count = max(1, -(-token_count // 1024))
    segment, positions = layout(row_lengths[0], token_count)
    cosine, sine_tab = rotary_tables(positions, head_dim)
    cosine = cosine[:, None, :]
    sine_tab = sine_tab[:, None, :]
    attn_set = (
        lax.all_gather(norm_attn, "dp", axis=0, tiled=True),
        lax.all_gather(w_query, "dp", axis=0, tiled=True),
        lax.all_gather(w_key, "dp", axis=0, tiled=True),
        lax.all_gather(w_value, "dp", axis=0, tiled=True),
        lax.all_gather(w_out, "dp", axis=1, tiled=True),
        lax.all_gather(b_query, "dp", axis=1, tiled=True),
        lax.all_gather(b_key, "dp", axis=1, tiled=True),
        lax.all_gather(b_value, "dp", axis=1, tiled=True),
    )
    mlp_set = (
        lax.all_gather(norm_mlp, "dp", axis=0, tiled=True),
        lax.all_gather(w_gate, "dp", axis=0, tiled=True),
        lax.all_gather(w_up, "dp", axis=0, tiled=True),
        lax.all_gather(w_down, "dp", axis=1, tiled=True),
    )
    gain_attn = attn_set[0].astype(jnp.float32)
    wq_full, wk_full, wv_full, wo_full = (attn_set[1], attn_set[2], attn_set[3], attn_set[4])
    bias_query = attn_set[5].reshape(-1).astype(jnp.float32)
    bias_key = attn_set[6].reshape(-1).astype(jnp.float32)
    bias_value = attn_set[7].reshape(-1).astype(jnp.float32)
    gain_mlp = mlp_set[0].astype(jnp.float32)
    wg_full, wu_full, wd_full = (mlp_set[1], mlp_set[2], mlp_set[3])
    normed_low = share_rows(rms_norm(hidden_in, gain_attn).astype(jnp.bfloat16))
    query_pre = product(normed_low, wq_full) + bias_query
    key_pre = product(normed_low, wk_full) + bias_key
    value_low = (product(normed_low, wv_full) + bias_value).astype(jnp.bfloat16)
    query_rot = rotate(
        query_pre.reshape(token_count, group_heads, head_dim), cosine, sine_tab
    ).astype(jnp.bfloat16)
    rotated_key_rows = rotate(key_pre[:, None, :], cosine, sine_tab)[:, 0].astype(jnp.bfloat16)
    heads_out, log_sums = attend_forward(
        query_rot, rotated_key_rows, value_low, segment, block_count
    )
    heads_low = heads_out.reshape(token_count, query_width).astype(jnp.bfloat16)
    residual = hidden_in + sum_rows(product(heads_low, wo_full))
    mlp_low = share_rows(rms_norm(residual, gain_mlp).astype(jnp.bfloat16))
    gate_pre = product(mlp_low, wg_full)
    up_pre = product(mlp_low, wu_full)
    sigmoid_gate = jax.nn.sigmoid(gate_pre)
    silu_gate = gate_pre * sigmoid_gate
    hidden_low = (silu_gate * up_pre).astype(jnp.bfloat16)
    block_out = residual + sum_rows(product(hidden_low, wd_full))
    grad_rows = share_grads(out_grad.astype(jnp.bfloat16))
    grad_hidden = contract_last(grad_rows, wd_full)
    grad_gate = (
        grad_hidden * up_pre * sigmoid_gate * (1.0 + gate_pre * (1.0 - sigmoid_gate))
    ).astype(jnp.bfloat16)
    grad_up = (grad_hidden * silu_gate).astype(jnp.bfloat16)
    mlp_args = (mlp_low, grad_gate, grad_up, grad_rows, hidden_low)
    grad_normed_mlp = sum_grads(contract_last(grad_gate, wg_full) + contract_last(grad_up, wu_full))
    _, mlp_pull = jax.vjp(rms_norm, residual, gain_mlp)
    grad_residual_part, grad_gain_mlp = mlp_pull(grad_normed_mlp)
    grad_residual = out_grad + grad_residual_part
    grad_attn_rows = share_grads(grad_residual.astype(jnp.bfloat16))
    grad_heads = contract_last(grad_attn_rows, wo_full).astype(jnp.bfloat16)
    query_grad, key_grad, value_grad = attend_backward(
        query_rot,
        rotated_key_rows,
        value_low,
        segment,
        block_count,
        log_sums,
        grad_heads.reshape(token_count, group_heads, head_dim),
    )
    grad_query = (
        unrotate(query_grad, cosine, sine_tab)
        .reshape(token_count, query_width)
        .astype(jnp.bfloat16)
    )
    grad_key = unrotate(key_grad[:, None, :], cosine, sine_tab)[:, 0].astype(jnp.bfloat16)
    grad_value = value_grad.astype(jnp.bfloat16)
    grad_normed_attn = sum_grads(
        contract_last(grad_query, wq_full)
        + contract_last(grad_key, wk_full)
        + contract_last(grad_value, wv_full)
    )
    _, attn_pull = jax.vjp(rms_norm, hidden_in, gain_attn)
    grad_in_part, grad_gain_attn = attn_pull(grad_normed_attn)
    grad_in = grad_residual + grad_in_part
    attn_args = (normed_low, grad_query, grad_key, grad_value, grad_attn_rows, heads_low)
    attn_width = query_width * 2 + head_dim * 2
    every_term = jnp.concatenate([attn_terms(*attn_args), mlp_terms(*mlp_args)], 1)
    every_part = lax.psum_scatter(every_term, "dp", scatter_dimension=0, tiled=True)
    attn_part = every_part[:, :attn_width]
    mlp_part = every_part[:, attn_width:]
    bias_vec = jnp.concatenate(
        [
            jnp.sum(grad_query.astype(jnp.float32), 0),
            jnp.sum(grad_key.astype(jnp.float32), 0),
            jnp.sum(grad_value.astype(jnp.float32), 0),
        ]
    )
    lane_pick = (jnp.arange(lanes, dtype=jnp.int32) == lane_index).astype(jnp.float32)
    bias_rows = lane_pick[:, None] * bias_vec[None, :]
    gain_rows = jnp.stack([grad_gain_attn, grad_gain_mlp])
    gain_total, bias_total = lax.psum((gain_rows, bias_rows), ("dp", "head"))
    grad_w_query = attn_part[:, :query_width]
    grad_w_key = attn_part[:, query_width : query_width + head_dim]
    grad_w_value = attn_part[:, query_width + head_dim : query_width + 2 * head_dim]
    grad_w_out = attn_part[:, query_width + 2 * head_dim :].T
    grad_w_gate = mlp_part[:, :hidden_width]
    grad_w_up = mlp_part[:, hidden_width : 2 * hidden_width]
    grad_w_down = mlp_part[:, 2 * hidden_width :].T
    grad_b_query = bias_total[:, :query_width]
    grad_b_key = bias_total[:, query_width : query_width + head_dim]
    grad_b_value = bias_total[:, query_width + head_dim :]
    return (
        block_out,
        grad_in,
        gain_total[0],
        grad_w_query,
        grad_b_query,
        grad_w_key,
        grad_b_key,
        grad_w_value,
        grad_b_value,
        grad_w_out,
        gain_total[1],
        grad_w_gate,
        grad_w_up,
        grad_w_down,
    )


def solution(mesh):
    placed = (
        P(("dp", "head"), None),
        P("dp", None),
        P("dp"),
        P("dp", "head"),
        P("head", "dp"),
        P("dp", "head"),
        P("head", "dp"),
        P("dp", "head"),
        P("head", "dp"),
        P("head", "dp"),
        P("dp"),
        P("dp", "head"),
        P("dp", "head"),
        P("head", "dp"),
        P(("dp", "head"), None),
    )
    return jax.shard_map(
        local,
        mesh=mesh,
        in_specs=placed,
        out_specs=(
            P(("dp", "head"), None),
            P(("dp", "head"), None),
            P(),
            P("dp", "head"),
            P(),
            P("dp", "head"),
            P(),
            P("dp", "head"),
            P(),
            P("head", "dp"),
            P(),
            P("dp", "head"),
            P("dp", "head"),
            P("head", "dp"),
        ),
        check_vma=False,
    )
```

profile of v0, /device:TPU:0, one launch (start us, length us, event | category | flops | bytes accessed | tf_op | source)
XLA Modules:
  0.0 2209.2 jit_solution(11285887290477938077)
XLA Ops:
  7.2 1.3 dynamic-slice.1
  10.5 1.4 multiply_reduce_fusion.1
  16.3 78.6 %all-reduce.6 = (bf16[1536]{0:T(1024)(128)(2,1)S(1)}, bf16[1536]{0:T(1024)(128)(2,1)S(1)}, bf16[128]{0:T(256)(128)(2,1)S(1)}, bf16[128]{0:T(256)(128)(2,1)S(1)}, bf16[768]{0:T(1024)(128)(2,1)S(1)}) all-reduce(bf16[1536]{0:T(1024)(128)(2,1)S(1)} %dynamic-update-slice.4, ...), channel_id=1, replica_groups=mesh['dp'=16,'head'=2] {'dp'}, use_global_device_ids=true, to_apply=%add.4 | all-reduce | flops 4096 | bytes 16384
  97.7 38.3 %all_gather.52 = bf16[1536,128]{1,0:T(8,128)(2,1)S(1)} all-gather(bf16[96,128]{1,0:T(8,128)(2,1)S(1)} %copy-done.44), channel_id=1, replica_groups=mesh['dp'=16,'head'=2] {'dp'}, dimensions={0}, use_global_device_ids=true | all-gather | bytes 417792 | tf_op jit(solution)/shard_map/all_gather | solution.py:226
  136.0 40.8 %all_gather.50 = bf16[1536,128]{1,0:T(8,128)(2,1)S(1)} all-gather(bf16[96,128]{1,0:T(8,128)(2,1)S(1)} %copy-done.45), channel_id=1, replica_groups=mesh['dp'=16,'head'=2] {'dp'}, dimensions={0}, use_global_device_ids=true | all-gather | bytes 417792 | tf_op jit(solution)/shard_map/all_gather | solution.py:227
  178.1 1.8 convolution_add_fusion.4
  180.7 1.1 mul.278
  181.8 2.7 copy.65
  184.4 1.1 fusion.37
  185.5 3.8 convolution_add_fusion.3
  189.3 2.7 copy.66
  192.0 1.3 slice_negate_fusion.1
  193.3 1.1 maximum_multiply_fusion
  194.4 2.7 copy.67
  197.1 2.1 add_convert_fusion.1
  199.5 1.7 fusion.58
  201.8 1.3 copy-done.2
  203.9 29.7 %all-gather.14.cloned.1.call-done = bf16[768,1536]{0,1:T(8,128)(2,1)} async-done(((bf16[768,96]{0,1:T(8,128)(2,1)}), bf16[768,1536]{0,1:T(8,128)(2,1)}) %all-gather.14.cloned.1.call-update) | async-done | bytes 2359312 | tf_op jit(solution)/shard_map/all_gather | solution.py:228
  233.6 3.8 convolution_convert_fusion.1
  237.5 7.6 reduce-scatter.6.cloned.1.call-done
  245.1 1.4 multiply_reduce_fusion
  248.9 2.1 convert_element_type.156
  252.0 6.1 all-gather.16.cloned.1.call-done
  258.1 167.4 %all-gather.20.cloned.1.call-done = bf16[1536,4480]{1,0:T(8,128)(2,1)} async-done(((bf16[96,4480]{1,0:T(8,128)(2,1)}), bf16[1536,4480]{1,0:T(8,128)(2,1)}) %all-gather.20.cloned.1.call-update) | async-done | bytes 13762576 | tf_op jit(solution)/shard_map/all_gather | solution.py:236
  425.5 12.8 fusion.60
  438.3 151.8 %all-gather.18.cloned.1.call-done = bf16[1536,4480]{1,0:T(8,128)(2,1)} async-done(((bf16[96,4480]{1,0:T(8,128)(2,1)}), bf16[1536,4480]{1,0:T(8,128)(2,1)}) %all-gather.18.cloned.1.call-update) | async-done | bytes 13762576 | tf_op jit(solution)/shard_map/all_gather | solution.py:235
  590.1 12.7 fusion.59
  602.8 164.4 %all-gather.22.cloned.1.call-done = bf16[4480,1536]{0,1:T(8,128)(2,1)} async-done(((bf16[4480,96]{0,1:T(8,128)(2,1)}), bf16[4480,1536]{0,1:T(8,128)(2,1)}) %all-gather.22.cloned.1.call-update) | async-done | bytes 13762576 | tf_op jit(solution)/shard_map/all_gather | solution.py:237
  767.2 14.2 multiply_convert_fusion
  781.5 12.9 fusion.61
  794.3 10.9 fusion.6
  805.8 6.6 reduce-scatter.10.cloned.1.call-done
  812.3 2.3 fusion.24
  814.6 1.2 fusion.52
  816.6 9.9 all-gather.26.cloned.1.call-done
  826.5 3.9 convolution_convert_fusion.2
  830.4 1.4 copy.73
  831.8 3.4 fusion.62
  835.2 1.8 convert_reduce_fusion.1
  837.0 7.5 fusion.29
  844.5 8.1 broadcast_multiply_fusion
  852.6 1.4 fusion.56
  857.0 1.2 convolution_add_fusion
  858.2 1.5 fusion.7
  859.8 15.5 convolution_convert_fusion
  875.5 3.6 convolution_dynamic-update-slice_fusion.3
  879.2 1.5 convolution_dynamic-update-slice_fusion.5
  880.6 1.5 convolution_dynamic-update-slice_fusion.4
  882.1 3.6 convolution_dynamic-update-slice_fusion.2
  885.7 12.4 convolution_dynamic-update-slice_fusion.1
  898.1 12.4 convolution_dynamic-update-slice_fusion
  910.5 12.4 bitcast_dynamic-update-slice_fusion
  923.0 1.4 reshape.219
  925.8 2.0 fusion.25
  928.5 45.5 %all-reduce.5 = (f32[2,1536]{1,0:T(2,128)}, f32[2,1024]{1,0:T(2,128)}) all-reduce(f32[2,1536]{1,0:T(2,128)} %pad_maximum_fusion.2, f32[2,1024]{1,0:T(2,128)} %broadcast_multiply_fusion.1), channel_id=1, replica_groups=mesh['dp'=16,'head'=2] {'dp','head'}, use_global_device_ids=true, to_apply=%region_16.17 | all-reduce | flops 5120 | bytes 40960 | tf_op jit(solution)/shard_map/psum | solution.py:319
  973.9 1.3 slice.99
  975.2 1.4 slice_reduce_fusion
  976.6 1.3 fusion.57
  977.9 1.3 multiply_multiply_fusion
  979.2 3.4 fusion.27
  982.5 1211.7 %reduce-scatter.14.cloned.1.call-done = f32[96,15232]{1,0:T(8,128)} async-done(((f32[1536,15232]{1,0:T(8,128)}), f32[96,15232]{1,0:T(8,128)}) %reduce-scatter.14.cloned.1.call-update) | async-done | bytes 5849104 | tf_op jit(solution)/shard_map/reduce_scatter | solution.py:306
  2194.2 1.5 fusion.55
  2195.7 1.9 slice_bitcast_fusion.1
  2197.6 4.9 slice_bitcast_fusion
  (176 shorter events, 20.5 us)
Async XLA Ops:
  7.2 87.7 %copy-start = (f32[192,1536]{1,0:T(8,128)S(1)}, f32[192,1536]{1,0:T(8,128)}, u32[]{:S(2)}) copy-start(f32[192,1536]{1,0:T(8,128)} %param.15) | copy-start | bytes 3538948
  7.2 170.9 %all-gather.10.cloned.1.call-start = ((), (), s32[]{:S(2)}) async-start(), calls=%async_computation.5 | async-start | bytes 1769472 | tf_op jit(solution)/shard_map/all_gather | solution.py:72
  10.5 86.9 %copy-start.50 = (s32[1,3]{1,0:T(1,128)S(1)}, s32[1,3]{1,0:T(1,128)}, u32[]{:S(2)}) copy-start(s32[1,3]{1,0:T(1,128)} %param.16) | copy-start | bytes 40
  10.5 87.2 %copy-start.44 = (bf16[96,128]{1,0:T(8,128)(2,1)S(1)}, bf16[96,128]{1,0:T(8,128)(2,1)}, u32[]{:S(2)}) copy-start(bf16[96,128]{1,0:T(8,128)(2,1)} %param.20) | copy-start | bytes 73732
  12.0 1.8 copy-start.49
  12.0 124.0 %copy-start.45 = (bf16[96,128]{1,0:T(8,128)(2,1)S(1)}, bf16[96,128]{1,0:T(8,128)(2,1)}, u32[]{:S(2)}) copy-start(bf16[96,128]{1,0:T(8,128)(2,1)} %param.22) | copy-start | bytes 73732
  12.0 85.6 %copy-start.47 = (f32[192]{0:T(256)}, f32[192]{0:T(256)S(1)}, u32[]{:S(2)}) copy-start(f32[192]{0:T(256)S(1)} %fusion.46) | copy-start | bytes 2308
  94.8 2.9 copy-start.39
  95.8 89.7 %all-gather.12.cloned.1.call-start = ((), (), s32[]{:S(2)}) async-start(), calls=%async_computation.6 | async-start | bytes 2506752 | tf_op jit(solution)/shard_map/all_gather | solution.py:225
  96.6 137.0 %all-gather.14.cloned.1.call-start = ((), (), s32[]{:S(2)}) async-start(), calls=%async_computation.7 | async-start | bytes 2506752 | tf_op jit(solution)/shard_map/all_gather | solution.py:228
  97.3 147.8 %reduce-scatter.6.cloned.1.call-start = ((), (), s32[]{:S(2)}) async-start(), calls=%async_computation.8 | async-start | bytes 1769472 | tf_op jit(solution)/shard_map/reduce_scatter | solution.py:76
  136.0 44.6 %copy-start.11 = (bf16[1536,128]{1,0:T(8,128)(2,1)}, bf16[1536,128]{1,0:T(8,128)(2,1)S(1)}, u32[]{:S(2)}) copy-start(bf16[1536,128]{1,0:T(8,128)(2,1)S(1)} %all_gather.52) | copy-start | bytes 1179652
  176.8 7.6 copy-start.13
  178.1 2.6 copy-start.27
  178.1 2.6 copy-start.29
  180.6 3.8 copy-start.21
  180.7 12.6 copy-start.33
  180.7 3.8 copy-start.1
  201.3 1.8 copy-start.2
  201.3 1.8 copy-start.38
  203.9 33.6 %copy-start.35 = (bf16[128,6,384]{2,0,1:T(8,128)(2,1)}, bf16[128,6,384]{2,0,1:T(8,128)(2,1)S(1)}, u32[]{:S(2)}) copy-start(bf16[128,6,384]{2,0,1:T(8,128)(2,1)S(1)} %fusion.21) | copy-start | bytes 1769476
  237.5 20.6 all-gather.16.cloned.1.call-start
  245.1 1.4 copy-start.4
  246.5 568.1 %copy-start.43 = (f32[192]{0:T(256)}, f32[192]{0:T(256)S(1)}, u32[]{:S(2)}) copy-start(f32[192]{0:T(256)S(1)} %fusion.47) | copy-start | bytes 2308
  247.5 178.0 %all-gather.20.cloned.1.call-start = ((), (), s32[]{:S(2)}) async-start(), calls=%async_computation.11 | async-start | bytes 14622720 | tf_op jit(solution)/shard_map/all_gather | solution.py:236
  248.1 341.9 %all-gather.18.cloned.1.call-start = ((), (), s32[]{:S(2)}) async-start(), calls=%async_computation.10 | async-start | bytes 14622720 | tf_op jit(solution)/shard_map/all_gather | solution.py:235
  248.9 353.9 %all-gather.24.cloned.1.call-start = ((), (), s32[]{:S(2)}) async-start(), calls=%async_computation.14 | async-start | bytes 1769472 | tf_op jit(solution)/shard_map/all_gather | solution.py:82
  251.1 516.2 %all-gather.22.cloned.1.call-start = ((), (), s32[]{:S(2)}) async-start(), calls=%async_computation.12 | async-start | bytes 14622720 | tf_op jit(solution)/shard_map/all_gather | solution.py:237
  251.8 560.5 %reduce-scatter.10.cloned.1.call-start = ((), (), s32[]{:S(2)}) async-start(), calls=%async_computation.15 | async-start | bytes 1769472 | tf_op jit(solution)/shard_map/reduce_scatter | solution.py:86
  781.5 12.9 copy-start.17
  781.5 12.9 copy-start.15
  805.3 21.2 all-gather.26.cloned.1.call-start
  812.3 2.3 copy-start.5
  812.3 2.3 copy-start.7
  814.6 1.2 copy-start.48
  815.9 109.9 %reduce-scatter.12.cloned.1.call-start = ((), (), s32[]{:S(2)}) async-start(), calls=%async_computation.17 | async-start | bytes 1769472 | tf_op jit(solution)/shard_map/reduce_scatter | solution.py:86
  831.8 3.4 copy-start.3
  831.8 3.4 copy-start.41
  837.0 7.5 copy-start.34
  837.0 7.5 copy-start.37
  837.0 7.5 copy-start.42
  852.6 1.4 copy-start.30
  852.6 1.5 copy-start.28
  852.6 2.1 copy-start.12
  854.1 1.3 copy-start.22
  854.1 1.4 copy-start.24
  855.3 1.7 copy-start.20
  857.0 1.2 copy-start.14
  857.0 1.2 copy-start.31
  859.7 119.5 %reduce-scatter.8.cloned.1.call-start = ((), (), s32[]{:S(2)}) async-start(), calls=%async_computation.13 | async-start | bytes 1769472 | tf_op jit(solution)/shard_map/reduce_scatter | solution.py:76
  875.3 1318.9 %reduce-scatter.14.cloned.1.call-start = ((), (), s32[]{:S(2)}) async-start(), calls=%async_computation.18 | async-start | bytes 99434496 | tf_op jit(solution)/shard_map/reduce_scatter | solution.py:306
  875.5 3.6 copy-start.26
  879.2 1.5 copy-start.32
  879.2 3.0 copy-start.19
  879.2 3.0 copy-start.36
  882.1 3.6 copy-start.9
  882.1 3.6 copy-start.18
  885.7 12.4 copy-start.16
  898.1 12.4 copy-start.10
  898.1 12.4 copy-start.23
  922.9 2.9 copy-start.40
  923.0 56.2 %copy-start.6 = (f32[192,1536]{1,0:T(8,128)S(1)}, f32[192,1536]{1,0:T(8,128)}, u32[]{:S(2)}) copy-start(f32[192,1536]{1,0:T(8,128)} %param.29) | copy-start | bytes 3538948
  923.0 56.2 %copy-start.8 = (bf16[192,1536]{1,0:T(8,128)(2,1)S(1)}, bf16[192,1536]{1,0:T(8,128)(2,1)}, u32[]{:S(2)}) copy-start(bf16[192,1536]{1,0:T(8,128)(2,1)} %reduce-scatter.10.cloned.1.call-done) | copy-start | bytes 1769476
  925.8 2.0 copy-start.46
  (1 other events, 0.6 us)
Sparse Core Ops, SparseCore 0:
  96.0 5.0 all-gather.9
  103.9 65.4 all-gather.11
  172.2 61.3 all-gather.13
  237.6 7.4 reduce-scatter.5
  247.7 10.3 all-gather.15
  261.1 164.3 all-gather.19
  428.7 161.3 all-gather.17
  592.2 7.4 all-gather.23
  602.9 164.3 all-gather.21
  805.4 6.8 reduce-scatter.9
  816.0 10.4 all-gather.25
  859.8 9.8 reduce-scatter.11
  875.4 9.8 reduce-scatter.7
  923.1 1271.0 reduce-scatter.13
where the time goes:
time: 2220 us; the launch traced here: 2210 us
  waiting for transfers between devices  1760 us (79%)
  blocking collectives  203 us (9%)
  matrix products  167 us (8%)
  local copies, waits for them, and re-layouts  32.4 us (1%)
  other arithmetic  29.9 us (1%)
    reduce_scatter x1, waiting for transfers between devices, local(): lax.psum_scatter(every_term, 'dp', scatter_dimension=0, tiled=True)  1210 us
    all_gather x1, waiting for transfers between devices, local(): lax.all_gather(w_up, 'dp', axis=0, tiled=True)  167 us
    all_gather x1, waiting for transfers between devices, local(): lax.all_gather(w_down, 'dp', axis=1, tiled=True)  164 us
    all_gather x1, waiting for transfers between devices, local(): lax.all_gather(w_gate, 'dp', axis=0, tiled=True)  152 us
    unnamed x1, blocking collectives  78.6 us
    dot_general x7, matrix products, product(): return jnp.dot(left_side, right_side, preferred_element_type=jnp.float32)  51.6 us
    dot_general x7, matrix products, contract_first(): lax.dot_general(left_side, right_side, (((0,), (0,)), ((), ())), preferre...  47.4 us
    psum x1, blocking collectives, local(): gain_total, bias_total = lax.psum((gain_rows, bias_rows), ('dp', 'head'))  45.5 us
  transfers between devices with their start and end apart: 14, of which 9 were waited for; matrix products, arithmetic and copies ran while one was open for 6% of the time, Pallas kernels for 0%

commit v1 on v0

v1 whole, which is shorter than its diff:
```python
import math

import jax
import jax.numpy as jnp
from jax import lax
from jax.sharding import PartitionSpec as P

NORM_EPS = 1e-06
ROPE_BASE = 1000000.0
MASKED = -1e30


def rms_norm(value_rows, gain_vec):
    return (
        value_rows
        * lax.rsqrt(jnp.mean(value_rows * value_rows, axis=-1, keepdims=True) + NORM_EPS)
        * gain_vec
    )


def layout(lengths_row, token_count):
    row_ends = jnp.cumsum(lengths_row)
    places = jnp.arange(token_count, dtype=jnp.int32)
    passed = (places[:, None] >= row_ends[None, :]).astype(jnp.int32)
    segment = jnp.sum(passed, axis=1)
    offset = jnp.sum(passed * lengths_row[None, :], axis=1)
    return (segment, places - offset)


def rotary_tables(positions, head_dim):
    half_dim = head_dim // 2
    frequency = jnp.exp(
        jnp.arange(half_dim, dtype=jnp.float32) * (-2.0 * math.log(ROPE_BASE) / head_dim)
    )
    angles = positions.astype(jnp.float32)[:, None] * frequency[None, :]
    cosine = jnp.cos(angles)
    sine_tab = jnp.sin(angles)
    return (jnp.concatenate([cosine, cosine], -1), jnp.concatenate([sine_tab, sine_tab], -1))


def rotate(value_rows, cosine, sine_tab):
    half_dim = value_rows.shape[-1] // 2
    turned = jnp.concatenate([-value_rows[..., half_dim:], value_rows[..., :half_dim]], -1)
    return value_rows * cosine + turned * sine_tab


def unrotate(grads_in, cosine, sine_tab):
    half_dim = grads_in.shape[-1] // 2
    scaled = grads_in * sine_tab
    return grads_in * cosine + jnp.concatenate(
        [scaled[..., half_dim:], -scaled[..., :half_dim]], -1
    )


def product(left_side, right_side):
    return jnp.dot(left_side, right_side, preferred_element_type=jnp.float32)


def contract_last(left_side, right_side):
    return lax.dot_general(
        left_side, right_side, (((1,), (1,)), ((), ())), preferred_element_type=jnp.float32
    )


def contract_first(left_side, right_side):
    return lax.dot_general(
        left_side, right_side, (((0,), (0,)), ((), ())), preferred_element_type=jnp.float32
    )


def attend_forward(query_rot, key_rot, value_low, allowed):
    score_scale = 1.0 / math.sqrt(query_rot.shape[-1])
    raw = jnp.einsum("qhd,kd->hqk", query_rot, key_rot, preferred_element_type=jnp.float32)
    scores = jnp.where(allowed[None], raw * score_scale, MASKED)
    row_max = jnp.max(scores, axis=-1, keepdims=True)
    exp_scores = jnp.exp(scores - row_max)
    row_total = jnp.sum(exp_scores, axis=-1, keepdims=True)
    probs = exp_scores / row_total
    heads_out = jnp.einsum(
        "hqk,kd->qhd", probs.astype(jnp.bfloat16), value_low, preferred_element_type=jnp.float32
    )
    return (heads_out, row_max + jnp.log(row_total))


def attend_backward(query_rot, key_rot, value_low, allowed, log_sums, grad_heads):
    score_scale = 1.0 / math.sqrt(query_rot.shape[-1])
    raw = jnp.einsum("qhd,kd->hqk", query_rot, key_rot, preferred_element_type=jnp.float32)
    scores = jnp.where(allowed[None], raw * score_scale, MASKED)
    probs = jnp.exp(scores - log_sums)
    probs_low = probs.astype(jnp.bfloat16)
    value_grad = jnp.einsum(
        "hqk,qhd->kd", probs_low, grad_heads, preferred_element_type=jnp.float32
    )
    grad_probs = jnp.einsum(
        "qhd,kd->hqk", grad_heads, value_low, preferred_element_type=jnp.float32
    )
    centre = jnp.sum(grad_probs * probs, axis=-1, keepdims=True)
    grad_scores = (probs * (grad_probs - centre) * score_scale).astype(jnp.bfloat16)
    query_grad = jnp.einsum(
        "hqk,kd->qhd", grad_scores, key_rot, preferred_element_type=jnp.float32
    )
    key_grad = jnp.einsum(
        "hqk,qhd->kd", grad_scores, query_rot, preferred_element_type=jnp.float32
    )
    return (query_grad, key_grad, value_grad)


DP = ("z", "p")
POOL = ("z", "head")


def gather(x, axes):
    return lax.all_gather(x, axes, axis=0, tiled=True)


def scatter_sum(x, axes):
    return lax.psum_scatter(x.astype(jnp.bfloat16), axes, scatter_dimension=0, tiled=True)


def local(
    hidden_in,
    row_lengths,
    norm_attn,
    w_query,
    b_query,
    w_key,
    b_key,
    w_value,
    b_value,
    w_out,
    norm_mlp,
    w_gate,
    w_up,
    w_down,
    out_grad,
):
    bf = jnp.bfloat16
    quarters = lax.axis_size("z")
    plane = lax.axis_size("p")
    lanes = lax.axis_size("head")
    lane_index = lax.axis_index("head")
    shards = quarters * plane
    local_rows = hidden_in.shape[0]
    token_count = local_rows * lanes
    depth = norm_attn.shape[0]
    width = hidden_in.shape[1]
    head_dim = w_key.shape[1]
    query_width = w_query.shape[1]
    group_heads = query_width // head_dim
    hidden_width = w_gate.shape[1]
    part_width = hidden_width // quarters
    segment, positions = layout(row_lengths[0], token_count)
    cosine, sine_tab = rotary_tables(positions, head_dim)
    cosine = cosine[:, None, :]
    sine_tab = sine_tab[:, None, :]
    place = jnp.arange(token_count, dtype=jnp.int32)
    allowed = (segment[:, None] == segment[None, :]) & (place[None, :] <= place[:, None])

    attn_set = gather(jnp.concatenate([w_query, w_key, w_value, w_out.T], 1), DP)
    small = gather(
        jnp.concatenate([norm_attn, norm_mlp, b_query[0], b_key[0], b_value[0]])[None], DP
    )
    wq_full = attn_set[:, :query_width]
    wk_full = attn_set[:, query_width : query_width + head_dim]
    wv_full = attn_set[:, query_width + head_dim : query_width + 2 * head_dim]
    wo_rows = attn_set[:, query_width + 2 * head_dim :]
    cuts = [depth, depth, b_query.shape[1], b_key.shape[1], b_value.shape[1]]
    edges = [sum(cuts[:i]) for i in range(6)]
    gain_attn, gain_mlp, bias_query, bias_key, bias_value = [
        small[:, edges[i] : edges[i + 1]].reshape(-1).astype(jnp.float32) for i in range(5)
    ]

    def hidden_parts(rows):
        split = rows.reshape(depth, quarters, part_width).transpose(1, 0, 2)
        mine = lax.all_to_all(split, "z", 0, 0, tiled=True)
        return mine

    mlp_set = jnp.concatenate(
        [hidden_parts(w_gate), hidden_parts(w_up), hidden_parts(w_down.T)], -1
    )
    mlp_set = lax.all_gather(mlp_set, "p", axis=1, tiled=False).reshape(width, 3 * part_width)
    wg = mlp_set[:, :part_width]
    wu = mlp_set[:, part_width : 2 * part_width]
    wd_rows = mlp_set[:, 2 * part_width :]
    grad_rows = gather(out_grad.astype(bf), POOL)

    normed_low = gather(rms_norm(hidden_in, gain_attn).astype(bf), "head")
    query_pre = product(normed_low, wq_full) + bias_query
    key_pre = product(normed_low, wk_full) + bias_key
    value_low = (product(normed_low, wv_full) + bias_value).astype(bf)
    query_rot = rotate(
        query_pre.reshape(token_count, group_heads, head_dim), cosine, sine_tab
    ).astype(bf)
    key_rot = rotate(key_pre[:, None, :], cosine, sine_tab)[:, 0].astype(bf)
    heads_out, log_sums = attend_forward(query_rot, key_rot, value_low, allowed)
    heads_low = heads_out.reshape(token_count, query_width).astype(bf)
    residual = hidden_in + scatter_sum(contract_last(heads_low, wo_rows), "head").astype(
        jnp.float32
    )
    mlp_low = gather(rms_norm(residual, gain_mlp).astype(bf), POOL)
    gate_pre = product(mlp_low, wg)
    up_pre = product(mlp_low, wu)
    sigmoid_gate = jax.nn.sigmoid(gate_pre)
    silu_gate = gate_pre * sigmoid_gate
    hidden_low = (silu_gate * up_pre).astype(bf)
    block_out = residual + scatter_sum(contract_last(hidden_low, wd_rows), POOL).astype(
        jnp.float32
    )
    grad_hidden = product(grad_rows, wd_rows)
    grad_gate = (
        grad_hidden * up_pre * sigmoid_gate * (1.0 + gate_pre * (1.0 - sigmoid_gate))
    ).astype(bf)
    grad_up = (grad_hidden * silu_gate).astype(bf)
    grad_normed_mlp = scatter_sum(
        contract_last(grad_gate, wg) + contract_last(grad_up, wu), POOL
    ).astype(jnp.float32)
    mlp_terms = jnp.concatenate(
        [
            contract_first(mlp_low, grad_gate),
            contract_first(mlp_low, grad_up),
            contract_first(grad_rows, hidden_low),
        ],
        1,
    ).astype(bf)
    mlp_terms = mlp_terms.reshape(quarters, plane, depth, 3 * part_width).transpose(1, 0, 2, 3)
    mlp_terms = scatter_sum(mlp_terms.reshape(width, 3 * part_width), "p")
    mlp_terms = mlp_terms.reshape(quarters, depth, 3 * part_width)
    mlp_terms = lax.all_to_all(mlp_terms, "z", 0, 0, tiled=True).astype(jnp.float32)

    def whole_rows(index):
        piece = mlp_terms[:, :, index * part_width : (index + 1) * part_width]
        return piece.transpose(1, 0, 2).reshape(depth, hidden_width)

    grad_w_gate, grad_w_up = (whole_rows(0), whole_rows(1))
    grad_w_down = (
        mlp_terms[:, :, 2 * part_width :].transpose(0, 2, 1).reshape(hidden_width, depth)
    )

    _, mlp_pull = jax.vjp(rms_norm, residual, gain_mlp)
    grad_residual_part, grad_gain_mlp = mlp_pull(grad_normed_mlp)
    grad_residual = out_grad + grad_residual_part
    grad_attn_rows = gather(grad_residual.astype(bf), "head")
    grad_heads = product(grad_attn_rows, wo_rows).astype(bf)
    query_grad, key_grad, value_grad = attend_backward(
        query_rot,
        key_rot,
        value_low,
        allowed,
        log_sums,
        grad_heads.reshape(token_count, group_heads, head_dim),
    )
    grad_query = (
        unrotate(query_grad, cosine, sine_tab).reshape(token_count, query_width).astype(bf)
    )
    grad_key = unrotate(key_grad[:, None, :], cosine, sine_tab)[:, 0].astype(bf)
    grad_value = value_grad.astype(bf)
    grad_qkv = jnp.concatenate([grad_query, grad_key, grad_value], 1)
    grad_normed_attn = scatter_sum(
        contract_last(grad_qkv, attn_set[:, : query_width + 2 * head_dim]), "head"
    ).astype(jnp.float32)
    _, attn_pull = jax.vjp(rms_norm, hidden_in, gain_attn)
    grad_in_part, grad_gain_attn = attn_pull(grad_normed_attn)
    grad_in = grad_residual + grad_in_part
    attn_terms = jnp.concatenate(
        [contract_first(normed_low, grad_qkv), contract_first(grad_attn_rows, heads_low)], 1
    )
    attn_part = scatter_sum(attn_terms, DP).astype(jnp.float32)
    bias_vec = jnp.sum(grad_qkv.astype(jnp.float32), 0)
    lane_pick = (jnp.arange(lanes, dtype=jnp.int32) == lane_index).astype(jnp.float32)
    bias_rows = lane_pick[:, None] * bias_vec[None, :]
    gain_rows = jnp.stack([grad_gain_attn, grad_gain_mlp])
    gain_total, bias_total = lax.psum((gain_rows, bias_rows), ("z", "p", "head"))
    return (
        block_out,
        grad_in,
        gain_total[0],
        attn_part[:, :query_width],
        bias_total[:, :query_width],
        attn_part[:, query_width : query_width + head_dim],
        bias_total[:, query_width : query_width + head_dim],
        attn_part[:, query_width + head_dim : query_width + 2 * head_dim],
        bias_total[:, query_width + head_dim :],
        attn_part[:, query_width + 2 * head_dim :].T,
        gain_total[1],
        grad_w_gate,
        grad_w_up,
        grad_w_down,
    )


def solution(mesh):
    shards = mesh.shape["dp"]
    plane = 4 if shards % 4 == 0 else 1
    split = jax.sharding.Mesh(
        mesh.devices.reshape(shards // plane, plane, mesh.shape["head"]), ("z", "p", "head")
    )
    rows = P(("z", "p", "head"), None)
    deep = P(DP, "head")
    wide = P("head", DP)
    placed = (
        rows,
        P(DP, None),
        P(DP),
        deep,
        wide,
        deep,
        wide,
        deep,
        wide,
        wide,
        P(DP),
        deep,
        deep,
        wide,
        rows,
    )
    return jax.shard_map(
        local,
        mesh=split,
        in_specs=placed,
        out_specs=(
            rows,
            rows,
            P(),
            deep,
            P(),
            deep,
            P(),
            deep,
            P(),
            wide,
            P(),
            deep,
            deep,
            wide,
        ),
        check_vma=False,
    )
```

time: 2220 us -> 983 us (0.44)
  waiting for transfers between devices: 1760 us -> 482 us
  local copies, waits for them, and re-layouts: 32.4 us -> 101 us
  blocking collectives: 203 us -> 165 us
    reduce_scatter x5, waiting for transfers between devices: 1230 us -> 61.9 us  [scatter_sum(): lax.psum_scatter(x.astype(jnp.bfloat16), axes, scatter_dimension=0, tiled...]
    all_gather x9 -> x6, waiting for transfers between devices: 529 us -> 268 us  [the longest x5 169 us: gather(): return lax.all_gather(x, axes, axis=0, tiled=True)]
    unnamed x14 -> x13, waiting for transfers between devices: 3.42 us -> 134 us
    unnamed x1 -> x0, blocking collectives: 78.6 us -> none
    psum x1, blocking collectives: 45.5 us -> 98 us  [local(): lax.psum((gain_rows, bias_rows), ('z', 'p', 'head'))]
    all_gather x2 -> x1, blocking collectives: 79.1 us -> 42.4 us  [gather(): return lax.all_gather(x, axes, axis=0, tiled=True)]
    concatenate x0 -> x3, local copies, waits for them, and re-layouts: none -> 27.2 us  [the longest x1 18.3 us: local(): jnp.concatenate([contract_first(mlp_low, grad_gate), contract_first(mlp_l...]
    all_to_all x0 -> x1, blocking collectives: none -> 24.2 us  [hidden_parts(): mine = lax.all_to_all(split, 'z', 0, 0, tiled=True)]
  transfers between devices with their start and end apart: 14 -> 15, of which waited for: 9 -> 9; matrix products, arithmetic and copies ran while one was open for 6% -> 23% of each run, Pallas kernels for 0% -> 0%
where the time goes in v1:
time: 983 us; the launch traced here: 972 us
  waiting for transfers between devices  482 us (49%)
  blocking collectives  165 us (17%)
  matrix products  154 us (16%)
  local copies, waits for them, and re-layouts  101 us (10%)
  other arithmetic  41.4 us (4%)
  between operations  16.5 us (2%)
  starting transfers between devices  13.7 us (1%)
    all_gather x5, waiting for transfers between devices, gather(): return lax.all_gather(x, axes, axis=0, tiled=True)  169 us
    unnamed x13, waiting for transfers between devices  134 us
    all_gather x1, waiting for transfers between devices, local(): lax.all_gather(mlp_set, 'p', axis=1, tiled=False)  99.3 us
    psum x1, blocking collectives, local(): lax.psum((gain_rows, bias_rows), ('z', 'p', 'head'))  98 us
    reduce_scatter x5, waiting for transfers between devices, scatter_sum(): lax.psum_scatter(x.astype(jnp.bfloat16), axes, scatter_dimension=0, tiled...  61.9 us
    dot_general x7, matrix products, product(): return jnp.dot(left_side, right_side, preferred_element_type=jnp.float32)  51.3 us
    dot_general x5, matrix products, contract_last(): lax.dot_general(left_side, right_side, (((1,), (1,)), ((), ())), preferre...  45.2 us
    all_gather x1, blocking collectives, gather(): return lax.all_gather(x, axes, axis=0, tiled=True)  42.4 us
  transfers between devices with their start and end apart: 15, of which 9 were waited for; matrix products, arithmetic and copies ran while one was open for 23% of the time, Pallas kernels for 0%

profile of v1, /device:TPU:0, one launch (start us, length us, event | category | flops | bytes accessed | tf_op | source)
XLA Modules:
  0.0 972.3 jit_solution(6179180559083666939)
XLA Ops:
  8.1 3.5 concatenate.55
  11.7 1.4 multiply_reduce_fusion.1
  13.1 42.4 %all-gather.2 = bf16[16,1,256]{2,1,0:T(2,128)(2,1)S(1)} all-gather(bf16[1,1,256]{2,1,0:T(2,128)(2,1)S(1)} %reshape.292), channel_id=2, replica_groups=mesh['z'=4,'p'=4,'head'=2] {'z','p'}, dimensions={0}, use_global_device_ids=true | all-gather | bytes 8704 | tf_op jit(solution)/shard_map/all_gather | solution.py:113
  55.7 2.3 multiply_convert_fusion.4
  60.5 4.2 all-to-all-start
  68.9 86.2 %all-gather.12.cloned.1.call-done = bf16[1536,1792]{1,0:T(8,128)(2,1)} async-done(((bf16[96,1792]{1,0:T(8,128)(2,1)}), bf16[1536,1792]{1,0:T(8,128)(2,1)}) %all-gather.12.cloned.1.call-update) | async-done | bytes 5505040 | tf_op jit(solution)/shard_map/all_gather | solution.py:113
  155.0 1.8 convolution_add_fusion
  156.9 3.1 fusion.39
  166.0 2.3 add_convert_fusion.2
  169.7 1.8 fusion.61
  171.5 1.8 fusion.82
  175.9 3.5 all-to-all-start.1
  179.4 3.9 convolution_convert_fusion.6
  184.2 17.1 %all-to-all-done.1 = bf16[4,96,1120]{2,1,0:T(8,128)(2,1)S(1)} async-done(((bf16[4,96,1120]{2,1,0:T(8,128)(2,1)}), bf16[4,96,1120]{2,1,0:T(8,128)(2,1)S(1)}, u32[]{:S(2)}, u32[]{:S(2)}) %all-to-all-start.1) | async-done | bytes 860192 | tf_op jit(solution)/shard_map/all_to_all | solution.py:175
  201.3 24.2 %all_to_all.20 = bf16[4,96,1120]{2,1,0:T(8,128)(2,1)S(1)} all-to-all(bf16[4,96,1120]{2,1,0:T(8,128)(2,1)S(1)} %bitcast.148), channel_id=1, replica_groups=mesh['z'=4,'p'=4,'head'=2] {'z'}, dimensions={0} | all-to-all | bytes 1720320 | tf_op jit(solution)/shard_map/all_to_all | solution.py:175
  225.4 5.4 concatenate.63
  232.4 2.1 multiply_convert_fusion.3
  235.7 99.3 %all-gather.20.cloned.1.call-done = bf16[4,384,3360]{2,1,0:T(8,128)(2,1)} async-done(((bf16[4,96,3360]{2,1,0:T(8,128)(2,1)}), bf16[4,384,3360]{2,1,0:T(8,128)(2,1)}) %all-gather.20.cloned.1.call-update) | async-done | bytes 10321936 | tf_op jit(solution)/shard_map/all_gather | solution.py:181
  335.0 53.4 %all-gather.14.cloned.1.call-done = bf16[1536,1536]{1,0:T(8,128)(2,1)} async-done(((bf16[192,1536]{1,0:T(8,128)(2,1)}), bf16[1536,1536]{1,0:T(8,128)(2,1)}) %all-gather.14.cloned.1.call-update) | async-done | bytes 4718608 | tf_op jit(solution)/shard_map/all_gather | solution.py:113
  388.4 12.9 %fusion.12 = f32[1536,1120]{0,1:T(8,128)} fusion(bf16[1536,1536]{1,0:T(8,128)(2,1)} %all-gather.14.cloned.1.call-done, bf16[1536,3360]{1,0:T(8,128)(2,1)} %bitcast.166), kind=kOutput, calls=%fused_computation.31 | convolution fusion | flops 5284823040 | bytes 15138816 | tf_op jit(solution)/shard_map/dot_general | solution.py:56
  401.3 9.9 %fusion.16 = f32[1536,1120]{0,1:T(8,128)} fusion(bf16[1536,1536]{1,0:T(8,128)(2,1)S(1)} %copy-done.36, bf16[1536,3360]{1,0:T(8,128)(2,1)} %bitcast.167), kind=kOutput, calls=%fused_computation.35 | convolution fusion | flops 5284823040 | bytes 15138816 | tf_op jit(solution)/shard_map/dot_general | solution.py:56
  411.2 29.3 %all-gather.16.cloned.1.call-done = bf16[1536,1536]{1,0:T(8,128)(2,1)} async-done(((bf16[192,1536]{1,0:T(8,128)(2,1)}), bf16[1536,1536]{1,0:T(8,128)(2,1)}) %all-gather.16.cloned.1.call-update) | async-done | bytes 4718608 | tf_op jit(solution)/shard_map/all_gather | solution.py:113
  440.5 17.8 %multiply_convert_fusion = (bf16[1536,1120]{0,1:T(8,128)(2,1)S(1)}, bf16[1536,1120]{0,1:T(8,128)(2,1)S(1)}, bf16[1536,1120]{0,1:T(8,128)(2,1)}) fusion(f32[1536,1120]{0,1:T(8,128)} %fusion.16, f32[1536,1120]{0,1:T(8,128)} %fusion.12, bf16[1536,1536]{1,0:T(8,128)(2,1)} %all-gather.16.cloned.1.call-done, bf16[1536,3360]{1,0:T(8,128)(2,1)} %bitcast.168), kind=kOutput, calls=%fused_computation.7 | convolution fusion | flops 5310627840 | bytes 32342016 | tf_op jit(solution)/shard_map/dot_general | solution.py:56
  458.3 11.0 %fusion.14 = f32[1536,1536]{1,0:T(8,128)S(1)} fusion(bf16[1536,1120]{0,1:T(8,128)(2,1)S(1)} %get-tuple-element.109, bf16[1536,3360]{1,0:T(8,128)(2,1)} %bitcast.169), kind=kOutput, calls=%fused_computation.33 | convolution fusion | flops 5284823040 | bytes 16416768 | tf_op jit(solution)/shard_map/dot_general | solution.py:60
  469.3 13.3 %add_convert_fusion = bf16[1536,1536]{1,0:T(8,128)(2,1)} fusion(f32[1536,1536]{1,0:T(8,128)S(1)} %fusion.14, bf16[1536,1120]{0,1:T(8,128)(2,1)S(1)} %get-tuple-element.108, bf16[1536,3360]{1,0:T(8,128)(2,1)} %bitcast.170), kind=kOutput, calls=%fused_computation.1 | convolution fusion | flops 5289541632 | bytes 21135360 | tf_op jit(solution)/shard_map/dot_general | solution.py:60
  482.7 9.7 %fusion.2 = bf16[1536,1120]{0,1:T(8,128)(2,1)} fusion(bf16[1536,1120]{0,1:T(8,128)(2,1)} %get-tuple-element.110, bf16[1536,1536]{1,0:T(8,128)(2,1)} %all-gather.16.cloned.1.call-done), kind=kOutput, calls=%fused_computation.12 | convolution fusion | flops 5286543360 | bytes 11599872 | tf_op jit(solution)/shard_map/dot_general | solution.py:66
  492.5 5.7 copy.170
  498.1 9.8 %convolution_convert_fusion.1 = bf16[1536,1120]{0,1:T(8,128)(2,1)} fusion(bf16[1536,1120]{0,1:T(8,128)(2,1)} %copy-done.38, bf16[1536,1536]{1,0:T(8,128)(2,1)} %all-gather.14.cloned.1.call-done), kind=kOutput, calls=%fused_computation.4 | convolution fusion | flops 5286543360 | bytes 11599872 | tf_op jit(solution)/shard_map/dot_general | solution.py:66
  507.9 5.7 copy.168
  513.7 22.5 %reduce-scatter.13.cloned.1.call-done = bf16[192,1536]{1,0:T(8,128)(2,1)} async-done(((bf16[1536,1536]{1,0:T(8,128)(2,1)}), bf16[192,1536]{1,0:T(8,128)(2,1)}) %reduce-scatter.13.cloned.1.call-update) | async-done | bytes 589840 | tf_op jit(solution)/shard_map/reduce_scatter | solution.py:117
  536.2 2.1 fusion.48
  538.4 2.3 fusion.78
  540.7 9.7 %convolution_convert_fusion = bf16[1536,1120]{0,1:T(8,128)(2,1)} fusion(bf16[1536,1120]{0,1:T(8,128)(2,1)} %copy-done.39, bf16[1536,1536]{1,0:T(8,128)(2,1)} %all-gather.14.cloned.1.call-done), kind=kOutput, calls=%fused_computation.3 | convolution fusion | flops 5286543360 | bytes 11599872 | tf_op jit(solution)/shard_map/dot_general | solution.py:66
  550.4 5.7 copy.169
  556.1 18.3 %concatenate.73 = bf16[4,4,96,3360]{3,2,1,0:T(8,128)(2,1)} concatenate(bf16[4,4,96,1120]{3,2,1,0:T(8,128)(2,1)} %bitcast.140, bf16[4,4,96,1120]{3,2,1,0:T(8,128)(2,1)} %bitcast.141, bf16[4,4,96,1120]{3,2,1,0:T(8,128)(2,1)} %bitcast.139), dimensions={3} | concatenate | bytes 20643840 | tf_op jit(solution)/shard_map/concatenate | solution.py:217
  574.4 9.3 copy.171
  584.6 3.9 fusion.42
  588.5 1.5 copy.163
  590.1 3.2 fusion.83
  593.3 8.4 fusion.53
  602.8 1.8 fusion.68
  604.6 8.5 broadcast_multiply_fusion
  613.1 1.7 fusion.79
  614.8 1.6 fusion.52
  617.8 4.4 fusion.18
  622.2 12.7 %convolution_convert_fusion.3 = bf16[1536,1536]{1,0:T(8,128)(2,1)} fusion(bf16[1536,1120]{0,1:T(8,128)(2,1)} %get-tuple-element.110, bf16[1536,3360]{1,0:T(8,128)(2,1)} %bitcast.171), kind=kOutput, calls=%fused_computation.6 | convolution fusion | flops 5287182336 | bytes 11698176 | tf_op jit(solution)/shard_map/dot_general | solution.py:60
  635.3 3.0 convolution_convert_fusion.5
  638.3 1.8 convolution_convert_fusion.4
  640.1 2.8 pad_maximum_fusion
  642.9 8.0 copy.189
  650.9 35.9 %reduce-scatter.17.cloned.1.call-done = bf16[384,3360]{1,0:T(8,128)(2,1)} async-done(((bf16[1536,3360]{1,0:T(8,128)(2,1)}), bf16[384,3360]{1,0:T(8,128)(2,1)}) %reduce-scatter.17.cloned.1.call-update) | async-done | bytes 2580496 | tf_op jit(solution)/shard_map/reduce_scatter | solution.py:117
  686.8 4.7 all-to-all-start.3
  694.9 3.5 reduce-scatter.15.cloned.1.call-done
  698.3 2.0 fusion.49
  701.7 98.0 %all-reduce = (f32[2,1536]{1,0:T(2,128)}, f32[2,1024]{1,0:T(2,128)}) all-reduce(f32[2,1536]{1,0:T(2,128)} %pad_maximum_fusion.5, f32[2,1024]{1,0:T(2,128)} %broadcast_multiply_fusion.1), channel_id=1, replica_groups=mesh['z'=4,'p'=4,'head'=2] {'z','p','head'}, use_global_device_ids=true, to_apply=%region_16.17 | all-reduce | flops 5120 | bytes 40960 | tf_op jit(solution)/shard_map/psum | solution.py:272
  804.9 3.4 fusion.51
  808.2 134.3 %reduce-scatter.19.cloned.1.call-done = bf16[96,1792]{1,0:T(8,128)(2,1)} async-done(((bf16[1536,1792]{1,0:T(8,128)(2,1)}), bf16[96,1792]{1,0:T(8,128)(2,1)}) %reduce-scatter.19.cloned.1.call-update) | async-done | bytes 344080
  947.1 2.1 convert_element_type.219
  949.2 2.8 slice_bitcast_fusion
  953.1 2.1 reshape.283
  955.2 2.6 copy.173
  957.9 2.1 reshape.282
  960.0 2.6 copy.172
  962.6 2.1 reshape.281
  (173 shorter events, 39.7 us)
Async XLA Ops:
  8.0 50.0 %copy-start.22 = (bf16[768,96]{0,1:T(8,128)(2,1)S(1)}, bf16[768,96]{0,1:T(8,128)(2,1)}, u32[]{:S(2)}) copy-start(bf16[768,96]{0,1:T(8,128)(2,1)} %param.24) | copy-start | bytes 442372
  8.0 50.0 %copy-start.29 = (bf16[96,128]{1,0:T(8,128)(2,1)S(1)}, bf16[96,128]{1,0:T(8,128)(2,1)}, u32[]{:S(2)}) copy-start(bf16[96,128]{1,0:T(8,128)(2,1)} %param.22) | copy-start | bytes 73732
  8.0 50.0 %copy-start.30 = (bf16[96,128]{1,0:T(8,128)(2,1)S(1)}, bf16[96,128]{1,0:T(8,128)(2,1)}, u32[]{:S(2)}) copy-start(bf16[96,128]{1,0:T(8,128)(2,1)} %param.20) | copy-start | bytes 73732
  8.0 50.0 %copy-start.23 = (bf16[96,768]{1,0:T(8,128)(2,1)S(1)}, bf16[96,768]{1,0:T(8,128)(2,1)}, u32[]{:S(2)}) copy-start(bf16[96,768]{1,0:T(8,128)(2,1)} %param.18) | copy-start | bytes 442372
  8.1 50.8 %copy-start.15 = (bf16[96,4480]{1,0:T(8,128)(2,1)S(1)}, bf16[96,4480]{1,0:T(8,128)(2,1)}, u32[]{:S(2)}) copy-start(bf16[96,4480]{1,0:T(8,128)(2,1)} %param.26) | copy-start | bytes 2580484
  8.1 60.8 %all-gather.10.cloned.1.call-start = ((), (), s32[]{:S(2)}) async-start(), calls=%async_computation.10 | async-start | bytes 1769472 | tf_op jit(solution)/shard_map/all_gather | solution.py:113
  13.1 47.4 %copy-start.33 = (f32[192]{0:T(256)}, f32[192]{0:T(256)S(1)}, u32[]{:S(2)}) copy-start(f32[192]{0:T(256)S(1)} %multiply_reduce_fusion.1) | copy-start | bytes 2308
  13.1 47.4 %copy-start.31 = (f32[192]{0:T(256)}, f32[192]{0:T(256)S(1)}, u32[]{:S(2)}) copy-start(f32[192]{0:T(256)S(1)} %fusion.72) | copy-start | bytes 2308
  55.7 3.1 copy-start.24
  57.9 7.7 copy-start.16
  58.0 97.0 %all-gather.12.cloned.1.call-start = ((), (), s32[]{:S(2)}) async-start(), calls=%async_computation.11 | async-start | bytes 5849088 | tf_op jit(solution)/shard_map/all_gather | solution.py:113
  59.5 7.8 copy-start.34
  60.5 115.3 %all-to-all-start = ((bf16[4,96,1120]{2,1,0:T(8,128)(2,1)}), bf16[4,96,1120]{2,1,0:T(8,128)(2,1)}, u32[]{:S(2)}, u32[]{:S(2)}) async-start(bf16[4,96,1120]{2,1,0:T(8,128)(2,1)} %bitcast.135), calls=%async_computation.1 | async-start | bytes 1769472 | tf_op jit(solution)/shard_map/all_to_all | solution.py:175
  68.8 91.6 %copy-start.13 = (f32[384,64]{0,1:T(8,128)}, f32[384,64]{0,1:T(8,128)S(1)}, u32[]{:S(2)}) copy-start(f32[384,64]{0,1:T(8,128)S(1)} %get-tuple-element.135) | copy-start | bytes 294916
  68.8 91.6 %copy-start.14 = (f32[384,64]{0,1:T(8,128)}, f32[384,64]{0,1:T(8,128)S(1)}, u32[]{:S(2)}) copy-start(f32[384,64]{0,1:T(8,128)S(1)} %get-tuple-element.136) | copy-start | bytes 294916
  160.4 3.1 copy-start.7
  161.2 0.7 copy-start.11
  163.4 2.7 copy-start.8
  164.6 5.1 copy-start.6
  164.6 5.1 copy-start.35
  171.5 2.3 copy-start.26
  173.3 1.7 copy-start.1
  175.8 7.5 copy-start.37
  175.9 25.4 %all-to-all-start.1 = ((bf16[4,96,1120]{2,1,0:T(8,128)(2,1)}), bf16[4,96,1120]{2,1,0:T(8,128)(2,1)S(1)}, u32[]{:S(2)}, u32[]{:S(2)}) async-start(bf16[4,96,1120]{2,1,0:T(8,128)(2,1)} %bitcast.134), calls=%async_computation.2 | async-start | bytes 1769472 | tf_op jit(solution)/shard_map/all_to_all | solution.py:175
  179.4 51.6 %reduce-scatter.9.cloned.1.call-start = ((), (), s32[]{:S(2)}) async-start(), calls=%async_computation.12 | async-start | bytes 1769472 | tf_op jit(solution)/shard_map/reduce_scatter | solution.py:117
  179.4 4.0 copy-start.17
  183.4 151.6 %all-gather.20.cloned.1.call-start = ((), (), s32[]{:S(2)}) async-start(), calls=%async_computation.20 | async-start | bytes 13271040 | tf_op jit(solution)/shard_map/all_gather | solution.py:181
  225.4 5.5 copy-start
  230.8 3.7 copy-start.4
  230.8 157.6 %all-gather.14.cloned.1.call-start = ((), (), s32[]{:S(2)}) async-start(), calls=%async_computation.13 | async-start | bytes 5308416 | tf_op jit(solution)/shard_map/all_gather | solution.py:113
  232.3 306.0 %copy-start.28 = (f32[192]{0:T(256)}, f32[192]{0:T(256)S(1)}, u32[]{:S(2)}) copy-start(f32[192]{0:T(256)S(1)} %fusion.73) | copy-start | bytes 2308
  234.5 206.1 %all-gather.16.cloned.1.call-start = ((), (), s32[]{:S(2)}) async-start(), calls=%async_computation.15 | async-start | bytes 5308416 | tf_op jit(solution)/shard_map/all_gather | solution.py:113
  235.4 300.8 %reduce-scatter.13.cloned.1.call-start = ((), (), s32[]{:S(2)}) async-start(), calls=%async_computation.16 | async-start | bytes 5308416 | tf_op jit(solution)/shard_map/reduce_scatter | solution.py:117
  388.4 12.9 %copy-start.36 = (bf16[1536,1536]{1,0:T(8,128)(2,1)S(1)}, bf16[1536,1536]{1,0:T(8,128)(2,1)}, u32[]{:S(2)}) copy-start(bf16[1536,1536]{1,0:T(8,128)(2,1)} %all-gather.14.cloned.1.call-done) | copy-start | bytes 14155780
  458.3 11.0 %copy-start.38 = (bf16[1536,1120]{0,1:T(8,128)(2,1)}, bf16[1536,1120]{0,1:T(8,128)(2,1)S(1)}, u32[]{:S(2)}) copy-start(bf16[1536,1120]{0,1:T(8,128)(2,1)S(1)} %get-tuple-element.109) | copy-start | bytes 10321924
  458.3 11.0 %copy-start.39 = (bf16[1536,1120]{0,1:T(8,128)(2,1)}, bf16[1536,1120]{0,1:T(8,128)(2,1)S(1)}, u32[]{:S(2)}) copy-start(bf16[1536,1120]{0,1:T(8,128)(2,1)S(1)} %get-tuple-element.108) | copy-start | bytes 10321924
  482.7 101.9 %all-gather.18.cloned.1.call-start = ((), (), s32[]{:S(2)}) async-start(), calls=%async_computation.17 | async-start | bytes 1769472 | tf_op jit(solution)/shard_map/all_gather | solution.py:113
  507.9 28.3 %copy-start.3 = (bf16[192,1536]{1,0:T(8,128)(2,1)S(1)}, bf16[192,1536]{1,0:T(8,128)(2,1)}, u32[]{:S(2)}) copy-start(bf16[192,1536]{1,0:T(8,128)(2,1)} %reduce-scatter.9.cloned.1.call-done) | copy-start | bytes 1769476
  538.4 12.1 %copy-start.32 = (f32[192]{0:T(256)}, f32[192]{0:T(256)S(1)}, u32[]{:S(2)}) copy-start(f32[192]{0:T(256)S(1)} %multiply_multiply_fusion.1) | copy-start | bytes 2308
  540.7 146.1 %reduce-scatter.17.cloned.1.call-start = ((), (), s32[]{:S(2)}) async-start(), calls=%async_computation.19 | async-start | bytes 13271040 | tf_op jit(solution)/shard_map/reduce_scatter | solution.py:117
  583.7 114.6 %reduce-scatter.15.cloned.1.call-start = ((), (), s32[]{:S(2)}) async-start(), calls=%async_computation.18 | async-start | bytes 1769472 | tf_op jit(solution)/shard_map/reduce_scatter | solution.py:117
  613.1 3.3 copy-start.2
  613.1 3.3 copy-start.27
  614.8 3.0 copy-start.18
  616.4 0.8 copy-start.9
  617.1 0.6 copy-start.20
  622.2 182.7 %reduce-scatter.11.cloned.1.call-start = ((), (), s32[]{:S(2)}) async-start(), calls=%async_computation.14 | async-start | bytes 5308416 | tf_op jit(solution)/shard_map/reduce_scatter | solution.py:117
  634.9 3.3 copy-start.10
  634.9 307.6 %reduce-scatter.19.cloned.1.call-start = ((), (), s32[]{:S(2)}) async-start(), calls=%async_computation.21 | async-start | bytes 5849088
  635.2 3.0 copy-start.12
  635.2 3.0 copy-start.19
  635.3 3.0 copy-start.21
  650.9 47.5 %copy-start.25 = (f32[1536]{0:T(1024)S(1)}, f32[1536]{0:T(1024)}, u32[]{:S(2)}) copy-start(f32[1536]{0:T(1024)} %copy-done.24) | copy-start | bytes 18436
  686.8 118.1 %copy-start.5 = (bf16[192,1536]{1,0:T(8,128)(2,1)S(1)}, bf16[192,1536]{1,0:T(8,128)(2,1)}, u32[]{:S(2)}) copy-start(bf16[192,1536]{1,0:T(8,128)(2,1)} %reduce-scatter.13.cloned.1.call-done) | copy-start | bytes 1769476
  686.8 260.3 %all-to-all-start.3 = ((bf16[4,96,3360]{2,1,0:T(8,128)(2,1)}), bf16[4,96,3360]{2,1,0:T(8,128)(2,1)}, u32[]{:S(2)}, u32[]{:S(2)}) async-start(bf16[4,96,3360]{2,1,0:T(8,128)(2,1)} %bitcast.149), calls=%async_computation.8 | async-start | bytes 5308416 | tf_op jit(solution)/shard_map/all_to_all | solution.py:228
Sparse Core Ops, SparseCore 0:
  58.1 5.0 all-gather.9
  66.6 88.3 all-gather.11
  183.5 9.0 reduce-scatter.8
  540.8 7.6 all-gather.17
Sparse Core Ops, SparseCore 1:
  230.9 104.0 all-gather.19
  337.2 51.2 all-gather.13
  390.6 49.9 all-gather.15
  482.8 53.4 reduce-scatter.12
  583.8 102.9 reduce-scatter.16
  689.7 8.6 reduce-scatter.14
  700.5 92.0 reduce-scatter.10
  797.7 144.8 reduce-scatter.18

commit v2 on v1

--- a/solution.py
+++ b/solution.py
@@ -1,8 +1,11 @@
+import functools
 import math
 
 import jax
 import jax.numpy as jnp
 from jax import lax
+from jax.experimental import pallas as pl
+from jax.experimental.pallas import tpu as pltpu
 from jax.sharding import PartitionSpec as P
 
 NORM_EPS = 1e-06
@@ -103,6 +106,386 @@
         "hqk,qhd->kd", grad_scores, query_rot, preferred_element_type=jnp.float32
     )
     return (query_grad, key_grad, value_grad)
+
+
+MESH_ID = pl.DeviceIdType.MESH
+PLANE = 4
+
+
+def flipped(index, mask):
+    bit = 1
+    while bit <= mask:
+        if mask & bit:
+            index = index + bit - 2 * bit * lax.rem(lax.div(index, bit), 2)
+        bit *= 2
+    return index
+
+
+def here():
+    return (lax.axis_index("z"), lax.axis_index("p"), lax.axis_index("head"))
+
+
+def greet(peers):
+    bar = pltpu.get_barrier_semaphore()
+    for peer in peers:
+        pl.semaphore_signal(bar, inc=1, device_id=peer, device_id_type=MESH_ID)
+    pl.semaphore_wait(bar, len(peers))
+
+
+def gather_kernel(
+    quarters,
+    part_cols,
+    aset,
+    small,
+    gate,
+    up,
+    down,
+    grad,
+    aset_all,
+    small_all,
+    gate_all,
+    up_all,
+    down_all,
+    grad_all,
+    a_send,
+    a_recv,
+    m_send,
+    m_recv,
+    s_send,
+    s_recv,
+    g_send,
+    g_recv,
+    l_sem,
+):
+    z, p, c = here()
+    dp = z * PLANE + p
+    hidden = gate.shape[1]
+
+    def at(zz, pp):
+        return (zz, pp, c)
+
+    def send(src, dst, ssem, rsem, peer):
+        copy = pltpu.make_async_remote_copy(
+            src_ref=src, dst_ref=dst, send_sem=ssem, recv_sem=rsem,
+            device_id=peer, device_id_type=MESH_ID,
+        )
+        copy.start()
+        return copy
+
+    pair = (z, p, 1 - c)
+    masks = [(kz, kp) for kz in range(quarters) for kp in range(PLANE) if kz or kp]
+    greet([at(flipped(z, kz), flipped(p, kp)) for kz, kp in masks] + [pair])
+
+    def start_of(quarter):
+        first = jnp.minimum(quarter * part_cols, hidden - part_cols)
+        return pl.multiple_of(first, 128)
+
+    px, py = flipped(p, 1), flipped(p, 2)
+    sent = []
+    arrive = {}
+
+    def own_of(weight):
+        return weight.at[:, pl.ds(start_of(z), part_cols)]
+
+    sets = [
+        (aset_all, aset, lambda zz: aset, a_send, a_recv),
+        (gate_all, own_of(gate), lambda zz: gate.at[:, pl.ds(start_of(zz), part_cols)], m_send.at[0], m_recv.at[0]),
+        (up_all, own_of(up), lambda zz: up.at[:, pl.ds(start_of(zz), part_cols)], m_send.at[1], m_recv.at[1]),
+        (down_all, own_of(down), lambda zz: down.at[:, pl.ds(start_of(zz), part_cols)], m_send.at[2], m_recv.at[2]),
+    ]
+
+    def line(s, k):
+        whole, _, part, ss, rs = sets[s]
+        zz = flipped(z, k)
+        sent.append(send(part(zz), whole.at[dp], ss.at[k, 0], rs.at[k, 0], at(zz, p)))
+
+    def fan(s, k):
+        whole, own, _, ss, rs = sets[s]
+        slot = flipped(z, k) * PLANE + p
+        src = own if k == 0 else whole.at[slot]
+        if k:
+            landed(s, k, 0)
+        sent.append(send(src, whole.at[slot], ss.at[k, 1], rs.at[k, 1], at(z, px)))
+        sent.append(send(src, whole.at[slot], ss.at[k, 2], rs.at[k, 2], at(z, py)))
+
+    def landed(s, k, role):
+        whole, _, _, ss, rs = sets[s]
+        slot = flipped(z, k) * PLANE + flipped(p, role)
+        pltpu.make_async_copy(whole.at[slot], whole.at[slot], rs.at[k, role]).wait()
+
+    def relay(s, k):
+        whole, _, _, ss, rs = sets[s]
+        role = 1 if k % 2 == 0 else 2
+        landed(s, k, role)
+        slot = flipped(z, k) * PLANE + flipped(p, role)
+        to = py if role == 1 else px
+        sent.append(send(whole.at[slot], whole.at[slot], ss.at[k, 3], rs.at[k, 3], at(z, to)))
+
+    def rest(s, k):
+        landed(s, k, 2 if k % 2 == 0 else 1)
+        landed(s, k, 3)
+
+    for n, (kz, kp) in enumerate(masks):
+        sent.append(send(small, small_all.at[dp], s_send.at[n], s_recv.at[n], at(flipped(z, kz), flipped(p, kp))))
+    local = [
+        pltpu.make_async_copy(small, small_all.at[dp], l_sem.at[0]),
+        pltpu.make_async_copy(aset, aset_all.at[dp], l_sem.at[1]),
+        pltpu.make_async_copy(sets[1][1], gate_all.at[dp], l_sem.at[2]),
+        pltpu.make_async_copy(sets[2][1], up_all.at[dp], l_sem.at[3]),
+        pltpu.make_async_copy(sets[3][1], down_all.at[dp], l_sem.at[4]),
+        pltpu.make_async_copy(grad, grad_all.at[0, c], l_sem.at[5]),
+    ]
+    fan(0, 0)
+    for k in range(1, quarters):
+        line(0, k)
+    for s in (1, 2, 3):
+        for k in range(1, quarters):
+            line(s, k)
+    for copy in local:
+        copy.start()
+    sent.append(send(grad, grad_all.at[0, c], g_send.at[0, 1], g_recv.at[0, 1], pair))
+    for k in range(1, quarters):
+        sent.append(send(grad, grad_all.at[k, c], g_send.at[k, 0], g_recv.at[k, 0], at(flipped(z, k), p)))
+    fan(1, 0)
+    relay(0, 0)
+    for k in range(1, quarters):
+        fan(0, k)
+    fan(2, 0)
+    fan(3, 0)
+    for k in range(1, quarters):
+        relay(0, k)
+    relay(1, 0)
+    for k in range(1, quarters):
+        fan(1, k)
+    relay(2, 0)
+    relay(3, 0)
+    for k in range(1, quarters):
+        fan(2, k)
+        relay(1, k)
+    for k in range(1, quarters):
+        fan(3, k)
+        relay(2, k)
+    for k in range(1, quarters):
+        relay(3, k)
+    for k in range(1, quarters):
+        slot = grad_all.at[k, c]
+        pltpu.make_async_copy(slot, slot, g_recv.at[k, 0]).wait()
+        sent.append(send(slot, slot, g_send.at[k, 1], g_recv.at[k, 1], pair))
+    for k in range(quarters):
+        slot = grad_all.at[k, 1 - c]
+        pltpu.make_async_copy(slot, slot, g_recv.at[k, 1]).wait()
+    for s in range(4):
+        for k in range(quarters):
+            rest(s, k)
+    for n, (kz, kp) in enumerate(masks):
+        slot = small_all.at[flipped(z, kz) * PLANE + flipped(p, kp)]
+        pltpu.make_async_copy(slot, slot, s_recv.at[n]).wait()
+    for copy in local:
+        copy.wait()
+    for copy in sent:
+        copy.wait_send()
+
+
+def gather_all(aset, small, gate, up, down, grad, shards, part_cols):
+    quarters = shards // PLANE
+    bf = jnp.bfloat16
+    depth = aset.shape[0]
+    dma = pltpu.SemaphoreType.DMA
+    part = jax.ShapeDtypeStruct((shards, depth, part_cols), bf)
+    return pl.pallas_call(
+        functools.partial(gather_kernel, quarters, part_cols),
+        out_shape=(
+            jax.ShapeDtypeStruct((shards,) + aset.shape, bf),
+            jax.ShapeDtypeStruct((shards,) + small.shape, bf),
+            part,
+            part,
+            part,
+            jax.ShapeDtypeStruct((quarters, 2) + grad.shape, bf),
+        ),
+        in_specs=[pl.BlockSpec(memory_space=pl.ANY)] * 6,
+        out_specs=[pl.BlockSpec(memory_space=pl.ANY)] * 6,
+        scratch_shapes=[
+            dma((quarters, 4)),
+            dma((quarters, 4)),
+            dma((3, quarters, 4)),
+            dma((3, quarters, 4)),
+            dma((shards - 1,)),
+            dma((shards - 1,)),
+            dma((quarters, 2)),
+            dma((quarters, 2)),
+            dma((6,)),
+        ],
+        compiler_params=pltpu.CompilerParams(collective_id=0, has_side_effects=True),
+    )(aset, small, gate, up, down, grad)
+
+AHEAD = 1
+LAG = 1
+PARTS = (1, 2, 3, 0)
+def reduce_kernel(
+    quarters,
+    small,
+    attn,
+    gate,
+    up,
+    down,
+    small_sum,
+    attn_sum,
+    gate_out,
+    up_out,
+    down_out,
+    small_all,
+    attn_slots,
+    mlp_slots,
+    attn_line,
+    staged,
+    t_send,
+    t_recv,
+    z_send,
+    z_recv,
+    s_send,
+    s_recv,
+    l_sem,
+):
+    z, p, c = here()
+    pair = (z, p, 1 - c)
+    masks = [(kz, kp) for kz in range(quarters) for kp in range(PLANE) if kz or kp]
+    greet([(flipped(z, kz), flipped(p, kp), c) for kz, kp in masks] + [pair])
+    sent = []
+
+    def send(src, dst, ssem, rsem, peer):
+        copy = pltpu.make_async_remote_copy(
+            src_ref=src, dst_ref=dst, send_sem=ssem, recv_sem=rsem,
+            device_id=peer, device_id_type=MESH_ID,
+        )
+        copy.start()
+        sent.append(copy)
+
+    def landed(ref, sem):
+        pltpu.make_async_copy(ref, ref, sem).wait()
+
+    side = [(z, flipped(p, 1), c), (z, flipped(p, 2), c)]
+    sources = (attn, gate, up, down)
+    outs = (None, gate_out, up_out, down_out)
+
+    def slots(s, k, role):
+        return attn_slots.at[k, role] if s == 0 else mlp_slots.at[s - 1, k, role]
+
+    def block(s, k, kp):
+        return sources[s].at[flipped(z, k) * PLANE + flipped(p, kp)]
+
+    def first(s, k):
+        way = k % 2
+        send(block(s, k, 3), slots(s, k, 0), t_send.at[s, k, 0], t_recv.at[s, k, 0], side[way])
+        send(block(s, k, 1 + way), slots(s, k, 1), t_send.at[s, k, 1], t_recv.at[s, k, 1], side[way])
+
+    def add(ref, other):
+        total = ref[...].astype(jnp.float32) + other[...].astype(jnp.float32)
+        ref[...] = total.astype(ref.dtype)
+
+    def relay(s, k):
+        way = k % 2
+        slot = slots(s, k, 0)
+        landed(slot, t_recv.at[s, k, 0])
+        add(slot, block(s, k, 2 - way))
+        send(slot, slots(s, k, 2), t_send.at[s, k, 2], t_recv.at[s, k, 2], side[1 - way])
+
+    local = []
+
+    def last(s, k):
+        one, two = (slots(s, k, 1), slots(s, k, 2))
+        landed(one, t_recv.at[s, k, 1])
+        landed(two, t_recv.at[s, k, 2])
+        total = (
+            block(s, k, 0)[...].astype(jnp.float32)
+            + one[...].astype(jnp.float32)
+            + two[...].astype(jnp.float32)
+        )
+        one[...] = total.astype(one.dtype)
+        if s == 0:
+            if k:
+                send(one, attn_line.at[k], z_send.at[s, k], z_recv.at[s, k], (flipped(z, k), p, c))
+        elif k:
+            send(one, outs[s].at[z], z_send.at[s, k], z_recv.at[s, k], (flipped(z, k), p, c))
+        else:
+            copy = pltpu.make_async_copy(one, outs[s].at[z], l_sem.at[s])
+            copy.start()
+            local.append(copy)
+
+    dp = z * PLANE + p
+    for n, (kz, kp) in enumerate(masks):
+        send(small, small_all.at[dp], s_send.at[n], s_recv.at[n], (flipped(z, kz), flipped(p, kp), c))
+    ks = list(range(1, quarters)) + [0]
+    order = [(s, k) for i in range(0, quarters, 2) for s in PARTS for k in ks[i : i + 2]]
+    for i in range(-AHEAD, len(order) + LAG):
+        if 0 <= i + AHEAD < len(order):
+            first(*order[i + AHEAD])
+        if 0 <= i < len(order):
+            relay(*order[i])
+        if 0 <= i - LAG:
+            last(*order[i - LAG])
+    small_all[dp] = small[...]
+    for n, (kz, kp) in enumerate(masks):
+        slot = small_all.at[flipped(z, kz) * PLANE + flipped(p, kp)]
+        landed(slot, s_recv.at[n])
+    total = small_all[0]
+    for i in range(1, quarters * PLANE):
+        total = total + small_all[i]
+    staged[...] = total
+    small_sum[c] = total
+    send(staged, small_sum.at[c], s_send.at[len(masks)], s_recv.at[len(masks)], pair)
+    landed(small_sum.at[1 - c], s_recv.at[len(masks)])
+    for k in range(1, quarters):
+        landed(attn_line.at[k], z_recv.at[0, k])
+    total = attn_slots[0, 1].astype(jnp.float32)
+    for k in range(1, quarters):
+        total = total + attn_line[k].astype(jnp.float32)
+    attn_sum[...] = total
+    for s in (1, 2, 3):
+        for k in range(1, quarters):
+            landed(outs[s].at[flipped(z, k)], z_recv.at[s, k])
+    for copy in local:
+        copy.wait()
+    for copy in sent:
+        copy.wait_send()
+
+
+def reduce_all(small, attn, gate, up, down, shards):
+    quarters = shards // PLANE
+    bf = jnp.bfloat16
+    dma = pltpu.SemaphoreType.DMA
+    depth, part_cols = gate.shape[1:]
+    vmem = pl.BlockSpec(memory_space=pltpu.VMEM)
+    hbm = pl.BlockSpec(memory_space=pl.ANY)
+    quarter_out = jax.ShapeDtypeStruct((quarters, depth, part_cols), bf)
+    return pl.pallas_call(
+        functools.partial(reduce_kernel, quarters),
+        out_shape=(
+            jax.ShapeDtypeStruct((2,) + small.shape, jnp.float32),
+            jax.ShapeDtypeStruct(attn.shape[1:], jnp.float32),
+            quarter_out,
+            quarter_out,
+            quarter_out,
+        ),
+        in_specs=[vmem] * 5,
+        out_specs=[vmem, vmem, hbm, hbm, hbm],
+        scratch_shapes=[
+            pltpu.VMEM((shards,) + small.shape, jnp.float32),
+            pltpu.VMEM((quarters, 3) + attn.shape[1:], bf),
+            pltpu.VMEM((3, quarters, 3, depth, part_cols), bf),
+            pltpu.VMEM((quarters,) + attn.shape[1:], bf),
+            pltpu.VMEM(small.shape, jnp.float32),
+            dma((4, quarters, 3)),
+            dma((4, quarters, 3)),
+            dma((4, quarters)),
+            dma((4, quarters)),
+            dma((shards,)),
+            dma((shards,)),
+            dma((4,)),
+        ],
+        compiler_params=pltpu.CompilerParams(
+            collective_id=1, has_side_effects=True, vmem_limit_bytes=50 * 2**20
+        ),
+    )(small, attn, gate, up, down)
 
 
 DP = ("z", "p")
@@ -136,10 +519,9 @@
 ):
     bf = jnp.bfloat16
     quarters = lax.axis_size("z")
-    plane = lax.axis_size("p")
     lanes = lax.axis_size("head")
     lane_index = lax.axis_index("head")
-    shards = quarters * plane
+    shards = quarters * PLANE
     local_rows = hidden_in.shape[0]
     token_count = local_rows * lanes
     depth = norm_attn.shape[0]
@@ -148,7 +530,10 @@
     query_width = w_query.shape[1]
     group_heads = query_width // head_dim
     hidden_width = w_gate.shape[1]
-    part_width = hidden_width // quarters
+    part_width = -(-hidden_width // (128 * quarters)) * 128
+    quarter = lax.axis_index("z")
+    first_unit = jnp.minimum(quarter * part_width, hidden_width - part_width)
+    valid = first_unit + jnp.arange(part_width, dtype=jnp.int32) >= quarter * part_width
     segment, positions = layout(row_lengths[0], token_count)
     cosine, sine_tab = rotary_tables(positions, head_dim)
     cosine = cosine[:, None, :]
@@ -156,10 +541,25 @@
     place = jnp.arange(token_count, dtype=jnp.int32)
     allowed = (segment[:, None] == segment[None, :]) & (place[None, :] <= place[:, None])
 
-    attn_set = gather(jnp.concatenate([w_query, w_key, w_value, w_out.T], 1), DP)
-    small = gather(
-        jnp.concatenate([norm_attn, norm_mlp, b_query[0], b_key[0], b_value[0]])[None], DP
-    )
+    small = jnp.concatenate([norm_attn, norm_mlp, b_query[0], b_key[0], b_value[0]])
+    used = small.shape[0]
+    rows_used = -(-used // (128 * 16)) * 16
+    small = jnp.pad(small, (0, rows_used * 128 - used)).reshape(rows_used, 128)
+    attn_set, small, wg, wu, wd_rows, grad_rows = gather_all(
+        jnp.concatenate([w_query, w_key, w_value, w_out.T], 1),
+        small,
+        w_gate,
+        w_up,
+        w_down.T,
+        out_grad.astype(bf),
+        shards,
+        part_width,
+    )
+    attn_set = attn_set.reshape(width, attn_set.shape[2])
+    small = small.reshape(shards, rows_used * 128)
+    wg, wu, wd_rows = [w.reshape(width, part_width) for w in (wg, wu, wd_rows)]
+    grad_rows = grad_rows[lax.bitwise_xor(jnp.arange(quarters, dtype=jnp.int32), quarter)]
+    grad_rows = grad_rows.reshape(quarters * token_count, width)
     wq_full = attn_set[:, :query_width]
     wk_full = attn_set[:, query_width : query_width + head_dim]
     wv_full = attn_set[:, query_width + head_dim : query_width + 2 * head_dim]
@@ -169,20 +569,6 @@
     gain_attn, gain_mlp, bias_query, bias_key, bias_value = [
         small[:, edges[i] : edges[i + 1]].reshape(-1).astype(jnp.float32) for i in range(5)
     ]
-
-    def hidden_parts(rows):
-        split = rows.reshape(depth, quarters, part_width).transpose(1, 0, 2)
-        mine = lax.all_to_all(split, "z", 0, 0, tiled=True)
-        return mine
-
-    mlp_set = jnp.concatenate(
-        [hidden_parts(w_gate), hidden_parts(w_up), hidden_parts(w_down.T)], -1
-    )
-    mlp_set = lax.all_gather(mlp_set, "p", axis=1, tiled=False).reshape(width, 3 * part_width)
-    wg = mlp_set[:, :part_width]
-    wu = mlp_set[:, part_width : 2 * part_width]
-    wd_rows = mlp_set[:, 2 * part_width :]
-    grad_rows = gather(out_grad.astype(bf), POOL)
 
     normed_low = gather(rms_norm(hidden_in, gain_attn).astype(bf), "head")
     query_pre = product(normed_low, wq_full) + bias_query
@@ -198,8 +584,8 @@
         jnp.float32
     )
     mlp_low = gather(rms_norm(residual, gain_mlp).astype(bf), POOL)
-    gate_pre = product(mlp_low, wg)
-    up_pre = product(mlp_low, wu)
+    gate_pre = jnp.where(valid, product(mlp_low, wg), 0.0)
+    up_pre = jnp.where(valid, product(mlp_low, wu), 0.0)
     sigmoid_gate = jax.nn.sigmoid(gate_pre)
     silu_gate = gate_pre * sigmoid_gate
     hidden_low = (silu_gate * up_pre).astype(bf)
@@ -214,27 +600,14 @@
     grad_normed_mlp = scatter_sum(
         contract_last(grad_gate, wg) + contract_last(grad_up, wu), POOL
     ).astype(jnp.float32)
-    mlp_terms = jnp.concatenate(
-        [
-            contract_first(mlp_low, grad_gate),
-            contract_first(mlp_low, grad_up),
-            contract_first(grad_rows, hidden_low),
-        ],
-        1,
-    ).astype(bf)
-    mlp_terms = mlp_terms.reshape(quarters, plane, depth, 3 * part_width).transpose(1, 0, 2, 3)
-    mlp_terms = scatter_sum(mlp_terms.reshape(width, 3 * part_width), "p")
-    mlp_terms = mlp_terms.reshape(quarters, depth, 3 * part_width)
-    mlp_terms = lax.all_to_all(mlp_terms, "z", 0, 0, tiled=True).astype(jnp.float32)
-
-    def whole_rows(index):
-        piece = mlp_terms[:, :, index * part_width : (index + 1) * part_width]
-        return piece.transpose(1, 0, 2).reshape(depth, hidden_width)
-
-    grad_w_gate, grad_w_up = (whole_rows(0), whole_rows(1))
-    grad_w_down = (
-        mlp_terms[:, :, 2 * part_width :].transpose(0, 2, 1).reshape(hidden_width, depth)
-    )
+    mlp_terms = [
+        contract_first(left, right).astype(bf).reshape(shards, depth, part_width)
+        for left, right in (
+            (mlp_low, grad_gate),
+            (mlp_low, grad_up),
+            (grad_rows, hidden_low),
+        )
+    ]
 
     _, mlp_pull = jax.vjp(rms_norm, residual, gain_mlp)
     grad_residual_part, grad_gain_mlp = mlp_pull(grad_normed_mlp)
@@ -264,12 +637,28 @@
     attn_terms = jnp.concatenate(
         [contract_first(normed_low, grad_qkv), contract_first(grad_attn_rows, heads_low)], 1
     )
-    attn_part = scatter_sum(attn_terms, DP).astype(jnp.float32)
     bias_vec = jnp.sum(grad_qkv.astype(jnp.float32), 0)
-    lane_pick = (jnp.arange(lanes, dtype=jnp.int32) == lane_index).astype(jnp.float32)
-    bias_rows = lane_pick[:, None] * bias_vec[None, :]
-    gain_rows = jnp.stack([grad_gain_attn, grad_gain_mlp])
-    gain_total, bias_total = lax.psum((gain_rows, bias_rows), ("z", "p", "head"))
+    small_grads = jnp.concatenate([grad_gain_attn, grad_gain_mlp, bias_vec]).reshape(-1, 128)
+    small_total, attn_part, *quarter_grads = reduce_all(
+        small_grads,
+        attn_terms.astype(bf).reshape(shards, depth, attn_terms.shape[1]),
+        *mlp_terms,
+        shards,
+    )
+    small_total = small_total.reshape(lanes, -1)
+    gain_total = jnp.sum(small_total[:, : 2 * width], 0).reshape(2, width)
+    bias_total = small_total[:, 2 * width :]
+
+    def whole_rows(parts):
+        taken = []
+        for index in range(quarters):
+            skip = max(0, index * part_width - (hidden_width - part_width))
+            if skip < part_width:
+                taken.append(parts[index][:, skip:])
+        return jnp.concatenate(taken, 1).astype(jnp.float32)
+
+    grad_w_gate, grad_w_up, grad_w_down = [whole_rows(parts) for parts in quarter_grads]
+    grad_w_down = grad_w_down.T
     return (
         block_out,
         grad_in,

time: 983 us -> 673 us (0.68)
  waiting for transfers between devices: 482 us -> 132 us
  Pallas kernels: 0 us -> 300 us
  blocking collectives: 165 us -> 0 us
  local copies, waits for them, and re-layouts: 101 us -> 30.9 us
  matrix products: 154 us -> 141 us
  starting transfers between devices: 13.7 us -> 0.82 us
    pallas_call x0 -> x2, Pallas kernels: none -> 300 us  [the longest x1 156 us: reduce_all(): pl.pallas_call(functools.partial(reduce_kernel, quarters), out_shape=(jax...]
    unnamed x13 -> x7, waiting for transfers between devices: 134 us -> 0.11 us
    all_gather x5 -> x3, waiting for transfers between devices: 169 us -> 67.8 us  [gather(): return lax.all_gather(x, axes, axis=0, tiled=True)]
    all_gather x1 -> x0, waiting for transfers between devices: 99.3 us -> none  [local(): lax.all_gather(mlp_set, 'p', axis=1, tiled=False)]
    psum x1 -> x0, blocking collectives: 98 us -> none  [local(): lax.psum((gain_rows, bias_rows), ('z', 'p', 'head'))]
    all_gather x1 -> x0, blocking collectives: 42.4 us -> none  [gather(): return lax.all_gather(x, axes, axis=0, tiled=True)]
    all_to_all x1 -> x0, blocking collectives: 24.2 us -> none  [hidden_parts(): mine = lax.all_to_all(split, 'z', 0, 0, tiled=True)]
    concatenate x2 -> x0, local copies, waits for them, and re-layouts: 23.6 us -> none  [the longest x1 18.3 us: local(): jnp.concatenate([contract_first(mlp_low, grad_gate), contract_first(mlp_l...]
  transfers between devices with their start and end apart: 15 -> 7, of which waited for: 9 -> 5; matrix products, arithmetic and copies ran while one was open for 23% -> 11% of each run, Pallas kernels for 0% -> 24%
where the time goes in v2:
time: 673 us; the launch traced here: 660 us
  Pallas kernels  300 us (45%)
  matrix products  141 us (21%)
  waiting for transfers between devices  132 us (20%)
  other arithmetic  40.9 us (6%)
  local copies, waits for them, and re-layouts  30.9 us (5%)
  between operations  15.3 us (2%)
    pallas_call x1, Pallas kernels, reduce_all(): pl.pallas_call(functools.partial(reduce_kernel, quarters), out_shape=(jax...  156 us
    pallas_call x1, Pallas kernels, gather_all(): pl.pallas_call(functools.partial(gather_kernel, quarters, part_cols), out...  144 us
    all_gather x3, waiting for transfers between devices, gather(): return lax.all_gather(x, axes, axis=0, tiled=True)  67.8 us
    reduce_scatter x4, waiting for transfers between devices, scatter_sum(): lax.psum_scatter(x.astype(jnp.bfloat16), axes, scatter_dimension=0, tiled...  63.7 us
    dot_general x7, matrix products, product(): return jnp.dot(left_side, right_side, preferred_element_type=jnp.float32)  43 us
    dot_general x5, matrix products, contract_last(): lax.dot_general(left_side, right_side, (((1,), (1,)), ((), ())), preferre...  38.8 us
    dot_general x5, matrix products, contract_first(): lax.dot_general(left_side, right_side, (((0,), (0,)), ((), ())), preferre...  34.8 us
  transfers between devices with their start and end apart: 7, of which 5 were waited for; matrix products, arithmetic and copies ran while one was open for 11% of the time, Pallas kernels for 24%

profile of v2, /device:TPU:0, one launch (start us, length us, event | category | flops | bytes accessed | tf_op | source)
XLA Modules:
  0.0 660.2 jit_solution(5368990410188089502)
XLA Ops:
  7.3 1.5 multiply_reduce_fusion.1
  8.8 3.4 concatenate.57
  12.8 2.1 convert_element_type.179.grad
  15.0 0.8 pad_maximum_fusion.2.aset
  15.8 144.0 %shard_map.254 = (bf16[16,96,1792]{2,1,0:T(8,128)(2,1)}, bf16[16,16,128]{2,1,0:T(8,128)(2,1)}, bf16[16,96,1152]{2,1,0:T(8,128)(2,1)}, bf16[16,96,1152]{2,1,0:T(8...) custom-call(bf16[96,1792]{1,0:T(8,128)(2,1)} %pad_maximum_fusion.2.aset, ...), custom_call_target="tpu_custom_call" | custom-call | tf_op jit(solution)/shard_map/pallas_call | solution.py:295
  159.8 0.9 copy.91
  161.4 1.0 multiply_convert_fusion.4
  163.7 0.8 fusion.53
  164.5 1.1 multiply_cosine_fusion
  165.6 14.3 %all-gather.4.cloned.1.call-done = bf16[384,1536]{1,0:T(8,128)(2,1)} async-done(((bf16[192,1536]{1,0:T(8,128)(2,1)}), bf16[384,1536]{1,0:T(8,128)(2,1)}) %all-gather.4.cloned.1.call-update) | async-done | bytes 1179664 | tf_op jit(solution)/shard_map/all_gather | solution.py:496
  179.9 1.8 convolution_add_fusion
  183.2 3.1 fusion.29
  186.7 2.4 pad_maximum_fusion.3
  189.8 1.4 copy.60
  191.3 0.8 copy-done.21
  192.2 1.4 copy.62
  194.0 2.6 add_convert_fusion.2
  196.6 1.4 copy.63
  198.0 1.7 fusion.74
  200.3 1.7 copy-done.17
  201.9 1.5 fusion.51
  203.4 0.8 fusion.35
  204.3 4.1 convolution_convert_fusion.5
  208.5 9.8 %reduce-scatter.5.cloned.1.call-done = bf16[192,1536]{1,0:T(8,128)(2,1)} async-done(((bf16[384,1536]{1,0:T(8,128)(2,1)}), bf16[192,1536]{1,0:T(8,128)(2,1)}) %reduce-scatter.5.cloned.1.call-update) | async-done | bytes 589840 | tf_op jit(solution)/shard_map/reduce_scatter | solution.py:500
  218.4 1.3 multiply_reduce_fusion
  220.8 2.1 multiply_convert_fusion.3
  223.5 5.3 gather_fusion
  228.8 47.1 %all-gather.6.cloned.1.call-done = bf16[1536,1536]{1,0:T(8,128)(2,1)} async-done(((bf16[192,1536]{1,0:T(8,128)(2,1)}), bf16[1536,1536]{1,0:T(8,128)(2,1)}) %all-gather.6.cloned.1.call-update) | async-done | bytes 4718608 | tf_op jit(solution)/shard_map/all_gather | solution.py:496
  276.0 11.1 %convolution_select_fusion = f32[1536,1152]{1,0:T(8,128)} fusion(bf16[1536,1536]{1,0:T(8,128)(2,1)} %all-gather.6.cloned.1.call-done, bf16[1536,1152]{1,0:T(8,128)(2,1)} %bitcast.209, pred[1152]{0:T(1024)(128)(4,1)S(1)} %add_compare_fusion), kind=kOutput, calls=%fused_computation.2 | convolution fusion | flops 5437587456 | bytes 15336576 | tf_op jit(solution)/shard_map/dot_general | solution.py:59
  287.1 8.2 %convolution_select_fusion.1 = f32[1536,1152]{1,0:T(8,128)} fusion(bf16[1536,1536]{1,0:T(8,128)(2,1)S(1)} %copy-done.44, bf16[1536,1152]{1,0:T(8,128)(2,1)S(1)} %bitcast.211, pred[1152]{0:T(1024)(128)(4,1)S(1)} %add_compare_fusion), kind=kOutput, calls=%fused_computation.3 | convolution fusion | flops 5437587456 | bytes 15336576 | tf_op jit(solution)/shard_map/dot_general | solution.py:59
  295.4 13.4 %multiply_convert_fusion = (bf16[1536,1152]{1,0:T(8,128)(2,1)}, bf16[1536,1152]{1,0:T(8,128)(2,1)S(1)}, bf16[1536,1152]{1,0:T(8,128)(2,1)}) fusion(f32[1536,1152]{1,0:T(8,128)} %convolution_select_fusion.1, f32[1536,1152]{1,0:T(8,128)} %convolution_select_fusion, bf16[1536,1536]{1,0:T(8,128)(2,1)S(1)} %bitcast.171, bf16[1536,1152]{1,0:T(8,128)(2,1)S(1)} %bitcast.208), kind=kOutput, calls=%fused_computation.9 | convolution fusion | flops 5462360064 | bytes 33030144 | tf_op jit(solution)/shard_map/dot_general | solution.py:59
  308.8 9.0 %fusion.75 = f32[1536,1536]{1,0:T(8,128)} fusion(bf16[1536,1152]{1,0:T(8,128)(2,1)S(1)} %get-tuple-element.43, bf16[1536,1152]{1,0:T(8,128)(2,1)S(1)} %bitcast.212), kind=kOutput, calls=%fused_computation.161 | convolution fusion | flops 5435817984 | bytes 16515072 | tf_op jit(solution)/shard_map/dot_general | solution.py:63
  317.7 10.7 %add_convert_fusion = bf16[1536,1536]{1,0:T(8,128)(2,1)} fusion(f32[1536,1536]{1,0:T(8,128)} %fusion.75, bf16[1536,1152]{1,0:T(8,128)(2,1)S(1)} %copy-done.52, bf16[1536,1152]{1,0:T(8,128)(2,1)S(1)} %bitcast.210), kind=kOutput, calls=%fused_computation.4 | convolution fusion | flops 5440536576 | bytes 21233664 | tf_op jit(solution)/shard_map/dot_general | solution.py:63
  328.5 53.9 %reduce-scatter.9.cloned.1.call-done = bf16[192,1536]{1,0:T(8,128)(2,1)} async-done(((bf16[1536,1536]{1,0:T(8,128)(2,1)}), bf16[192,1536]{1,0:T(8,128)(2,1)}) %reduce-scatter.9.cloned.1.call-update) | async-done | bytes 589840 | tf_op jit(solution)/shard_map/reduce_scatter | solution.py:500
  382.3 2.2 fusion.38
  384.6 0.7 multiply_multiply_fusion.1
  385.8 1.9 fusion.69
  387.7 1.3 log_add_fusion
  389.1 6.4 all-gather.8.cloned.1.call-done
  395.4 3.9 fusion.32
  399.4 2.1 copy.68
  401.5 3.6 fusion.76
  405.1 1.3 fusion.47
  406.4 8.4 %fusion.43 = f32[384,128]{0,1:T(8,128)} fusion(f32[384,384,6]{1,0,2:T(8,128)} %fusion.76, f32[6,384,384]{1,2,0:T(8,128)} %copy-done.1, f32[6,384]{1,0:T(8,128)} %log_add_fusion, f32[384,6,128]{0,2,1:T(8,128)} %copy-done.7, f32[384,6,128]{0,2,1:T(8,128)} %bitcast.173, f32[384,128]{0,1:T(8,128)} %copy-done.13), kind=kOutput, calls=%fused_computation.76 | convolution fusion | flops 233572992 | bytes 9839616 | tf_op jit(solution)/shard_map/hqk,qhd->kd/dot_general | solution.py:105
  414.8 8.3 %broadcast_multiply_fusion = (f32[384,6,128]{0,2,1:T(8,128)}, f32[384,6,128]{0,2,1:T(8,128)}) fusion(f32[384,128]{0,1:T(8,128)} %get-tuple-element.73, bf16[384,128,1]{0,1,2:T(8,128)(2,1)} %get-tuple-element.72, f32[384,384,6]{1,0,2:T(8,128)} %fusion.76, f32[6,384,384]{1,2,0:T(8,128)} %copy-done.1, f32[6,384]{1,0:T(8,128)} %log_add_fusion), kind=kOutput, calls=%fused_computation.88 | convolution fusion | flops 232983168 | bytes 9741312 | tf_op jit(solution)/shard_map/hqk,kd->qhd/dot_general | solution.py:102
  423.2 1.5 fusion.70
  426.0 4.4 fusion.8
  430.5 10.8 %convolution_convert_fusion.3 = bf16[1536,1536]{1,0:T(8,128)(2,1)} fusion(bf16[1536,1152]{1,0:T(8,128)(2,1)} %get-tuple-element.44, bf16[1536,1152]{1,0:T(8,128)(2,1)} %bitcast.207), kind=kOutput, calls=%fused_computation.8 | convolution fusion | flops 5438177280 | bytes 11796480 | tf_op jit(solution)/shard_map/dot_general | solution.py:63
  441.3 10.6 %convolution_convert_fusion = bf16[1536,1152]{1,0:T(8,128)(2,1)} fusion(bf16[1536,1536]{1,0:T(8,128)(2,1)} %bitcast.168, bf16[1536,1152]{1,0:T(8,128)(2,1)} %get-tuple-element.44), kind=kOutput, calls=%fused_computation.5 | convolution fusion | flops 5437587456 | bytes 11796480 | tf_op jit(solution)/shard_map/dot_general | solution.py:69
  452.0 9.6 %convolution_convert_fusion.1 = bf16[1536,1152]{1,0:T(8,128)(2,1)} fusion(bf16[1536,1536]{1,0:T(8,128)(2,1)} %all-gather.6.cloned.1.call-done, bf16[1536,1152]{1,0:T(8,128)(2,1)S(1)} %copy-done.53), kind=kOutput, calls=%fused_computation.6 | convolution fusion | flops 5437587456 | bytes 11796480 | tf_op jit(solution)/shard_map/dot_general | solution.py:69
  461.5 9.8 %convolution_convert_fusion.2 = bf16[1536,1152]{1,0:T(8,128)(2,1)} fusion(bf16[1536,1536]{1,0:T(8,128)(2,1)} %all-gather.6.cloned.1.call-done, bf16[1536,1152]{1,0:T(8,128)(2,1)S(1)} %copy-done.51), kind=kOutput, calls=%fused_computation.7 | convolution fusion | flops 5437587456 | bytes 11796480 | tf_op jit(solution)/shard_map/dot_general | solution.py:69
  471.3 2.4 copy.73
  473.7 2.0 convert_reduce_fusion
  475.7 3.0 convolution_convert_fusion.6
  478.7 1.9 convolution_convert_fusion.4
  480.6 2.9 pad_maximum_fusion.attn
  483.5 1.5 fusion.39
  485.0 0.7 maximum_bitcast_fusion.small
  485.7 155.7 %shard_map.255 = (f32[2,32,128]{2,1,0:T(8,128)S(1)}, f32[96,1792]{1,0:T(8,128)S(1)}, bf16[4,96,1152]{2,1,0:T(8,128)(2,1)S(1)}, bf16[4,96,1152]{2,1,0:T(8,128)(2,1)S(1)}, bf16[4,96,1152]{2,1,0:T(8,128)(2,1)S(1)}) custom-call(f32[32,128]{1,0:T(8,128)S(1)} %maximum_bitcast_fusion.small, bf16[16,96,1792]{2,1,0:T(8,128)(2,1)} %pad_maximum_fusion.attn, ...), custom_call_target="tpu_custom_call" | custom-call | tf_op jit(solution)/shard_map/pallas_call | solution.py:460
  644.7 0.8 slice_bitcast_fusion
  645.6 1.3 maximum_convert_fusion
  646.9 1.3 maximum_convert_fusion.1
  648.2 1.3 convert_bitcast_fusion
  649.5 3.4 fusion.41
  (167 shorter events, 13.6 us)
Async XLA Ops:
  7.2 7.8 %copy-start.27 = (bf16[768,96]{0,1:T(8,128)(2,1)S(1)}, bf16[768,96]{0,1:T(8,128)(2,1)}, u32[]{:S(2)}) copy-start(bf16[768,96]{0,1:T(8,128)(2,1)} %param.24) | copy-start | bytes 442372
  7.2 7.8 %copy-start.35 = (bf16[96,128]{1,0:T(8,128)(2,1)S(1)}, bf16[96,128]{1,0:T(8,128)(2,1)}, u32[]{:S(2)}) copy-start(bf16[96,128]{1,0:T(8,128)(2,1)} %param.22) | copy-start | bytes 73732
  7.2 7.8 %copy-start.36 = (bf16[96,128]{1,0:T(8,128)(2,1)S(1)}, bf16[96,128]{1,0:T(8,128)(2,1)}, u32[]{:S(2)}) copy-start(bf16[96,128]{1,0:T(8,128)(2,1)} %param.20) | copy-start | bytes 73732
  7.2 7.8 %copy-start.28 = (bf16[96,768]{1,0:T(8,128)(2,1)S(1)}, bf16[96,768]{1,0:T(8,128)(2,1)}, u32[]{:S(2)}) copy-start(bf16[96,768]{1,0:T(8,128)(2,1)} %param.18) | copy-start | bytes 442372
  7.2 172.7 %all-gather.4.cloned.1.call-start = ((), (), s32[]{:S(2)}) async-start(), calls=%async_computation.4 | async-start | bytes 1769472 | tf_op jit(solution)/shard_map/all_gather | solution.py:496
  8.8 4.1 copy-start.40
  8.8 152.6 %copy-start.37 = (f32[192]{0:T(256)}, f32[192]{0:T(256)S(1)}, u32[]{:S(2)}) copy-start(f32[192]{0:T(256)S(1)} %fusion.62) | copy-start | bytes 2308
  15.0 146.4 %copy-start = (f32[192,1536]{1,0:T(8,128)S(1)}, f32[192,1536]{1,0:T(8,128)}, u32[]{:S(2)}) copy-start(f32[192,1536]{1,0:T(8,128)} %param.15) | copy-start | bytes 3538948
  15.8 147.7 %copy-start.42 = (s32[1,3]{1,0:T(1,128)S(1)}, s32[1,3]{1,0:T(1,128)}, u32[]{:S(2)}) copy-start(s32[1,3]{1,0:T(1,128)} %param.16) | copy-start | bytes 40
  162.5 55.9 %reduce-scatter.5.cloned.1.call-start = ((), (), s32[]{:S(2)}) async-start(), calls=%async_computation.5 | async-start | bytes 1769472 | tf_op jit(solution)/shard_map/reduce_scatter | solution.py:500
  181.8 0.7 copy-start.15
  186.3 2.8 copy-start.9
  186.7 4.6 copy-start.8
  189.1 0.7 copy-start.13
  191.2 0.9 copy-start.21
  192.1 1.9 copy-start.10
  192.2 4.4 copy-start.7
  199.7 3.7 copy-start.1
  199.7 3.7 copy-start.29
  199.8 2.2 copy-start.17
  199.8 2.2 copy-start.43
  201.9 2.3 copy-start.31
  203.4 0.8 copy-start.30
  204.3 4.1 copy-start.49
  204.3 4.2 copy-start.33
  208.4 67.6 %all-gather.6.cloned.1.call-start = ((), (), s32[]{:S(2)}) async-start(), calls=%async_computation.6 | async-start | bytes 5308416 | tf_op jit(solution)/shard_map/all_gather | solution.py:496
  219.7 0.6 copy-start.39
  220.2 0.6 copy-start.34
  222.9 159.4 %reduce-scatter.9.cloned.1.call-start = ((), (), s32[]{:S(2)}) async-start(), calls=%async_computation.8 | async-start | bytes 5308416 | tf_op jit(solution)/shard_map/reduce_scatter | solution.py:500
  276.0 11.1 %copy-start.44 = (bf16[1536,1536]{1,0:T(8,128)(2,1)S(1)}, bf16[1536,1536]{1,0:T(8,128)(2,1)}, u32[]{:S(2)}) copy-start(bf16[1536,1536]{1,0:T(8,128)(2,1)} %all-gather.6.cloned.1.call-done) | copy-start | bytes 14155780
  276.0 11.1 %copy-start.47 = (bf16[16,96,1152]{2,1,0:T(8,128)(2,1)S(1)}, bf16[16,96,1152]{2,1,0:T(8,128)(2,1)}, u32[]{:S(2)}) copy-start(bf16[16,96,1152]{2,1,0:T(8,128)(2,1)} %get-tuple-element.27) | copy-start | bytes 10616836
  276.0 19.4 %slice-start = ((s8[4718592]{0:T(1024)(128)(4,1)}), s8[4194304]{0:T(1024)(128)(4,1)S(1)}, s32[]{:S(2)}) async-start(s8[4718592]{0:T(1024)(128)(4,1)} %bitcast.169), calls=%async_computation.11 | async-start | bytes 8388608
  287.1 8.2 %slice-start.1 = ((s8[4718592]{0:T(1024)(128)(4,1)}), s8[524288]{0:T(1024)(128)(4,1)S(1)}, s32[]{:S(2)}) async-start(s8[4718592]{0:T(1024)(128)(4,1)} %bitcast.169), calls=%async_computation.12 | async-start | bytes 1048576
  287.1 8.2 %copy-start.45 = (bf16[16,96,1152]{2,1,0:T(8,128)(2,1)S(1)}, bf16[16,96,1152]{2,1,0:T(8,128)(2,1)}, u32[]{:S(2)}) copy-start(bf16[16,96,1152]{2,1,0:T(8,128)(2,1)} %get-tuple-element.29) | copy-start | bytes 10616836
  295.4 13.4 %copy-start.48 = (bf16[16,96,1152]{2,1,0:T(8,128)(2,1)S(1)}, bf16[16,96,1152]{2,1,0:T(8,128)(2,1)}, u32[]{:S(2)}) copy-start(bf16[16,96,1152]{2,1,0:T(8,128)(2,1)} %get-tuple-element.27) | copy-start | bytes 10616836
  308.7 9.0 %copy-start.50 = (bf16[1536,1152]{1,0:T(8,128)(2,1)}, bf16[1536,1152]{1,0:T(8,128)(2,1)S(1)}, u32[]{:S(2)}) copy-start(bf16[1536,1152]{1,0:T(8,128)(2,1)S(1)} %get-tuple-element.43) | copy-start | bytes 10616836
  308.7 9.0 %copy-start.46 = (bf16[16,96,1152]{2,1,0:T(8,128)(2,1)S(1)}, bf16[16,96,1152]{2,1,0:T(8,128)(2,1)}, u32[]{:S(2)}) copy-start(bf16[16,96,1152]{2,1,0:T(8,128)(2,1)} %get-tuple-element.28) | copy-start | bytes 10616836
  308.7 9.0 %copy-start.52 = (bf16[1536,1152]{1,0:T(8,128)(2,1)S(1)}, bf16[1536,1152]{1,0:T(8,128)(2,1)}, u32[]{:S(2)}) copy-start(bf16[1536,1152]{1,0:T(8,128)(2,1)} %get-tuple-element.42) | copy-start | bytes 10616836
  328.4 53.9 %copy-start.3 = (bf16[192,1536]{1,0:T(8,128)(2,1)S(1)}, bf16[192,1536]{1,0:T(8,128)(2,1)}, u32[]{:S(2)}) copy-start(bf16[192,1536]{1,0:T(8,128)(2,1)} %reduce-scatter.5.cloned.1.call-done) | copy-start | bytes 1769476
  328.4 57.4 %copy-start.4 = (f32[192,1536]{1,0:T(8,128)S(1)}, f32[192,1536]{1,0:T(8,128)}, u32[]{:S(2)}) copy-start(f32[192,1536]{1,0:T(8,128)} %param.29) | copy-start | bytes 3538948
  328.4 67.0 %all-gather.8.cloned.1.call-start = ((), (), s32[]{:S(2)}) async-start(), calls=%async_computation.9 | async-start | bytes 1769472 | tf_op jit(solution)/shard_map/all_gather | solution.py:496
  382.3 3.5 copy-start.5
  385.2 0.6 copy-start.38
  387.7 95.8 %reduce-scatter.11.cloned.1.call-start = ((), (), s32[]{:S(2)}) async-start(), calls=%async_computation.10 | async-start | bytes 1769472 | tf_op jit(solution)/shard_map/reduce_scatter | solution.py:500
  401.5 3.6 copy-start.2
  401.5 3.6 copy-start.6
  401.5 3.6 copy-start.32
  423.1 1.5 copy-start.20
  423.1 1.5 copy-start.22
  423.1 1.6 copy-start.19
  423.1 1.6 copy-start.14
  423.1 1.9 copy-start.16
  424.7 1.4 copy-start.25
  424.8 0.6 copy-start.23
  425.2 0.8 copy-start.11
  430.4 219.0 %reduce-scatter.7.cloned.1.call-start = ((), (), s32[]{:S(2)}) async-start(), calls=%async_computation.7 | async-start | bytes 5308416 | tf_op jit(solution)/shard_map/reduce_scatter | solution.py:500
  441.3 10.7 %copy-start.53 = (bf16[1536,1152]{1,0:T(8,128)(2,1)S(1)}, bf16[1536,1152]{1,0:T(8,128)(2,1)}, u32[]{:S(2)}) copy-start(bf16[1536,1152]{1,0:T(8,128)(2,1)} %get-tuple-element.42) | copy-start | bytes 10616836
  452.0 9.6 %copy-start.51 = (bf16[1536,1152]{1,0:T(8,128)(2,1)S(1)}, bf16[1536,1152]{1,0:T(8,128)(2,1)}, u32[]{:S(2)}) copy-start(bf16[1536,1152]{1,0:T(8,128)(2,1)} %copy-done.50) | copy-start | bytes 10616836
  475.7 3.0 copy-start.12
  475.7 3.0 copy-start.18
  475.7 3.0 copy-start.24
  475.7 3.0 copy-start.26
  642.1 0.8 copy-start.41
Sparse Core Ops, SparseCore 0:
  162.6 17.3 all-gather.3
  208.5 9.8 reduce-scatter.4
  223.0 52.9 all-gather.5
  328.5 53.7 reduce-scatter.8
  387.8 7.5 all-gather.7
  430.6 9.8 reduce-scatter.10
  442.7 56.1 reduce-scatter.6

commit v3 on v2

--- a/solution.py
+++ b/solution.py
@@ -119,6 +119,10 @@
             index = index + bit - 2 * bit * lax.rem(lax.div(index, bit), 2)
         bit *= 2
     return index
+
+
+def spot(z, p, c):
+    return {"z": z, "p": p, "head": c}
 
 
 def here():
@@ -162,7 +166,7 @@
     hidden = gate.shape[1]
 
     def at(zz, pp):
-        return (zz, pp, c)
+        return spot(zz, pp, c)
 
     def send(src, dst, ssem, rsem, peer):
         copy = pltpu.make_async_remote_copy(
@@ -172,7 +176,7 @@
         copy.start()
         return copy
 
-    pair = (z, p, 1 - c)
+    pair = spot(z, p, 1 - c)
     masks = [(kz, kp) for kz in range(quarters) for kp in range(PLANE) if kz or kp]
     greet([at(flipped(z, kz), flipped(p, kp)) for kz, kp in masks] + [pair])
 
@@ -318,6 +322,240 @@
         compiler_params=pltpu.CompilerParams(collective_id=0, has_side_effects=True),
     )(aset, small, gate, up, down, grad)
 
+
+TILE = 256
+
+
+def mlp_kernel(
+    quarters,
+    hidden,
+    own,
+    grads,
+    gate,
+    up,
+    down,
+    y_out,
+    d_out,
+    gate_out,
+    up_out,
+    down_out,
+    h_all,
+    g_all,
+    w_all,
+    act,
+    d_gate,
+    d_up,
+    y_part,
+    d_part,
+    y_slot,
+    d_slot,
+    d_line,
+    h_send,
+    h_recv,
+    hp_send,
+    hp_recv,
+    y_send,
+    y_recv,
+    d_send,
+    d_recv,
+    l_send,
+    l_recv,
+    load_sem,
+    out_sem,
+):
+    z, p, c = here()
+    pair = spot(z, p, 1 - c)
+    rows, width = own.shape
+    part_cols = gate.shape[1]
+    padded = w_all.shape[2]
+    tiles = padded // TILE
+
+    def moved(k):
+        total, bit = 0, 1
+        while bit < quarters:
+            a, b = lax.rem(lax.div(z, bit), 2), lax.rem(lax.div(k, bit), 2)
+            total = total + bit * (a + b - 2 * a * b)
+            bit *= 2
+        return total
+
+    def send(src, dst, ssem, rsem, peer):
+        pltpu.make_async_remote_copy(
+            src_ref=src, dst_ref=dst, send_sem=ssem, recv_sem=rsem,
+            device_id=peer, device_id_type=MESH_ID,
+        ).start()
+
+    def landed(ref, sem):
+        pltpu.make_async_copy(ref, ref, sem).wait()
+
+    def half(k, lane):
+        return h_all.at[k, pl.ds(pl.multiple_of(lane * rows, 16), rows)]
+
+    loads = [
+        pltpu.make_async_copy(w, w_all.at[i, :, pl.ds(0, part_cols)], load_sem.at[i])
+        for i, w in enumerate((gate, up, down))
+    ] + [pltpu.make_async_copy(grads, g_all, load_sem.at[3]), pltpu.make_async_copy(own, half(0, c), load_sem.at[4])]
+    for copy in loads:
+        copy.start()
+    greet([spot(flipped(z, k), p, c) for k in range(1, quarters)] + [pair])
+    send(own, half(0, c), hp_send.at[0], hp_recv.at[0], pair)
+    for k in range(1, quarters):
+        send(own, half(k, c), h_send.at[k], h_recv.at[k], spot(flipped(z, k), p, c))
+    if padded > part_cols:
+        for i in range(3):
+            w_all[i, :, part_cols:] = jnp.zeros((width, padded - part_cols), w_all.dtype)
+    first = jnp.minimum(z * part_cols, hidden - part_cols)
+    skip = z * part_cols - first
+    for copy in loads:
+        copy.wait()
+
+    def finish(k):
+        mine, other = (y_part.at[k, c], y_slot.at[k])
+        landed(other, y_recv.at[k])
+        other[...] = (other[...].astype(jnp.float32) + mine[...].astype(jnp.float32)).astype(other.dtype)
+        pltpu.make_async_copy(other, y_out.at[k], out_sem.at[0, k]).start()
+        mine, other = (d_part.at[k, c], d_slot.at[k])
+        landed(other, d_recv.at[k])
+        other[...] = (other[...].astype(jnp.float32) + mine[...].astype(jnp.float32)).astype(other.dtype)
+
+        @pl.when(k > 0)
+        def _():
+            send(other, d_line.at[k], l_send.at[k], l_recv.at[k], spot(moved(k), p, c))
+
+    def block(k, carry):
+        @pl.when(k > 0)
+        def _():
+            landed(half(k, c), h_recv.at[k])
+            send(half(k, c), half(k, c), hp_send.at[k], hp_recv.at[k], pair)
+
+        landed(half(k, 1 - c), hp_recv.at[k])
+
+        def units(n, carry):
+            cols = pl.ds(pl.multiple_of(n * TILE, TILE), TILE)
+            h = h_all[k]
+            g = jnp.dot(h, w_all[0, :, cols], preferred_element_type=jnp.float32)
+            u = jnp.dot(h, w_all[1, :, cols], preferred_element_type=jnp.float32)
+            da = jnp.dot(g_all[k], w_all[2, :, cols], preferred_element_type=jnp.float32)
+            column = n * TILE + lax.broadcasted_iota(jnp.int32, (1, TILE), 1)
+            ok = column >= skip
+            g = jnp.where(ok, g, 0.0)
+            u = jnp.where(ok, u, 0.0)
+            s = 1.0 / (1.0 + jnp.exp(-g))
+            sg = g * s
+            act[k, :, cols] = (sg * u).astype(act.dtype)
+            d_gate[k, :, cols] = (da * u * s * (1.0 + g * (1.0 - s))).astype(act.dtype)
+            d_up[k, :, cols] = (da * sg).astype(act.dtype)
+            return carry
+
+        lax.fori_loop(0, tiles, units, 0)
+
+        @pl.when(k > 0)
+        def _():
+            finish(k - 1)
+
+        def model(n, carry):
+            cols = pl.ds(pl.multiple_of(n * TILE, TILE), TILE)
+
+            def back(left, index):
+                return lax.dot_general(
+                    left[k], w_all[index, cols, :], (((1,), (1,)), ((), ())),
+                    preferred_element_type=jnp.float32,
+                )
+
+            y = back(act, 2).astype(act.dtype)
+            d = (back(d_gate, 0) + back(d_up, 1)).astype(act.dtype)
+            for lane in range(2):
+                y_part[k, lane, :, cols] = y[lane * rows : (lane + 1) * rows]
+                d_part[k, lane, :, cols] = d[lane * rows : (lane + 1) * rows]
+            return carry
+
+        lax.fori_loop(0, width // TILE, model, 0)
+        send(y_part.at[k, 1 - c], y_slot.at[k], y_send.at[k], y_recv.at[k], pair)
+        send(d_part.at[k, 1 - c], d_slot.at[k], d_send.at[k], d_recv.at[k], pair)
+        return carry
+
+    lax.fori_loop(0, quarters, block, 0)
+    finish(quarters - 1)
+
+    outs = (gate_out, up_out, down_out)
+
+    def weight(n, carry):
+        cols = pl.ds(pl.multiple_of(n * TILE, TILE), TILE)
+        for i, (left, right) in enumerate(((h_all, d_gate), (h_all, d_up), (g_all, act))):
+            total = None
+            for k in range(quarters):
+                term = lax.dot_general(
+                    left[k, :, cols], right[k], (((0,), (0,)), ((), ())),
+                    preferred_element_type=jnp.float32,
+                )
+                total = term if total is None else total + term
+            w_all[i, cols, :] = total.astype(act.dtype)
+            pltpu.make_async_copy(
+                w_all.at[i, cols, pl.ds(0, part_cols)], outs[i].at[cols, :], out_sem.at[1 + i, n]
+            ).start()
+        return carry
+
+    lax.fori_loop(0, width // TILE, weight, 0)
+    total = d_slot[0].astype(jnp.float32)
+    for k in range(1, quarters):
+        landed(d_line.at[k], l_recv.at[k])
+        total = total + d_line[k].astype(jnp.float32)
+    d_out[...] = total
+    for n in range(width // TILE):
+        for i in range(3):
+            tile = w_all.at[i, pl.ds(n * TILE, TILE), pl.ds(0, part_cols)]
+            pltpu.make_async_copy(tile, outs[i].at[pl.ds(n * TILE, TILE), :], out_sem.at[1 + i, n]).wait()
+    for k in range(quarters):
+        pltpu.make_async_copy(y_slot.at[k], y_out.at[k], out_sem.at[0, k]).wait()
+        landed(half(k, c), hp_send.at[k])
+        landed(y_part.at[k, 1 - c], y_send.at[k])
+        landed(d_part.at[k, 1 - c], d_send.at[k])
+        if k:
+            landed(own, h_send.at[k])
+            landed(d_slot.at[k], l_send.at[k])
+
+
+def mlp_all(own, grads, gate, up, down, hidden):
+    bf = jnp.bfloat16
+    quarters, block_rows, width = grads.shape
+    part_cols = gate.shape[1]
+    padded = -(-part_cols // TILE) * TILE
+    rows = own.shape[0]
+    dma = pltpu.SemaphoreType.DMA
+    hbm = pl.BlockSpec(memory_space=pl.ANY)
+    vmem = pl.BlockSpec(memory_space=pltpu.VMEM)
+    grad_w = jax.ShapeDtypeStruct((width, part_cols), bf)
+    steps = max(quarters, width // TILE)
+    return pl.pallas_call(
+        functools.partial(mlp_kernel, quarters, hidden),
+        out_shape=(
+            jax.ShapeDtypeStruct((quarters, rows, width), bf),
+            jax.ShapeDtypeStruct((rows, width), jnp.float32),
+            grad_w,
+            grad_w,
+            grad_w,
+        ),
+        in_specs=[hbm] * 5,
+        out_specs=[hbm, vmem, hbm, hbm, hbm],
+        scratch_shapes=[
+            pltpu.VMEM((quarters, block_rows, width), bf),
+            pltpu.VMEM((quarters, block_rows, width), bf),
+            pltpu.VMEM((3, width, padded), bf),
+            pltpu.VMEM((quarters, block_rows, padded), bf),
+            pltpu.VMEM((quarters, block_rows, padded), bf),
+            pltpu.VMEM((quarters, block_rows, padded), bf),
+            pltpu.VMEM((quarters, 2, rows, width), bf),
+            pltpu.VMEM((quarters, 2, rows, width), bf),
+            pltpu.VMEM((quarters, rows, width), bf),
+            pltpu.VMEM((quarters, rows, width), bf),
+            pltpu.VMEM((quarters, rows, width), bf),
+        ]
+        + [dma((quarters,))] * 10
+        + [dma((5,)), dma((4, steps))],
+        compiler_params=pltpu.CompilerParams(
+            collective_id=2, has_side_effects=True, vmem_limit_bytes=60 * 2**20
+        ),
+    )(own, grads, gate, up, down)
+
 AHEAD = 1
 LAG = 1
 PARTS = (1, 2, 3, 0)
@@ -328,8 +566,10 @@
     gate,
     up,
     down,
+    y_half,
     small_sum,
     attn_sum,
+    y_sum,
     gate_out,
     up_out,
     down_out,
@@ -337,6 +577,7 @@
     attn_slots,
     mlp_slots,
     attn_line,
+    y_line,
     staged,
     t_send,
     t_recv,
@@ -344,12 +585,14 @@
     z_recv,
     s_send,
     s_recv,
+    y_send,
+    y_recv,
     l_sem,
 ):
     z, p, c = here()
-    pair = (z, p, 1 - c)
+    pair = spot(z, p, 1 - c)
     masks = [(kz, kp) for kz in range(quarters) for kp in range(PLANE) if kz or kp]
-    greet([(flipped(z, kz), flipped(p, kp), c) for kz, kp in masks] + [pair])
+    greet([spot(flipped(z, kz), flipped(p, kp), c) for kz, kp in masks] + [pair])
     sent = []
 
     def send(src, dst, ssem, rsem, peer):
@@ -363,7 +606,7 @@
     def landed(ref, sem):
         pltpu.make_async_copy(ref, ref, sem).wait()
 
-    side = [(z, flipped(p, 1), c), (z, flipped(p, 2), c)]
+    side = [spot(z, flipped(p, 1), c), spot(z, flipped(p, 2), c)]
     sources = (attn, gate, up, down)
     outs = (None, gate_out, up_out, down_out)
 
@@ -403,9 +646,9 @@
         one[...] = total.astype(one.dtype)
         if s == 0:
             if k:
-                send(one, attn_line.at[k], z_send.at[s, k], z_recv.at[s, k], (flipped(z, k), p, c))
+                send(one, attn_line.at[k], z_send.at[s, k], z_recv.at[s, k], spot(flipped(z, k), p, c))
         elif k:
-            send(one, outs[s].at[z], z_send.at[s, k], z_recv.at[s, k], (flipped(z, k), p, c))
+            send(one, outs[s].at[z], z_send.at[s, k], z_recv.at[s, k], spot(flipped(z, k), p, c))
         else:
             copy = pltpu.make_async_copy(one, outs[s].at[z], l_sem.at[s])
             copy.start()
@@ -413,7 +656,9 @@
 
     dp = z * PLANE + p
     for n, (kz, kp) in enumerate(masks):
-        send(small, small_all.at[dp], s_send.at[n], s_recv.at[n], (flipped(z, kz), flipped(p, kp), c))
+        send(small, small_all.at[dp], s_send.at[n], s_recv.at[n], spot(flipped(z, kz), flipped(p, kp), c))
+    for k in range(1, quarters):
+        send(y_half.at[k], y_line.at[k], y_send.at[k], y_recv.at[k], spot(flipped(z, k), p, c))
     ks = list(range(1, quarters)) + [0]
     order = [(s, k) for i in range(0, quarters, 2) for s in PARTS for k in ks[i : i + 2]]
     for i in range(-AHEAD, len(order) + LAG):
@@ -440,6 +685,11 @@
     for k in range(1, quarters):
         total = total + attn_line[k].astype(jnp.float32)
     attn_sum[...] = total
+    total = y_half[0].astype(jnp.float32)
+    for k in range(1, quarters):
+        landed(y_line.at[k], y_recv.at[k])
+        total = total + y_line[k].astype(jnp.float32)
+    y_sum[...] = total
     for s in (1, 2, 3):
         for k in range(1, quarters):
             landed(outs[s].at[flipped(z, k)], z_recv.at[s, k])
@@ -449,7 +699,7 @@
         copy.wait_send()
 
 
-def reduce_all(small, attn, gate, up, down, shards):
+def reduce_all(small, attn, gate, up, down, y_half, shards):
     quarters = shards // PLANE
     bf = jnp.bfloat16
     dma = pltpu.SemaphoreType.DMA
@@ -462,17 +712,19 @@
         out_shape=(
             jax.ShapeDtypeStruct((2,) + small.shape, jnp.float32),
             jax.ShapeDtypeStruct(attn.shape[1:], jnp.float32),
+            jax.ShapeDtypeStruct(y_half.shape[1:], jnp.float32),
             quarter_out,
             quarter_out,
             quarter_out,
         ),
-        in_specs=[vmem] * 5,
-        out_specs=[vmem, vmem, hbm, hbm, hbm],
+        in_specs=[vmem] * 6,
+        out_specs=[vmem, vmem, vmem, hbm, hbm, hbm],
         scratch_shapes=[
             pltpu.VMEM((shards,) + small.shape, jnp.float32),
             pltpu.VMEM((quarters, 3) + attn.shape[1:], bf),
             pltpu.VMEM((3, quarters, 3, depth, part_cols), bf),
             pltpu.VMEM((quarters,) + attn.shape[1:], bf),
+            pltpu.VMEM(y_half.shape, bf),
             pltpu.VMEM(small.shape, jnp.float32),
             dma((4, quarters, 3)),
             dma((4, quarters, 3)),
@@ -480,16 +732,21 @@
             dma((4, quarters)),
             dma((shards,)),
             dma((shards,)),
+            dma((quarters,)),
+            dma((quarters,)),
             dma((4,)),
         ],
         compiler_params=pltpu.CompilerParams(
             collective_id=1, has_side_effects=True, vmem_limit_bytes=50 * 2**20
         ),
-    )(small, attn, gate, up, down)
-
-
-DP = ("z", "p")
-POOL = ("z", "head")
+    )(small, attn, gate, up, down, y_half)
+
+
+DP = ("z", "p", "o")
+
+
+def copies_of(shards):
+    return max(1, shards // (PLANE * PLANE))
 
 
 def gather(x, axes):
@@ -522,6 +779,16 @@
     lanes = lax.axis_size("head")
     lane_index = lax.axis_index("head")
     shards = quarters * PLANE
+    copies = lax.axis_size("o")
+    if copies > 1:
+        norm_attn, norm_mlp, w_query, w_key, w_value, w_gate, w_up = [
+            lax.all_gather(x, "o", axis=0, tiled=True)
+            for x in (norm_attn, norm_mlp, w_query, w_key, w_value, w_gate, w_up)
+        ]
+        b_query, b_key, b_value, w_out, w_down = [
+            lax.all_gather(x, "o", axis=1, tiled=True)
+            for x in (b_query, b_key, b_value, w_out, w_down)
+        ]
     local_rows = hidden_in.shape[0]
     token_count = local_rows * lanes
     depth = norm_attn.shape[0]
@@ -531,9 +798,6 @@
     group_heads = query_width // head_dim
     hidden_width = w_gate.shape[1]
     part_width = -(-hidden_width // (128 * quarters)) * 128
-    quarter = lax.axis_index("z")
-    first_unit = jnp.minimum(quarter * part_width, hidden_width - part_width)
-    valid = first_unit + jnp.arange(part_width, dtype=jnp.int32) >= quarter * part_width
     segment, positions = layout(row_lengths[0], token_count)
     cosine, sine_tab = rotary_tables(positions, head_dim)
     cosine = cosine[:, None, :]
@@ -558,8 +822,7 @@
     attn_set = attn_set.reshape(width, attn_set.shape[2])
     small = small.reshape(shards, rows_used * 128)
     wg, wu, wd_rows = [w.reshape(width, part_width) for w in (wg, wu, wd_rows)]
-    grad_rows = grad_rows[lax.bitwise_xor(jnp.arange(quarters, dtype=jnp.int32), quarter)]
-    grad_rows = grad_rows.reshape(quarters * token_count, width)
+    grad_rows = grad_rows.reshape(quarters, token_count, width)
     wq_full = attn_set[:, :query_width]
     wk_full = attn_set[:, query_width : query_width + head_dim]
     wv_full = attn_set[:, query_width + head_dim : query_width + 2 * head_dim]
@@ -583,31 +846,10 @@
     residual = hidden_in + scatter_sum(contract_last(heads_low, wo_rows), "head").astype(
         jnp.float32
     )
-    mlp_low = gather(rms_norm(residual, gain_mlp).astype(bf), POOL)
-    gate_pre = jnp.where(valid, product(mlp_low, wg), 0.0)
-    up_pre = jnp.where(valid, product(mlp_low, wu), 0.0)
-    sigmoid_gate = jax.nn.sigmoid(gate_pre)
-    silu_gate = gate_pre * sigmoid_gate
-    hidden_low = (silu_gate * up_pre).astype(bf)
-    block_out = residual + scatter_sum(contract_last(hidden_low, wd_rows), POOL).astype(
-        jnp.float32
-    )
-    grad_hidden = product(grad_rows, wd_rows)
-    grad_gate = (
-        grad_hidden * up_pre * sigmoid_gate * (1.0 + gate_pre * (1.0 - sigmoid_gate))
-    ).astype(bf)
-    grad_up = (grad_hidden * silu_gate).astype(bf)
-    grad_normed_mlp = scatter_sum(
-        contract_last(grad_gate, wg) + contract_last(grad_up, wu), POOL
-    ).astype(jnp.float32)
-    mlp_terms = [
-        contract_first(left, right).astype(bf).reshape(shards, depth, part_width)
-        for left, right in (
-            (mlp_low, grad_gate),
-            (mlp_low, grad_up),
-            (grad_rows, hidden_low),
-        )
-    ]
+    y_half, grad_normed_mlp, *mlp_grads = mlp_all(
+        rms_norm(residual, gain_mlp).astype(bf), grad_rows, wg, wu, wd_rows, hidden_width
+    )
+    mlp_terms = [g.reshape(shards, depth, part_width) for g in mlp_grads]
 
     _, mlp_pull = jax.vjp(rms_norm, residual, gain_mlp)
     grad_residual_part, grad_gain_mlp = mlp_pull(grad_normed_mlp)
@@ -639,16 +881,13 @@
     )
     bias_vec = jnp.sum(grad_qkv.astype(jnp.float32), 0)
     small_grads = jnp.concatenate([grad_gain_attn, grad_gain_mlp, bias_vec]).reshape(-1, 128)
-    small_total, attn_part, *quarter_grads = reduce_all(
+    small_total, attn_part, y_sum, *quarter_grads = reduce_all(
         small_grads,
         attn_terms.astype(bf).reshape(shards, depth, attn_terms.shape[1]),
         *mlp_terms,
+        y_half,
         shards,
     )
-    small_total = small_total.reshape(lanes, -1)
-    gain_total = jnp.sum(small_total[:, : 2 * width], 0).reshape(2, width)
-    bias_total = small_total[:, 2 * width :]
-
     def whole_rows(parts):
         taken = []
         for index in range(quarters):
@@ -658,7 +897,17 @@
         return jnp.concatenate(taken, 1).astype(jnp.float32)
 
     grad_w_gate, grad_w_up, grad_w_down = [whole_rows(parts) for parts in quarter_grads]
+    if copies > 1:
+        small_total = lax.psum(small_total, "o")
+        attn_part, grad_w_gate, grad_w_up, grad_w_down = [
+            lax.psum_scatter(x, "o", scatter_dimension=0, tiled=True)
+            for x in (attn_part, grad_w_gate, grad_w_up, grad_w_down)
+        ]
     grad_w_down = grad_w_down.T
+    small_total = small_total.reshape(lanes, -1)
+    block_out = residual + y_sum
+    gain_total = jnp.sum(small_total[:, : 2 * width], 0).reshape(2, width)
+    bias_total = small_total[:, 2 * width :]
     return (
         block_out,
         grad_in,
@@ -679,29 +928,13 @@
 
 def solution(mesh):
     shards = mesh.shape["dp"]
-    plane = 4 if shards % 4 == 0 else 1
-    split = jax.sharding.Mesh(
-        mesh.devices.reshape(shards // plane, plane, mesh.shape["head"]), ("z", "p", "head")
-    )
-    rows = P(("z", "p", "head"), None)
+    shape = (shards // (PLANE * copies_of(shards)), PLANE, copies_of(shards), mesh.shape["head"])
+    split = jax.sharding.Mesh(mesh.devices.reshape(shape), DP + ("head",))
+    rows = P(DP + ("head",), None)
     deep = P(DP, "head")
     wide = P("head", DP)
     placed = (
-        rows,
-        P(DP, None),
-        P(DP),
-        deep,
-        wide,
-        deep,
-        wide,
-        deep,
-        wide,
-        wide,
-        P(DP),
-        deep,
-        deep,
-        wide,
-        rows,
+        rows, P(DP, None), P(DP), deep, wide, deep, wide, deep, wide, wide, P(DP), deep, deep, wide, rows
     )
     return jax.shard_map(
         local,

time: 673 us -> 573 us (0.85); the launches traced: 660 us -> 568 us
  Pallas kernels: 300 us -> 407 us
  matrix products: 141 us -> 42.5 us
  waiting for transfers between devices: 132 us -> 43.3 us
  other arithmetic: 40.9 us -> 33.7 us
    pallas_call x0 -> x1, Pallas kernels: none -> 105 us  [mlp_all(): pl.pallas_call(functools.partial(mlp_kernel, quarters, hidden), out_shape...]
    reduce_scatter x4 -> x2, waiting for transfers between devices: 63.7 us -> 9.35 us  [scatter_sum(): lax.psum_scatter(x.astype(jnp.bfloat16), axes, scatter_dimension=0, tiled...]
    all_gather x3 -> x2, waiting for transfers between devices: 67.8 us -> 33.9 us  [gather(): return lax.all_gather(x, axes, axis=0, tiled=True)]
    dot_general x7 -> x4, matrix products: 43 us -> 10.1 us  [product(): return jnp.dot(left_side, right_side, preferred_element_type=jnp.float32)]
    dot_general x5 -> x2, matrix products: 38.8 us -> 8.18 us  [contract_last(): lax.dot_general(left_side, right_side, (((1,), (1,)), ((), ())), preferre...]
    dot_general x5 -> x2, matrix products: 34.8 us -> 4.44 us  [contract_first(): lax.dot_general(left_side, right_side, (((0,), (0,)), ((), ())), preferre...]
  transfers between devices with their start and end apart: 7 -> 4, of which waited for: 5 -> 4; matrix products, arithmetic and copies ran while one was open for 11% -> 2% of each run, Pallas kernels for 24% -> 0%
where the time goes in v3:
time: 573 us; the launch traced here: 568 us
  Pallas kernels  407 us (71%)
  waiting for transfers between devices  43.3 us (8%)
  matrix products  42.5 us (7%)
  other arithmetic  33.7 us (6%)
  local copies, waits for them, and re-layouts  26.2 us (5%)
  between operations  14.4 us (3%)
    pallas_call x1, Pallas kernels, reduce_all(): pl.pallas_call(functools.partial(reduce_kernel, quarters), out_shape=(jax...  158 us
    pallas_call x1, Pallas kernels, gather_all(): pl.pallas_call(functools.partial(gather_kernel, quarters, part_cols), out...  144 us
    pallas_call x1, Pallas kernels, mlp_all(): pl.pallas_call(functools.partial(mlp_kernel, quarters, hidden), out_shape...  105 us
    all_gather x2, waiting for transfers between devices, gather(): return lax.all_gather(x, axes, axis=0, tiled=True)  33.9 us
  transfers between devices with their start and end apart: 4, of which 4 were waited for; matrix products, arithmetic and copies ran while one was open for 2% of the time, Pallas kernels for 0%

profile of v3, /device:TPU:0, one launch (start us, length us, event | category | flops | bytes accessed | tf_op | source)
XLA Modules:
  0.0 567.7 jit_solution(13353418352517900524)
XLA Ops:
  7.3 1.5 multiply_reduce_fusion.3
  8.8 0.6 copy-done.38
  9.4 3.4 concatenate.57
  12.8 0.6 pad_bitcast_fusion.small
  13.4 0.9 convert_element_type.149.grad
  14.3 0.8 pad_maximum_fusion.2.aset
  15.1 144.0 %shard_map.254 = (bf16[16,96,1792]{2,1,0:T(8,128)(2,1)}, bf16[16,16,128]{2,1,0:T(8,128)(2,1)}, bf16[16,96,1152]{2,1,0:T(8,128)(2,1)}, bf16[16,96,1152]{2,1,0:T(8...) custom-call(bf16[96,1792]{1,0:T(8,128)(2,1)} %pad_maximum_fusion.2.aset, ...), custom_call_target="tpu_custom_call" | custom-call | tf_op jit(solution)/shard_map/pallas_call | solution.py:299
  159.1 0.9 copy.91
  160.0 0.7 slice_convert_fusion
  160.7 1.0 multiply_convert_fusion.1
  162.5 0.8 fusion.48
  163.7 15.5 %all-gather.3.cloned.1.call-done = bf16[384,1536]{1,0:T(8,128)(2,1)} async-done(((bf16[192,1536]{1,0:T(8,128)(2,1)}), bf16[384,1536]{1,0:T(8,128)(2,1)}) %all-gather.3.cloned.1.call-update) | async-done | bytes 1179664 | tf_op jit(solution)/shard_map/all_gather | solution.py:753
  179.2 1.9 convolution_add_fusion
  181.2 2.7 fusion.26
  184.4 0.8 pad_maximum_fusion.3
  185.2 0.7 copy-done.13
  186.0 1.4 copy.60
  187.5 0.8 copy-done.24
  188.4 1.4 copy.62
  189.8 0.7 copy-done.11
  190.5 2.3 add_convert_fusion.1
  192.8 2.1 copy.63
  194.9 1.9 fusion.69
  197.3 0.8 copy-done.17
  198.1 1.5 fusion.46
  199.6 0.8 fusion.32
  200.4 0.8 copy-done.41
  201.2 3.8 convolution_convert_fusion.1
  205.3 0.8 reshape.292
  206.1 9.0 %reduce-scatter.3.cloned.1.call-done = bf16[192,1536]{1,0:T(8,128)(2,1)} async-done(((bf16[384,1536]{1,0:T(8,128)(2,1)}), bf16[192,1536]{1,0:T(8,128)(2,1)}) %reduce-scatter.3.cloned.1.call-update) | async-done | bytes 589840 | tf_op jit(solution)/shard_map/reduce_scatter | solution.py:757
  215.1 1.7 multiply_reduce_fusion.2
  216.8 1.0 copy-done.2
  217.8 1.0 multiply_convert_fusion.own
  218.7 105.2 %shard_map.255 = (bf16[4,192,1536]{2,1,0:T(8,128)(2,1)}, f32[192,1536]{1,0:T(8,128)}, bf16[1536,1152]{1,0:T(8,128)(2,1)}, bf16[1536,1152]{1,0:T(8,128)(2,1)}, bf16[1536,1152]{1,0:T(8,128)(2,1)}) custom-call(bf16[192,1536]{1,0:T(8,128)(2,1)} %multiply_convert_fusion.own, bf16[4,384,1536]{2,1,0:T(8,128)(2,1)} %bitcast.151, bf16[1536,1152]{1,0:T(8,128)(2,1)} %bitcast.152, ...), custom_call_target="tpu_custom_call" | custom-call | tf_op jit(solution)/shard_map/pallas_call | solution.py:528
  324.0 2.7 multiply_reduce_fusion
  326.7 2.8 fusion.63
  329.8 1.3 log_add_fusion
  331.1 18.4 %all-gather.5.cloned.1.call-done = bf16[384,1536]{1,0:T(8,128)(2,1)} async-done(((bf16[192,1536]{1,0:T(8,128)(2,1)}), bf16[384,1536]{1,0:T(8,128)(2,1)}) %all-gather.5.cloned.1.call-update) | async-done | bytes 1179664 | tf_op jit(solution)/shard_map/all_gather | solution.py:753
  349.5 3.9 fusion.29
  353.4 2.1 copy.68
  355.5 3.6 fusion.70
  359.1 1.4 fusion.42
  360.5 6.1 %fusion.38 = f32[384,128]{0,1:T(8,128)} fusion(f32[384,384,6]{1,0,2:T(8,128)} %fusion.70, f32[6,384,384]{1,2,0:T(8,128)S(1)} %get-tuple-element.96, f32[6,384]{1,0:T(8,128)} %log_add_fusion, f32[384,6,128]{0,2,1:T(8,128)} %copy-done.6, f32[384,6,128]{0,2,1:T(8,128)} %bitcast.149, f32[384,128]{0,1:T(8,128)} %copy-done.13), kind=kOutput, calls=%fused_computation.58 | convolution fusion | flops 233572992 | bytes 9839616 | tf_op jit(solution)/shard_map/hqk,qhd->kd/dot_general | solution.py:105
  366.6 6.1 %broadcast_multiply_fusion = (f32[384,6,128]{0,2,1:T(8,128)}, f32[384,6,128]{0,2,1:T(8,128)}) fusion(f32[384,128]{0,1:T(8,128)} %get-tuple-element.84, bf16[384,128,1]{0,1,2:T(8,128)(2,1)} %get-tuple-element.83, f32[384,384,6]{1,0,2:T(8,128)} %fusion.70, f32[6,384,384]{1,2,0:T(8,128)S(1)} %get-tuple-element.96, f32[6,384]{1,0:T(8,128)} %log_add_fusion), kind=kOutput, calls=%fused_computation.70 | convolution fusion | flops 232983168 | bytes 9741312 | tf_op jit(solution)/shard_map/hqk,kd->qhd/dot_general | solution.py:102
  372.7 1.5 fusion.65
  374.8 0.7 copy-done.26
  375.5 4.3 fusion.7
  379.9 1.2 copy-done.19
  381.1 0.7 copy.73
  382.1 2.6 convolution_convert_fusion.2
  384.7 1.9 convolution_convert_fusion
  386.6 2.9 pad_maximum_fusion.attn
  389.9 1.4 fusion.33
  391.3 157.7 %shard_map.256 = (f32[2,32,128]{2,1,0:T(8,128)S(1)}, f32[96,1792]{1,0:T(8,128)S(1)}, f32[192,1536]{1,0:T(8,128)}, bf16[4,96,1152]{2,1,0:T(8,128)(2,1)S(1)}, bf16...) custom-call(f32[32,128]{1,0:T(8,128)S(1)} %maximum_bitcast_fusion.small, ...), custom_call_target="tpu_custom_call" | custom-call | tf_op jit(solution)/shard_map/pallas_call | solution.py:710
  549.1 0.6 fusion.67
  549.7 0.6 slice.198
  550.3 0.6 fusion.66
  551.0 0.8 slice_bitcast_fusion
  551.8 2.4 add.105
  554.2 0.6 fusion.68
  555.1 1.3 maximum_convert_fusion
  556.4 1.3 maximum_convert_fusion.1
  557.8 1.3 convert_bitcast_fusion
  559.8 1.3 fusion.36
  (118 shorter events, 5.3 us)
Async XLA Ops:
  7.2 6.2 %copy-start.9 = (f32[192,1536]{1,0:T(8,128)S(1)}, f32[192,1536]{1,0:T(8,128)}, u32[]{:S(2)}) copy-start(f32[192,1536]{1,0:T(8,128)} %param.29) | copy-start | bytes 3538948
  7.2 7.1 %copy-start.27 = (bf16[768,96]{0,1:T(8,128)(2,1)S(1)}, bf16[768,96]{0,1:T(8,128)(2,1)}, u32[]{:S(2)}) copy-start(bf16[768,96]{0,1:T(8,128)(2,1)} %param.24) | copy-start | bytes 442372
  7.2 7.1 %copy-start.34 = (bf16[96,128]{1,0:T(8,128)(2,1)S(1)}, bf16[96,128]{1,0:T(8,128)(2,1)}, u32[]{:S(2)}) copy-start(bf16[96,128]{1,0:T(8,128)(2,1)} %param.22) | copy-start | bytes 73732
  7.2 7.1 %copy-start.35 = (bf16[96,128]{1,0:T(8,128)(2,1)S(1)}, bf16[96,128]{1,0:T(8,128)(2,1)}, u32[]{:S(2)}) copy-start(bf16[96,128]{1,0:T(8,128)(2,1)} %param.20) | copy-start | bytes 73732
  7.2 7.1 %copy-start.28 = (bf16[96,768]{1,0:T(8,128)(2,1)S(1)}, bf16[96,768]{1,0:T(8,128)(2,1)}, u32[]{:S(2)}) copy-start(bf16[96,768]{1,0:T(8,128)(2,1)} %param.18) | copy-start | bytes 442372
  7.2 172.0 %all-gather.3.cloned.1.call-start = ((), (), s32[]{:S(2)}) async-start(), calls=%async_computation.2 | async-start | bytes 1769472 | tf_op jit(solution)/shard_map/all_gather | solution.py:753
  8.8 0.6 copy-start.38
  9.4 151.4 %copy-start.36 = (f32[192]{0:T(256)}, f32[192]{0:T(256)S(1)}, u32[]{:S(2)}) copy-start(f32[192]{0:T(256)S(1)} %fusion.57) | copy-start | bytes 2308
  15.1 145.7 %copy-start = (f32[192,1536]{1,0:T(8,128)S(1)}, f32[192,1536]{1,0:T(8,128)}, u32[]{:S(2)}) copy-start(f32[192,1536]{1,0:T(8,128)} %param.15) | copy-start | bytes 3538948
  159.1 3.1 copy-start.40
  161.8 53.3 %reduce-scatter.3.cloned.1.call-start = ((), (), s32[]{:S(2)}) async-start(), calls=%async_computation.3 | async-start | bytes 1769472 | tf_op jit(solution)/shard_map/reduce_scatter | solution.py:757
  163.7 20.6 %copy-start.20 = (f32[384,64]{0,1:T(8,128)}, f32[384,64]{0,1:T(8,128)S(1)}, u32[]{:S(2)}) copy-start(f32[384,64]{0,1:T(8,128)S(1)} %get-tuple-element.93) | copy-start | bytes 294916
  163.7 20.6 %copy-start.22 = (f32[384,64]{0,1:T(8,128)}, f32[384,64]{0,1:T(8,128)S(1)}, u32[]{:S(2)}) copy-start(f32[384,64]{0,1:T(8,128)S(1)} %get-tuple-element.94) | copy-start | bytes 294916
  179.2 2.0 copy-start.16
  184.3 3.0 copy-start.8
  185.2 0.7 copy-start.13
  187.4 0.9 copy-start.24
  188.4 4.4 copy-start.6
  188.4 2.1 copy-start.11
  196.8 2.8 copy-start.29
  196.8 1.3 copy-start.17
  198.1 2.3 copy-start.31
  199.6 0.8 copy-start.30
  200.4 0.8 copy-start.41
  205.1 144.4 %all-gather.5.cloned.1.call-start = ((), (), s32[]{:S(2)}) async-start(), calls=%async_computation.4 | async-start | bytes 1769472 | tf_op jit(solution)/shard_map/all_gather | solution.py:753
  216.7 1.0 copy-start.2
  324.0 2.7 copy-start.3
  324.0 2.7 copy-start.10
  329.5 60.4 %reduce-scatter.5.cloned.1.call-start = ((), (), s32[]{:S(2)}) async-start(), calls=%async_computation.5 | async-start | bytes 1769472 | tf_op jit(solution)/shard_map/reduce_scatter | solution.py:757
  355.5 3.6 copy-start.5
  355.5 3.6 copy-start.32
  372.7 1.5 copy-start.23
  372.7 1.5 copy-start.25
  372.7 1.6 copy-start.21
  372.7 1.6 copy-start.14
  372.7 1.9 copy-start.15
  374.6 0.9 copy-start.26
  379.9 1.3 copy-start.19
  382.1 2.6 copy-start.18
  386.6 3.3 copy-start.1
  386.6 3.3 copy-start.37
  389.5 1.8 copy-start.33
  391.3 160.5 %copy-start.39 = (f32[192]{0:T(256)S(1)}, f32[192]{0:T(256)}, u32[]{:S(2)}) copy-start(f32[192]{0:T(256)} %copy-done.38) | copy-start | bytes 2308
  549.1 2.7 copy-start.4
  557.8 1.8 copy-start.7
  557.8 2.0 copy-start.12
Sparse Core Ops, SparseCore 0:
  161.9 17.3 all-gather.2
  205.2 9.8 reduce-scatter.2
  329.6 19.8 all-gather.4
  380.0 9.8 reduce-scatter.4

commit v4 on v3

v4 whole, which is shorter than its diff:
```python
import functools
import math

import jax
import jax.numpy as jnp
from jax import lax
from jax.experimental import pallas as pl
from jax.experimental.pallas import tpu as pltpu
from jax.sharding import PartitionSpec as P

NORM_EPS = 1e-06
ROPE_BASE = 1000000.0
MASKED = -1e30
MESH_ID = pl.DeviceIdType.MESH
PLANE = 4
DP = ("z", "p", "o")
LANE = 128
TILE = 256
BF = jnp.bfloat16
F32 = jnp.float32


def layout(lengths_row, token_count):
    row_ends = jnp.cumsum(lengths_row)
    places = jnp.arange(token_count, dtype=jnp.int32)
    passed = (places[:, None] >= row_ends[None, :]).astype(jnp.int32)
    segment = jnp.sum(passed, axis=1)
    offset = jnp.sum(passed * lengths_row[None, :], axis=1)
    return (segment, places - offset)


def rotary_tables(positions, head_dim):
    half_dim = head_dim // 2
    frequency = jnp.exp(
        jnp.arange(half_dim, dtype=F32) * (-2.0 * math.log(ROPE_BASE) / head_dim)
    )
    angles = positions.astype(F32)[:, None] * frequency[None, :]
    cosine = jnp.cos(angles)
    sine_tab = jnp.sin(angles)
    return (jnp.concatenate([cosine, cosine], -1), jnp.concatenate([-sine_tab, sine_tab], -1))


def dot(left, right):
    return jnp.dot(left, right, preferred_element_type=F32)


def dot_last(left, right):
    return lax.dot_general(left, right, (((1,), (1,)), ((), ())), preferred_element_type=F32)


def dot_first(left, right):
    return lax.dot_general(left, right, (((0,), (0,)), ((), ())), preferred_element_type=F32)


def flipped(index, mask):
    bit = 1
    while bit <= mask:
        if mask & bit:
            index = index + bit - 2 * bit * lax.rem(lax.div(index, bit), 2)
        bit *= 2
    return index


def moved(index, other, count):
    total, bit = 0, 1
    while bit < count:
        a, b = lax.rem(lax.div(index, bit), 2), lax.rem(lax.div(other, bit), 2)
        total = total + bit * (a + b - 2 * a * b)
        bit *= 2
    return total


def spot(z, p, c):
    return {"z": z, "p": p, "head": c}


def here():
    return (lax.axis_index("z"), lax.axis_index("p"), lax.axis_index("head"))


def greet(peers):
    bar = pltpu.get_barrier_semaphore()
    for peer in peers:
        pl.semaphore_signal(bar, inc=1, device_id=peer, device_id_type=MESH_ID)
    pl.semaphore_wait(bar, len(peers))


def push(src, dst, ssem, rsem, peer):
    copy = pltpu.make_async_remote_copy(
        src_ref=src, dst_ref=dst, send_sem=ssem, recv_sem=rsem,
        device_id=peer, device_id_type=MESH_ID,
    )
    copy.start()
    return copy


def landed(ref, sem):
    pltpu.make_async_copy(ref, ref, sem).wait()


def line_of(table, start, count):
    return jnp.concatenate([table[i : i + 1, :] for i in range(start, start + count)], axis=1)


def wide_mean(value):
    return jnp.mean(value, axis=-1, keepdims=True)


def softmax_of(query, key, mask_bias):
    scores = dot_last(query, key) * (1.0 / math.sqrt(query.shape[-1])) + mask_bias
    top = jnp.max(scores, axis=-1, keepdims=True)
    exp_scores = jnp.exp(scores - top)
    return exp_scores / jnp.sum(exp_scores, axis=-1, keepdims=True)


def gather_kernel(
    quarters,
    part_cols,
    aset,
    vec,
    gate,
    up,
    down,
    grad,
    hidden,
    cosine,
    sine_tab,
    mask_bias,
    aset_all,
    vec_sum,
    gate_all,
    up_all,
    down_all,
    grad_all,
    h1_all,
    q_out,
    k_out,
    v_out,
    o_out,
    r1_out,
    h2_out,
    vec_all,
    halves,
    pair_out,
    pair_in,
    a_send,
    a_recv,
    m_send,
    m_recv,
    s_send,
    s_recv,
    g_send,
    g_recv,
    p_send,
    p_recv,
    l_sem,
):
    z, p, c = here()
    dp = z * PLANE + p
    units = gate.shape[1]
    shards, depth = aset_all.shape[:2]
    rows, width = hidden.shape
    head_dim = cosine.shape[1]
    query_width = q_out.shape[1]
    qkv_width = query_width + 2 * head_dim
    group_heads = query_width // head_dim
    wide = width // LANE

    def at(zz, pp):
        return spot(zz, pp, c)

    pair = spot(z, p, 1 - c)
    masks = [(kz, kp) for kz in range(quarters) for kp in range(PLANE) if kz or kp]
    greet([at(flipped(z, kz), flipped(p, kp)) for kz, kp in masks] + [pair])

    px, py = flipped(p, 1), flipped(p, 2)
    sent = []

    def send(*args):
        sent.append(push(*args))

    def cols_of(weight, quarter):
        first = jnp.minimum(quarter * part_cols, units - part_cols)
        return weight.at[:, pl.ds(pl.multiple_of(first, LANE), part_cols)]

    sets = [(aset_all, lambda zz: aset, a_send, a_recv)] + [
        (whole, functools.partial(cols_of, weight), m_send.at[i], m_recv.at[i])
        for i, (whole, weight) in enumerate(((gate_all, gate), (up_all, up), (down_all, down)))
    ]

    def line(s, k):
        whole, part, ss, rs = sets[s]
        zz = flipped(z, k)
        send(part(zz), whole.at[dp], ss.at[k, 0], rs.at[k, 0], at(zz, p))

    def came(s, k, role):
        whole, _, _, rs = sets[s]
        landed(whole.at[flipped(z, k) * PLANE + flipped(p, role)], rs.at[k, role])

    def fan(s, k):
        whole, part, ss, rs = sets[s]
        slot = flipped(z, k) * PLANE + p
        src = whole.at[slot] if k else part(z)
        if k:
            came(s, k, 0)
        send(src, whole.at[slot], ss.at[k, 1], rs.at[k, 1], at(z, px))
        send(src, whole.at[slot], ss.at[k, 2], rs.at[k, 2], at(z, py))

    def relay(s, k):
        whole, _, ss, rs = sets[s]
        role = 1 if k % 2 == 0 else 2
        came(s, k, role)
        slot = flipped(z, k) * PLANE + flipped(p, role)
        to = py if role == 1 else px
        send(whole.at[slot], whole.at[slot], ss.at[k, 3], rs.at[k, 3], at(z, to))

    def rest(s, k):
        came(s, k, 2 if k % 2 == 0 else 1)
        came(s, k, 3)

    others = range(1, quarters)
    for n, (kz, kp) in enumerate(masks):
        send(vec, vec_all.at[dp], s_send.at[n], s_recv.at[n], at(flipped(z, kz), flipped(p, kp)))
    local = [
        pltpu.make_async_copy(vec, vec_all.at[dp], l_sem.at[0]),
        pltpu.make_async_copy(aset, aset_all.at[dp], l_sem.at[1]),
        pltpu.make_async_copy(cols_of(gate, z), gate_all.at[dp], l_sem.at[2]),
        pltpu.make_async_copy(cols_of(up, z), up_all.at[dp], l_sem.at[3]),
        pltpu.make_async_copy(cols_of(down, z), down_all.at[dp], l_sem.at[4]),
        pltpu.make_async_copy(grad, grad_all.at[0, c], l_sem.at[5]),
    ]
    fan(0, 0)
    for k in others:
        line(0, k)
    for s in (1, 2, 3):
        for k in others:
            line(s, k)
    for copy in local:
        copy.start()
    send(grad, grad_all.at[0, c], g_send.at[0, 1], g_recv.at[0, 1], pair)
    for k in others:
        send(grad, grad_all.at[k, c], g_send.at[k, 0], g_recv.at[k, 0], at(flipped(z, k), p))
    fan(1, 0)

    local[0].wait()
    for n, (kz, kp) in enumerate(masks):
        landed(vec_all.at[flipped(z, kz) * PLANE + flipped(p, kp)], s_recv.at[n])
    total = vec_all[0].astype(F32)
    for i in range(1, shards):
        total = total + vec_all[i].astype(F32)
    vec_sum[...] = total
    x = hidden[...]
    normed = x * lax.rsqrt(wide_mean(x * x) + NORM_EPS) * line_of(total, 0, wide)
    h1_all[c] = normed.astype(BF)
    send(h1_all.at[c], h1_all.at[c], p_send.at[0], p_recv.at[0], pair)

    relay(0, 0)
    for k in others:
        fan(0, k)
    fan(2, 0)
    fan(3, 0)
    for k in others:
        relay(0, k)
    relay(1, 0)
    local[1].wait()
    for k in range(quarters):
        rest(0, k)
    landed(h1_all.at[1 - c], p_recv.at[0])

    def project(n):
        cols = slice(n * TILE, (n + 1) * TILE)
        weight = aset_all[:, :, cols].reshape(width, TILE)
        out = dot(h1_all[...].reshape(2 * rows, width), weight)
        out = out + line_of(vec_sum[...], 2 * wide + n * TILE // LANE, TILE // LANE)
        for j in range(TILE // head_dim):
            head = n * TILE // head_dim + j
            u = out[:, j * head_dim : (j + 1) * head_dim]
            if head <= group_heads:
                u = u * cosine[...] + pltpu.roll(u, head_dim // 2, 1) * sine_tab[...]
            u = u.astype(BF)
            if head < group_heads:
                q_out[:, head * head_dim : (head + 1) * head_dim] = u
            elif head == group_heads:
                k_out[...] = u
            else:
                v_out[...] = u

    def attend(head):
        cols = slice(head * head_dim, (head + 1) * head_dim)
        probs = softmax_of(q_out[:, cols], k_out[...], mask_bias[...])
        o_out[:, cols] = dot(probs.astype(BF), v_out[...]).astype(BF)

    def leave(i):
        half = shards // 2
        weight = aset_all[i * half : (i + 1) * half, :, qkv_width:].reshape(width // 2, query_width)
        out = dot_last(o_out[...], weight)
        cols = slice(i * width // 2, (i + 1) * width // 2)
        halves[0, :, cols] = out[:rows]
        halves[1, :, cols] = out[rows:]

    def swap():
        pair_out[...] = halves[1 - c].astype(BF)
        send(pair_out, pair_in, p_send.at[1], p_recv.at[1], pair)

    def enter():
        landed(pair_in, p_recv.at[1])
        residual = hidden[...] + halves[c] + pair_in[...].astype(F32)
        r1_out[...] = residual
        gain = line_of(vec_sum[...], wide, wide)
        h2_out[...] = (residual * lax.rsqrt(wide_mean(residual * residual) + NORM_EPS) * gain).astype(BF)

    work = [functools.partial(project, n) for n in range(qkv_width // TILE)]
    work += [functools.partial(attend, head) for head in range(group_heads)]
    work += [functools.partial(leave, i) for i in range(2)] + [swap, enter]
    moves = [functools.partial(fan, 1, k) for k in others]
    moves += [functools.partial(relay, s, 0) for s in (2, 3)]
    for k in others:
        moves += [functools.partial(fan, 2, k), functools.partial(relay, 1, k)]
    for k in others:
        moves += [functools.partial(fan, 3, k), functools.partial(relay, 2, k)]
    moves += [functools.partial(relay, 3, k) for k in others]
    for i in range(max(len(work), len(moves))):
        if i < len(moves):
            moves[i]()
        if i < len(work):
            work[i]()
    for k in others:
        slot = grad_all.at[k, c]
        landed(slot, g_recv.at[k, 0])
        send(slot, slot, g_send.at[k, 1], g_recv.at[k, 1], pair)
    for k in range(quarters):
        landed(grad_all.at[k, 1 - c], g_recv.at[k, 1])
    for s in (1, 2, 3):
        for k in range(quarters):
            rest(s, k)
    for copy in local[2:]:
        copy.wait()
    for copy in sent:
        copy.wait_send()


def gather_all(aset, vec, gate, up, down, grad, hidden, cosine, sine_tab, mask_bias, quarters, part_cols):
    shards = quarters * PLANE
    depth, query_width = aset.shape[0], aset.shape[1]
    head_dim = cosine.shape[1]
    query_width = (aset.shape[1] - 2 * head_dim) // 2
    rows, width = hidden.shape
    dma = pltpu.SemaphoreType.DMA
    hbm = pl.BlockSpec(memory_space=pl.ANY)
    vmem = pl.BlockSpec(memory_space=pltpu.VMEM)
    shape = jax.ShapeDtypeStruct
    part = shape((shards, depth, part_cols), BF)
    return pl.pallas_call(
        functools.partial(gather_kernel, quarters, part_cols),
        out_shape=(
            shape((shards,) + aset.shape, BF),
            shape(vec.shape, F32),
            part,
            part,
            part,
            shape((quarters, 2) + grad.shape, BF),
            shape((2, rows, width), BF),
            shape((2 * rows, query_width), BF),
            shape((2 * rows, head_dim), BF),
            shape((2 * rows, head_dim), BF),
            shape((2 * rows, query_width), BF),
            shape((rows, width), F32),
            shape((rows, width), BF),
        ),
        in_specs=[hbm] * 6 + [vmem] * 4,
        out_specs=[vmem] * 2 + [hbm] * 4 + [vmem] * 7,
        scratch_shapes=[
            pltpu.VMEM((shards,) + vec.shape, BF),
            pltpu.VMEM((2, rows, width), F32),
            pltpu.VMEM((rows, width), BF),
            pltpu.VMEM((rows, width), BF),
            dma((quarters, 4)),
            dma((quarters, 4)),
            dma((3, quarters, 4)),
            dma((3, quarters, 4)),
            dma((shards - 1,)),
            dma((shards - 1,)),
            dma((quarters, 2)),
            dma((quarters, 2)),
            dma((2,)),
            dma((2,)),
            dma((6,)),
        ],
        compiler_params=pltpu.CompilerParams(
            collective_id=0, has_side_effects=True, vmem_limit_bytes=40 * 2**20
        ),
    )(aset, vec, gate, up, down, grad, hidden, cosine, sine_tab, mask_bias)


def mlp_kernel(
    quarters,
    hidden,
    own,
    grads,
    gate,
    up,
    down,
    y_out,
    d_out,
    gate_out,
    up_out,
    down_out,
    h_all,
    g_all,
    w_all,
    act,
    d_gate,
    d_up,
    y_part,
    d_part,
    y_slot,
    d_slot,
    d_line,
    h_send,
    h_recv,
    hp_send,
    hp_recv,
    y_send,
    y_recv,
    d_send,
    d_recv,
    l_send,
    l_recv,
    load_sem,
    out_sem,
):
    z, p, c = here()
    pair = spot(z, p, 1 - c)
    rows, width = own.shape
    part_cols = gate.shape[1]
    padded = w_all.shape[2]
    tiles = padded // TILE

    def half(k, lane):
        return h_all.at[k, pl.ds(pl.multiple_of(lane * rows, 16), rows)]

    loads = [
        pltpu.make_async_copy(w, w_all.at[i, :, pl.ds(0, part_cols)], load_sem.at[i])
        for i, w in enumerate((gate, up, down))
    ] + [pltpu.make_async_copy(grads, g_all, load_sem.at[3]), pltpu.make_async_copy(own, half(0, c), load_sem.at[4])]
    for copy in loads:
        copy.start()
    greet([spot(flipped(z, k), p, c) for k in range(1, quarters)] + [pair])
    push(own, half(0, c), hp_send.at[0], hp_recv.at[0], pair)
    for k in range(1, quarters):
        push(own, half(k, c), h_send.at[k], h_recv.at[k], spot(flipped(z, k), p, c))
    if padded > part_cols:
        for i in range(3):
            w_all[i, :, part_cols:] = jnp.zeros((width, padded - part_cols), w_all.dtype)
    first = jnp.minimum(z * part_cols, hidden - part_cols)
    skip = z * part_cols - first
    for copy in loads:
        copy.wait()

    def finish(k):
        mine, other = (y_part.at[k, c], y_slot.at[k])
        landed(other, y_recv.at[k])
        other[...] = (other[...].astype(F32) + mine[...].astype(F32)).astype(other.dtype)
        pltpu.make_async_copy(other, y_out.at[k], out_sem.at[0, k]).start()
        mine, other = (d_part.at[k, c], d_slot.at[k])
        landed(other, d_recv.at[k])
        other[...] = (other[...].astype(F32) + mine[...].astype(F32)).astype(other.dtype)

        @pl.when(k > 0)
        def _():
            push(other, d_line.at[k], l_send.at[k], l_recv.at[k], spot(moved(z, k, quarters), p, c))

    def block(k, carry):
        @pl.when(k > 0)
        def _():
            landed(half(k, c), h_recv.at[k])
            push(half(k, c), half(k, c), hp_send.at[k], hp_recv.at[k], pair)

        landed(half(k, 1 - c), hp_recv.at[k])

        def units(n, carry):
            cols = pl.ds(pl.multiple_of(n * TILE, TILE), TILE)
            h = h_all[k]
            g = jnp.dot(h, w_all[0, :, cols], preferred_element_type=F32)
            u = jnp.dot(h, w_all[1, :, cols], preferred_element_type=F32)
            da = jnp.dot(g_all[k], w_all[2, :, cols], preferred_element_type=F32)
            column = n * TILE + lax.broadcasted_iota(jnp.int32, (1, TILE), 1)
            ok = column >= skip
            g = jnp.where(ok, g, 0.0)
            u = jnp.where(ok, u, 0.0)
            s = 1.0 / (1.0 + jnp.exp(-g))
            sg = g * s
            act[k, :, cols] = (sg * u).astype(BF)
            d_gate[k, :, cols] = (da * u * s * (1.0 + g * (1.0 - s))).astype(BF)
            d_up[k, :, cols] = (da * sg).astype(BF)
            return carry

        lax.fori_loop(0, tiles, units, 0)

        @pl.when(k > 0)
        def _():
            finish(k - 1)

        def model(n, carry):
            cols = pl.ds(pl.multiple_of(n * TILE, TILE), TILE)

            def back(left, index):
                return lax.dot_general(
                    left[k], w_all[index, cols, :], (((1,), (1,)), ((), ())),
                    preferred_element_type=F32,
                )

            y = back(act, 2).astype(BF)
            d = (back(d_gate, 0) + back(d_up, 1)).astype(BF)
            for lane in range(2):
                y_part[k, lane, :, cols] = y[lane * rows : (lane + 1) * rows]
                d_part[k, lane, :, cols] = d[lane * rows : (lane + 1) * rows]
            return carry

        lax.fori_loop(0, width // TILE, model, 0)
        push(y_part.at[k, 1 - c], y_slot.at[k], y_send.at[k], y_recv.at[k], pair)
        push(d_part.at[k, 1 - c], d_slot.at[k], d_send.at[k], d_recv.at[k], pair)
        return carry

    lax.fori_loop(0, quarters, block, 0)
    finish(quarters - 1)

    outs = (gate_out, up_out, down_out)

    def weight(n, carry):
        cols = pl.ds(pl.multiple_of(n * TILE, TILE), TILE)
        for i, (left, right) in enumerate(((h_all, d_gate), (h_all, d_up), (g_all, act))):
            total = None
            for k in range(quarters):
                term = lax.dot_general(
                    left[k, :, cols], right[k], (((0,), (0,)), ((), ())),
                    preferred_element_type=F32,
                )
                total = term if total is None else total + term
            w_all[i, cols, :] = total.astype(BF)
            pltpu.make_async_copy(
                w_all.at[i, cols, pl.ds(0, part_cols)], outs[i].at[cols, :], out_sem.at[1 + i, n]
            ).start()
        return carry

    lax.fori_loop(0, width // TILE, weight, 0)
    total = d_slot[0].astype(F32)
    for k in range(1, quarters):
        landed(d_line.at[k], l_recv.at[k])
        total = total + d_line[k].astype(F32)
    d_out[...] = total
    for n in range(width // TILE):
        for i in range(3):
            tile = w_all.at[i, pl.ds(n * TILE, TILE), pl.ds(0, part_cols)]
            pltpu.make_async_copy(tile, outs[i].at[pl.ds(n * TILE, TILE), :], out_sem.at[1 + i, n]).wait()
    for k in range(quarters):
        pltpu.make_async_copy(y_slot.at[k], y_out.at[k], out_sem.at[0, k]).wait()
        landed(half(k, c), hp_send.at[k])
        landed(y_part.at[k, 1 - c], y_send.at[k])
        landed(d_part.at[k, 1 - c], d_send.at[k])
        if k:
            landed(own, h_send.at[k])
            landed(d_slot.at[k], l_send.at[k])


def mlp_all(own, grads, gate, up, down, hidden):
    bf = jnp.bfloat16
    quarters, block_rows, width = grads.shape
    part_cols = gate.shape[1]
    padded = -(-part_cols // TILE) * TILE
    rows = own.shape[0]
    dma = pltpu.SemaphoreType.DMA
    hbm = pl.BlockSpec(memory_space=pl.ANY)
    vmem = pl.BlockSpec(memory_space=pltpu.VMEM)
    grad_w = jax.ShapeDtypeStruct((width, part_cols), bf)
    steps = max(quarters, width // TILE)
    return pl.pallas_call(
        functools.partial(mlp_kernel, quarters, hidden),
        out_shape=(
            jax.ShapeDtypeStruct((quarters, rows, width), bf),
            jax.ShapeDtypeStruct((rows, width), F32),
            grad_w,
            grad_w,
            grad_w,
        ),
        in_specs=[hbm] * 5,
        out_specs=[hbm, vmem, hbm, hbm, hbm],
        scratch_shapes=[
            pltpu.VMEM((quarters, block_rows, width), bf),
            pltpu.VMEM((quarters, block_rows, width), bf),
            pltpu.VMEM((3, width, padded), bf),
            pltpu.VMEM((quarters, block_rows, padded), bf),
            pltpu.VMEM((quarters, block_rows, padded), bf),
            pltpu.VMEM((quarters, block_rows, padded), bf),
            pltpu.VMEM((quarters, 2, rows, width), bf),
            pltpu.VMEM((quarters, 2, rows, width), bf),
            pltpu.VMEM((quarters, rows, width), bf),
            pltpu.VMEM((quarters, rows, width), bf),
            pltpu.VMEM((quarters, rows, width), bf),
        ]
        + [dma((quarters,))] * 10
        + [dma((5,)), dma((4, steps))],
        compiler_params=pltpu.CompilerParams(
            collective_id=2, has_side_effects=True, vmem_limit_bytes=60 * 2**20
        ),
    )(own, grads, gate, up, down)


AHEAD = 1
LAG = 1


def reduce_kernel(
    quarters,
    gate,
    up,
    down,
    y_half,
    d_sum,
    r1,
    out_grad,
    hidden,
    h1_all,
    q_in,
    k_in,
    v_in,
    o_in,
    aset_all,
    vec_sum,
    cosine,
    sine_tab,
    mask_bias,
    small_sum,
    attn_sum,
    block_out,
    grad_in,
    gate_out,
    up_out,
    down_out,
    small,
    small_all,
    staged,
    attn_slots,
    mlp_slots,
    mlp_own,
    attn_line,
    y_line,
    attn_grads,
    da_all,
    dr1,
    do_all,
    dqkv,
    dk_sum,
    dv_sum,
    halves,
    pair_out,
    pair_in,
    t_send,
    t_recv,
    z_send,
    z_recv,
    s_send,
    s_recv,
    y_send,
    y_recv,
    p_send,
    p_recv,
    l_sem,
    own_sem,
):
    z, p, c = here()
    dp = z * PLANE + p
    pair = spot(z, p, 1 - c)
    shards, depth, attn_width = aset_all.shape
    rows, width = r1.shape
    head_dim = cosine.shape[1]
    query_width = q_in.shape[1]
    qkv_width = query_width + 2 * head_dim
    group_heads = query_width // head_dim
    wide = width // LANE
    others = range(1, quarters)
    scale = 1.0 / math.sqrt(head_dim)
    sources = (attn_grads, gate, up, down)
    outs = (None, gate_out, up_out, down_out)

    def source(s, k, kp):
        return sources[s].at[flipped(z, k) * PLANE + flipped(p, kp)]

    ks = list(others) + [0]
    units = [(s, k) for i in range(0, quarters, 2) for s in (1, 2, 3) for k in ks[i : i + 2]]
    for s, k in units:
        for i, kp in enumerate((0, 2 - k % 2)):
            pltpu.make_async_copy(source(s, k, kp), mlp_own.at[s - 1, k, i], own_sem.at[s - 1, k, i]).start()
    first_y = pltpu.make_async_copy(y_half.at[0], y_line.at[0], l_sem.at[0])
    first_y.start()
    masks = [(kz, kp) for kz in range(quarters) for kp in range(PLANE) if kz or kp]
    greet([spot(flipped(z, kz), flipped(p, kp), c) for kz, kp in masks] + [pair])
    sent = []
    local = []

    def send(*args):
        sent.append(push(*args))

    side = [spot(z, flipped(p, 1), c), spot(z, flipped(p, 2), c)]

    def slots(s, k, role):
        return attn_slots.at[k, role] if s == 0 else mlp_slots.at[s - 1, k, role]

    def term(s, k, i):
        if s == 0:
            return source(s, k, (0, 2 - k % 2)[i])
        return mlp_own.at[s - 1, k, i]

    def ready(s, k, i):
        if s:
            landed(mlp_own.at[s - 1, k, i], own_sem.at[s - 1, k, i])

    def first(s, k):
        way = k % 2
        send(source(s, k, 3), slots(s, k, 0), t_send.at[s, k, 0], t_recv.at[s, k, 0], side[way])
        send(source(s, k, 1 + way), slots(s, k, 1), t_send.at[s, k, 1], t_recv.at[s, k, 1], side[way])

    def relay(s, k):
        slot = slots(s, k, 0)
        ready(s, k, 1)
        landed(slot, t_recv.at[s, k, 0])
        slot[...] = (slot[...].astype(F32) + term(s, k, 1)[...].astype(F32)).astype(BF)
        send(slot, slots(s, k, 2), t_send.at[s, k, 2], t_recv.at[s, k, 2], side[1 - k % 2])

    def last(s, k):
        one, two = (slots(s, k, 1), slots(s, k, 2))
        ready(s, k, 0)
        landed(one, t_recv.at[s, k, 1])
        landed(two, t_recv.at[s, k, 2])
        total = term(s, k, 0)[...].astype(F32) + one[...].astype(F32) + two[...].astype(F32)
        one[...] = total.astype(BF)
        if s == 0:
            if k:
                send(one, attn_line.at[k], z_send.at[s, k], z_recv.at[s, k], spot(flipped(z, k), p, c))
        elif k:
            send(one, outs[s].at[z], z_send.at[s, k], z_recv.at[s, k], spot(flipped(z, k), p, c))
        else:
            copy = pltpu.make_async_copy(one, outs[s].at[z], l_sem.at[s])
            copy.start()
            local.append(copy)

    def note(value, start):
        for i in range(value.shape[1] // LANE):
            small[start + i : start + i + 1, :] = value[:, i * LANE : (i + 1) * LANE]

    def norm_back():
        residual, dh2 = (r1[...], d_sum[...])
        rho = lax.rsqrt(wide_mean(residual * residual) + NORM_EPS)
        n = residual * rho
        inner = dh2 * line_of(vec_sum[...], wide, wide)
        note(jnp.sum(dh2 * n, axis=0, keepdims=True), wide)
        total = out_grad[...] + rho * (inner - n * wide_mean(inner * n))
        dr1[...] = total
        da_all[c] = total.astype(BF)
        send(da_all.at[c], da_all.at[c], p_send.at[0], p_recv.at[0], pair)

    def heads_back(n):
        if n == 0:
            landed(da_all.at[1 - c], p_recv.at[0])
        cols = slice(n * TILE, (n + 1) * TILE)
        weight = aset_all[:, :, qkv_width + n * TILE : qkv_width + (n + 1) * TILE]
        do_all[:, cols] = dot(da_all[...].reshape(2 * rows, width), weight.reshape(width, TILE)).astype(BF)

    def unrotate(value):
        return value * cosine[...] - pltpu.roll(value, head_dim // 2, 1) * sine_tab[...]

    def attend_back(head):
        cols = slice(head * head_dim, (head + 1) * head_dim)
        query, grad = (q_in[:, cols], do_all[:, cols])
        probs = softmax_of(query, k_in[...], mask_bias[...])
        grad_probs = dot_last(grad, v_in[...])
        centre = jnp.sum(grad_probs * probs, axis=-1, keepdims=True)
        grad_scores = (probs * (grad_probs - centre) * scale).astype(BF)
        dqkv[:, cols] = unrotate(dot(grad_scores, k_in[...])).astype(BF)
        key_term = dot_first(grad_scores, query)
        value_term = dot_first(probs.astype(BF), grad)
        dk_sum[...] = key_term if head == 0 else dk_sum[...] + key_term
        dv_sum[...] = value_term if head == 0 else dv_sum[...] + value_term

    def keys_back():
        dqkv[:, query_width : query_width + head_dim] = unrotate(dk_sum[...]).astype(BF)
        dqkv[:, query_width + head_dim :] = dv_sum[...].astype(BF)
        note(jnp.sum(dqkv[...].astype(F32), axis=0, keepdims=True), 2 * wide)

    def inputs_back(i):
        half = shards // 2
        weight = aset_all[i * half : (i + 1) * half, :, :qkv_width].reshape(width // 2, qkv_width)
        out = dot_last(dqkv[...], weight)
        cols = slice(i * width // 2, (i + 1) * width // 2)
        halves[0, :, cols] = out[:rows]
        halves[1, :, cols] = out[rows:]
        if i:
            pair_out[...] = halves[1 - c].astype(BF)
            send(pair_out, pair_in, p_send.at[1], p_recv.at[1], pair)

    def weights_back(i):
        cols = slice(i * 4 * depth, (i + 1) * 4 * depth)
        blocks = slice(i * 4, (i + 1) * 4)
        left = h1_all[:, :, cols].reshape(2 * rows, 4 * depth)
        attn_grads[blocks, :, :qkv_width] = (
            dot_first(left, dqkv[...]).astype(BF).reshape(4, depth, qkv_width)
        )
        left = da_all[:, :, cols].reshape(2 * rows, 4 * depth)
        attn_grads[blocks, :, qkv_width:] = (
            dot_first(left, o_in[...]).astype(BF).reshape(4, depth, query_width)
        )

    def leave():
        landed(pair_in, p_recv.at[1])
        x = hidden[...]
        dh1 = halves[c] + pair_in[...].astype(F32)
        rho = lax.rsqrt(wide_mean(x * x) + NORM_EPS)
        n = x * rho
        inner = dh1 * line_of(vec_sum[...], 0, wide)
        note(jnp.sum(dh1 * n, axis=0, keepdims=True), 0)
        grad_in[...] = dr1[...] + rho * (inner - n * wide_mean(inner * n))
        for n, (kz, kp) in enumerate(masks):
            peer = spot(flipped(z, kz), flipped(p, kp), c)
            send(small, small_all.at[dp], s_send.at[n], s_recv.at[n], peer)
        small_all[dp] = small[...]

    work = [norm_back] + [functools.partial(heads_back, n) for n in range(query_width // TILE)]
    work += [functools.partial(attend_back, head) for head in range(group_heads)]
    work += [keys_back] + [functools.partial(inputs_back, i) for i in range(2)]
    work += [functools.partial(weights_back, i) for i in range(shards // 4)] + [leave]

    mlp_count = len(units)
    for k in others:
        send(y_half.at[k], y_line.at[k], y_send.at[k], y_recv.at[k], spot(flipped(z, k), p, c))
    units += [(0, k) for k in ks]
    for i in range(-AHEAD, len(units) + LAG):
        if i + AHEAD == mlp_count:
            while work:
                work.pop(0)()
        if 0 <= i + AHEAD < len(units):
            first(*units[i + AHEAD])
        if 0 <= i < len(units):
            relay(*units[i])
        if 0 <= i - LAG:
            last(*units[i - LAG])
        for _ in range(2):
            if work:
                work.pop(0)()
    for n, (kz, kp) in enumerate(masks):
        landed(small_all.at[flipped(z, kz) * PLANE + flipped(p, kp)], s_recv.at[n])
    total = small_all[0]
    for i in range(1, shards):
        total = total + small_all[i]
    staged[...] = total
    small_sum[c] = total
    send(staged, small_sum.at[c], s_send.at[len(masks)], s_recv.at[len(masks)], pair)
    first_y.wait()
    total = r1[...] + y_line[0].astype(F32)
    for k in others:
        landed(y_line.at[k], y_recv.at[k])
        total = total + y_line[k].astype(F32)
    block_out[...] = total
    landed(small_sum.at[1 - c], s_recv.at[len(masks)])
    total = attn_slots[0, 1].astype(F32)
    for k in others:
        landed(attn_line.at[k], z_recv.at[0, k])
        total = total + attn_line[k].astype(F32)
    attn_sum[...] = total
    for s in (1, 2, 3):
        for k in others:
            landed(outs[s].at[flipped(z, k)], z_recv.at[s, k])
    for copy in local:
        copy.wait()
    for copy in sent:
        copy.wait_send()


def reduce_all(quarters, mlp_grads, y_half, d_sum, r1, out_grad, hidden, h1_all, heads, aset_all, vec_sum, tables):
    shards = quarters * PLANE
    dma = pltpu.SemaphoreType.DMA
    depth, part_cols = mlp_grads[0].shape[1:]
    rows, width = r1.shape
    tokens, query_width = heads[0].shape
    head_dim = heads[1].shape[1]
    qkv_width = query_width + 2 * head_dim
    attn_shape = aset_all.shape[1:]
    vec_shape = vec_sum.shape
    vmem = pl.BlockSpec(memory_space=pltpu.VMEM)
    hbm = pl.BlockSpec(memory_space=pl.ANY)
    shape = jax.ShapeDtypeStruct
    quarter_out = shape((quarters, depth, part_cols), BF)
    return pl.pallas_call(
        functools.partial(reduce_kernel, quarters),
        out_shape=(
            shape((2,) + vec_shape, F32),
            shape(attn_shape, F32),
            shape((rows, width), F32),
            shape((rows, width), F32),
            quarter_out,
            quarter_out,
            quarter_out,
        ),
        in_specs=[hbm] * 4 + [vmem] * 14,
        out_specs=[vmem] * 4 + [hbm] * 3,
        scratch_shapes=[
            pltpu.VMEM(vec_shape, F32),
            pltpu.VMEM((shards,) + vec_shape, F32),
            pltpu.VMEM(vec_shape, F32),
            pltpu.VMEM((quarters, 3) + attn_shape, BF),
            pltpu.VMEM((3, quarters, 3, depth, part_cols), BF),
            pltpu.VMEM((3, quarters, 2, depth, part_cols), BF),
            pltpu.VMEM((quarters,) + attn_shape, BF),
            pltpu.VMEM((quarters, rows, width), BF),
            pltpu.VMEM((shards,) + attn_shape, BF),
            pltpu.VMEM((2, rows, width), BF),
            pltpu.VMEM((rows, width), F32),
            pltpu.VMEM((tokens, query_width), BF),
            pltpu.VMEM((tokens, qkv_width), BF),
            pltpu.VMEM((tokens, head_dim), F32),
            pltpu.VMEM((tokens, head_dim), F32),
            pltpu.VMEM((2, rows, width), F32),
            pltpu.VMEM((rows, width), BF),
            pltpu.VMEM((rows, width), BF),
            dma((4, quarters, 3)),
            dma((4, quarters, 3)),
            dma((4, quarters)),
            dma((4, quarters)),
            dma((shards,)),
            dma((shards,)),
            dma((quarters,)),
            dma((quarters,)),
            dma((2,)),
            dma((2,)),
            dma((4,)),
            dma((3, quarters, 2)),
        ],
        compiler_params=pltpu.CompilerParams(
            collective_id=1, has_side_effects=True, vmem_limit_bytes=60 * 2**20
        ),
    )(*mlp_grads, y_half, d_sum, r1, out_grad, hidden, h1_all, *heads, aset_all, vec_sum, *tables)


def local(
    hidden_in,
    row_lengths,
    norm_attn,
    w_query,
    b_query,
    w_key,
    b_key,
    w_value,
    b_value,
    w_out,
    norm_mlp,
    w_gate,
    w_up,
    w_down,
    out_grad,
):
    quarters = lax.axis_size("z")
    lanes = lax.axis_size("head")
    shards = quarters * PLANE
    copies = lax.axis_size("o")
    if copies > 1:
        norm_attn, norm_mlp, w_query, w_key, w_value, w_gate, w_up = [
            lax.all_gather(x, "o", axis=0, tiled=True)
            for x in (norm_attn, norm_mlp, w_query, w_key, w_value, w_gate, w_up)
        ]
        b_query, b_key, b_value, w_out, w_down = [
            lax.all_gather(x, "o", axis=1, tiled=True)
            for x in (b_query, b_key, b_value, w_out, w_down)
        ]
    token_count = hidden_in.shape[0] * lanes
    depth = norm_attn.shape[0]
    width = hidden_in.shape[1]
    head_dim = w_key.shape[1]
    query_width = w_query.shape[1]
    hidden_width = w_gate.shape[1]
    part_width = -(-hidden_width // (LANE * quarters)) * LANE
    segment, positions = layout(row_lengths[0], token_count)
    place = jnp.arange(token_count, dtype=jnp.int32)
    allowed = (segment[:, None] == segment[None, :]) & (place[None, :] <= place[:, None])
    tables = rotary_tables(positions, head_dim) + (jnp.where(allowed, 0.0, MASKED).astype(F32),)

    shard = lax.axis_index("z") * PLANE + lax.axis_index("p")

    def placed(part):
        whole = jnp.zeros((part.shape[0] * shards,), part.dtype)
        return lax.dynamic_update_slice(whole, part, (shard * part.shape[0],)).reshape(-1, LANE)

    vec = jnp.concatenate(
        [placed(x) for x in (norm_attn, norm_mlp, b_query[0], b_key[0], b_value[0])], 0
    )
    aset_all, vec_sum, wg, wu, wd, grad_rows, h1_all, *heads, residual, mlp_low = gather_all(
        jnp.concatenate([w_query, w_key, w_value, w_out.T], 1),
        vec,
        w_gate,
        w_up,
        w_down.T,
        out_grad.astype(BF),
        hidden_in,
        *tables,
        quarters,
        part_width,
    )
    y_half, dh2, *mlp_grads = mlp_all(
        mlp_low,
        grad_rows.reshape(quarters, token_count, width),
        *[w.reshape(width, part_width) for w in (wg, wu, wd)],
        hidden_width,
    )
    small_total, attn_part, block_out, grad_in, *quarter_grads = reduce_all(
        quarters,
        [g.reshape(shards, depth, part_width) for g in mlp_grads],
        y_half,
        dh2,
        residual,
        out_grad,
        hidden_in,
        h1_all,
        heads,
        aset_all,
        vec_sum,
        tables,
    )

    def whole_rows(parts):
        taken = []
        for index in range(quarters):
            skip = max(0, index * part_width - (hidden_width - part_width))
            if skip < part_width:
                taken.append(parts[index][:, skip:])
        return jnp.concatenate(taken, 1).astype(F32)

    grad_w_gate, grad_w_up, grad_w_down = [whole_rows(parts) for parts in quarter_grads]
    if copies > 1:
        small_total = lax.psum(small_total, "o")
        attn_part, grad_w_gate, grad_w_up, grad_w_down = [
            lax.psum_scatter(x, "o", scatter_dimension=0, tiled=True)
            for x in (attn_part, grad_w_gate, grad_w_up, grad_w_down)
        ]
    small_total = small_total.reshape(lanes, -1)
    gain_total = jnp.sum(small_total[:, : 2 * width], 0).reshape(2, width)
    bias_total = small_total[:, 2 * width :]
    return (
        block_out,
        grad_in,
        gain_total[0],
        attn_part[:, :query_width],
        bias_total[:, :query_width],
        attn_part[:, query_width : query_width + head_dim],
        bias_total[:, query_width : query_width + head_dim],
        attn_part[:, query_width + head_dim : query_width + 2 * head_dim],
        bias_total[:, query_width + head_dim :],
        attn_part[:, query_width + 2 * head_dim :].T,
        gain_total[1],
        grad_w_gate,
        grad_w_up,
        grad_w_down.T,
    )


def solution(mesh):
    shards = mesh.shape["dp"]
    copies = max(1, shards // (PLANE * PLANE))
    shape = (shards // (PLANE * copies), PLANE, copies, mesh.shape["head"])
    split = jax.sharding.Mesh(mesh.devices.reshape(shape), DP + ("head",))
    rows = P(DP + ("head",), None)
    deep = P(DP, "head")
    wide = P("head", DP)
    return jax.shard_map(
        local,
        mesh=split,
        in_specs=(
            rows,
            P(DP, None),
            P(DP),
            deep,
            wide,
            deep,
            wide,
            deep,
            wide,
            wide,
            P(DP),
            deep,
            deep,
            wide,
            rows,
        ),
        out_specs=(
            rows,
            rows,
            P(),
            deep,
            P(),
            deep,
            P(),
            deep,
            P(),
            wide,
            P(),
            deep,
            deep,
            wide,
        ),
        check_vma=False,
    )
```

time: 573 us -> 480 us (0.84)
  waiting for transfers between devices: 43.3 us -> 0 us
  matrix products: 42.5 us -> 0 us
  Pallas kernels: 407 us -> 443 us
  other arithmetic: 33.7 us -> 9.5 us
  between operations: 14.4 us -> 0.91 us
    dot_general x14 -> x0, matrix products: 42.5 us -> none  [the longest x4 10.1 us: product(): return jnp.dot(left_side, right_side, preferred_element_type=jnp.float32)]
    all_gather x2 -> x0, waiting for transfers between devices: 33.9 us -> none  [gather(): return lax.all_gather(x, axes, axis=0, tiled=True)]
    pallas_call x1, Pallas kernels: 158 us -> 181 us  [reduce_all(): pl.pallas_call(functools.partial(reduce_kernel, quarters), out_shape=(sha...]
    pallas_call x1, Pallas kernels: 105 us -> 115 us  [mlp_all(): pl.pallas_call(functools.partial(mlp_kernel, quarters, hidden), out_shape...]
    reduce_scatter x2 -> x0, waiting for transfers between devices: 9.35 us -> none  [scatter_sum(): lax.psum_scatter(x.astype(jnp.bfloat16), axes, scatter_dimension=0, tiled...]
    reduce_sum x6 -> x0, other arithmetic: 7.97 us -> none  [the longest x2 4.1 us: rms_norm(): value_rows * lax.rsqrt(jnp.mean(value_rows * value_rows, axis=-1, keepdim...]
    convert_element_type x13 -> x4, other arithmetic: 11.5 us -> 4.49 us  [the longest x2 2.61 us: whole_rows(): return jnp.concatenate(taken, 1).astype(F32)]
    unnamed x86 -> x45, local copies, waits for them, and re-layouts: 9.41 us -> 12.7 us
  transfers between devices with their start and end apart: 4 -> 0, of which waited for: 4 -> 0; matrix products, arithmetic and copies ran while one was open for 2% -> 0% of each run, Pallas kernels for 0% -> 0%
where the time goes in v4:
time: 480 us; the launch traced here: 476 us
  Pallas kernels  443 us (92%)
  local copies, waits for them, and re-layouts  22.3 us (5%)
  other arithmetic  9.5 us (2%)
    pallas_call x1, Pallas kernels, reduce_all(): pl.pallas_call(functools.partial(reduce_kernel, quarters), out_shape=(sha...  181 us
    pallas_call x1, Pallas kernels, gather_all(): pl.pallas_call(functools.partial(gather_kernel, quarters, part_cols), out...  148 us
    pallas_call x1, Pallas kernels, mlp_all(): pl.pallas_call(functools.partial(mlp_kernel, quarters, hidden), out_shape...  115 us
    unnamed x45, local copies, waits for them, and re-layouts  12.7 us

profile of v4, /device:TPU:0, one launch (start us, length us, event | category | flops | bytes accessed | tf_op | source)
XLA Modules:
  0.0 476.0 jit_solution(8960391984080883074)
XLA Ops:
  0.7 0.8 reduce-window.8
  1.5 0.8 dynamic_update_slice.20
  2.2 0.8 dynamic_update_slice.21
  3.0 0.9 dynamic_update_slice.19
  3.9 0.7 convert_reduce_fusion
  4.6 0.9 dynamic_update_slice.17
  5.5 0.8 dynamic_update_slice.18
  6.4 0.2 concatenate.22.vec
  6.5 1.0 pad_maximum_fusion.aset
  7.6 0.0 copy-start.9
  7.6 0.8 fusion.2
  8.3 0.0 copy-start.1
  8.4 0.0 copy-start.7
  8.4 0.0 copy-start.8
  8.4 0.2 pad_maximum_fusion.1
  8.6 0.0 copy-start.3
  8.6 0.0 copy-start.4
  8.6 0.1 fusion.1.mask_bias
  8.7 0.0 copy-start
  8.7 1.9 convert_element_type.20.grad
  10.6 0.0 copy-done.9
  10.6 0.0 copy-done.1
  10.6 0.0 copy-done.7
  10.6 0.3 copy-done.8
  10.9 147.5 %shard_map.254 = (bf16[16,96,1792]{2,1,0:T(8,128)(2,1)}, f32[32,128]{1,0:T(8,128)S(1)}, bf16[16,96,1152]{2,1,0:T(8,128)(2,1)S(1)}, bf16[16,96,1152]{2,1,0:T(8,12...) custom-call(bf16[96,1792]{1,0:T(8,128)(2,1)S(1)} %pad_maximum_fusion, ...), custom_call_target="tpu_custom_call" | custom-call | tf_op jit(solution)/shard_map/pallas_call | solution.py:353
  158.4 0.0 copy-done.3
  158.5 0.0 copy-done.4
  158.5 0.0 copy-done
  158.5 0.0 copy-start.2
  158.5 1.9 copy-done.2
  160.3 0.0 copy-start.5
  160.3 1.0 copy-done.5
  161.4 1.0 copy-done.6
  162.4 0.8 copy-done.10
  163.2 0.8 copy-done.11
  164.0 0.8 copy-done.12
  164.8 0.6 copy-done.13
  165.4 0.6 copy-done.14
  166.1 0.6 copy-done.15
  166.7 115.2 %shard_map.255 = (bf16[4,192,1536]{2,1,0:T(8,128)(2,1)}, f32[192,1536]{1,0:T(8,128)}, bf16[1536,1152]{1,0:T(8,128)(2,1)}, bf16[1536,1152]{1,0:T(8,128)(2,1)}, bf16[1536,1152]{1,0:T(8,128)(2,1)}) custom-call(bf16[192,1536]{1,0:T(8,128)(2,1)} %copy-done.12, bf16[4,384,1536]{2,1,0:T(8,128)(2,1)} %bitcast.50, bf16[1536,1152]{1,0:T(8,128)(2,1)} %bitcast.48, ...), custom_call_target="tpu_custom_call" | custom-call | tf_op jit(solution)/shard_map/pallas_call | solution.py:577
  281.9 180.5 %shard_map.256 = (f32[2,32,128]{2,1,0:T(8,128)}, f32[96,1792]{1,0:T(8,128)}, f32[192,1536]{1,0:T(8,128)}, f32[192,1536]{1,0:T(8,128)}, bf16[4,96,1152]{2,1,0:T(8...) custom-call(bf16[16,96,1152]{2,1,0:T(8,128)(2,1)} %bitcast.53, bf16[16,96,1152]{2,1,0:T(8,128)(2,1)} %bitcast.54, ...), custom_call_target="tpu_custom_call" | custom-call | tf_op jit(solution)/shard_map/pallas_call | solution.py:892
  462.4 0.0 copy-start.20
  462.4 0.9 copy.31
  463.3 0.6 fusion.4
  463.8 0.6 slice.108
  464.5 0.6 fusion.5
  465.1 1.5 fusion.3
  466.5 1.9 slice_bitcast_fusion
  468.4 0.0 copy-done.20
  468.4 0.1 slice_bitcast_fusion.12
  468.5 0.0 copy-start.19
  468.5 1.3 maximum_convert_fusion
  469.8 0.1 copy-done.19
  469.9 0.1 slice_bitcast_fusion.8
  470.0 0.0 copy-start.18
  470.0 1.3 maximum_convert_fusion.1
  471.3 0.1 copy-done.18
  471.4 0.1 slice_bitcast_fusion.4
  471.5 0.0 copy-start.17
  471.5 1.3 convert_bitcast_fusion
  472.8 0.4 copy-done.17
  473.3 1.0 copy.39
  474.3 0.7 copy-done.16
  475.0 1.0 copy.40
  (19 shorter events, 0.1 us)
Async XLA Ops:
  7.6 3.0 copy-start.9
  8.3 2.3 copy-start.1
  8.4 2.3 copy-start.7
  8.4 2.5 copy-start.8
  8.6 149.9 %copy-start.3 = (f32[384,128]{1,0:T(8,128)}, f32[384,128]{1,0:T(8,128)S(1)}, u32[]{:S(2)}) copy-start(f32[384,128]{1,0:T(8,128)S(1)} %get-tuple-element.89.cosine) | copy-start | bytes 589828
  8.6 149.9 %copy-start.4 = (f32[384,128]{1,0:T(8,128)}, f32[384,128]{1,0:T(8,128)S(1)}, u32[]{:S(2)}) copy-start(f32[384,128]{1,0:T(8,128)S(1)} %get-tuple-element.90.sine_tab) | copy-start | bytes 589828
  8.7 149.8 %copy-start = (f32[384,384]{1,0:T(8,128)}, f32[384,384]{1,0:T(8,128)S(1)}, u32[]{:S(2)}) copy-start(f32[384,384]{1,0:T(8,128)S(1)} %fusion.1.mask_bias) | copy-start | bytes 1769476
  158.5 1.9 copy-start.2
  160.3 1.0 copy-start.5
  161.4 1.0 copy-start.6
  162.4 0.8 copy-start.10
  163.2 0.8 copy-start.11
  164.0 0.8 copy-start.12
  164.8 0.6 copy-start.13
  165.4 0.6 copy-start.14
  166.1 0.6 copy-start.15
  462.4 6.0 %copy-start.20 = (bf16[4,96,1152]{2,1,0:T(8,128)(2,1)S(1)}, bf16[4,96,1152]{2,1,0:T(8,128)(2,1)}, u32[]{:S(2)}) copy-start(bf16[4,96,1152]{2,1,0:T(8,128)(2,1)} %get-tuple-element.61) | copy-start | bytes 2654212
  468.5 1.4 copy-start.19
  470.0 1.4 copy-start.18
  471.5 1.7 copy-start.17
  473.3 1.7 copy-start.16

commit v5 on v4

--- a/solution.py
+++ b/solution.py
@@ -21,7 +21,7 @@
 
 
 def layout(lengths_row, token_count):
-    row_ends = jnp.cumsum(lengths_row)
+    row_ends = jnp.stack([jnp.sum(lengths_row[: i + 1]) for i in range(lengths_row.shape[0])])
     places = jnp.arange(token_count, dtype=jnp.int32)
     passed = (places[:, None] >= row_ends[None, :]).astype(jnp.int32)
     segment = jnp.sum(passed, axis=1)
@@ -113,6 +113,58 @@
     return exp_scores / jnp.sum(exp_scores, axis=-1, keepdims=True)
 
 
+class line_spread:
+    def __init__(self, quarters, z, own, slot, g_send, g_recv, f_send, f_recv, at, pair):
+        self.quarters, self.z, self.own, self.slot = (quarters, z, own, slot)
+        self.g_send, self.g_recv, self.f_send, self.f_recv = (g_send, g_recv, f_send, f_recv)
+        self.at, self.pair = (at, pair)
+
+    def inside(self, zz):
+        return (zz >= 0) & (zz < self.quarters)
+
+    def begin(self):
+        for i, side in enumerate((-1, 1)):
+            to = self.z + side
+
+            @pl.when(self.inside(to))
+            def _():
+                push(
+                    self.own, self.slot(to, self.z), self.g_send.at[self.quarters + i],
+                    self.g_recv.at[self.z], self.at(to),
+                )
+
+    def pass_on(self, distance):
+        for side in (-1, 1):
+            src = self.z + side * distance
+            to = self.z - side
+
+            @pl.when(self.inside(src))
+            def _():
+                ref = self.slot(self.z, src)
+                landed(ref, self.g_recv.at[src])
+
+                @pl.when(self.inside(to))
+                def _():
+                    push(ref, self.slot(to, src), self.g_send.at[src], self.g_recv.at[src], self.at(to))
+
+                push(ref, ref, self.f_send.at[src], self.f_recv.at[src], self.pair)
+
+    def end(self):
+        for i, side in enumerate((-1, 1)):
+
+            @pl.when(self.inside(self.z + side))
+            def _():
+                landed(self.own, self.g_send.at[self.quarters + i])
+
+        for src in range(self.quarters):
+            landed(self.own, self.f_send.at[src])
+            right, left = (src < self.z, src > self.z)
+
+            @pl.when((right & self.inside(self.z + 1)) | (left & self.inside(self.z - 1)))
+            def _():
+                landed(self.own, self.g_send.at[src])
+
+
 def gather_kernel(
     quarters,
     part_cols,
@@ -121,17 +173,26 @@
     gate,
     up,
     down,
-    grad,
+    out_grad,
     hidden,
     cosine,
     sine_tab,
     mask_bias,
-    aset_all,
+    aset_out,
     vec_sum,
     gate_all,
     up_all,
     down_all,
     grad_all,
+    h1_keep,
+    q_keep,
+    k_keep,
+    v_keep,
+    o_keep,
+    r1_keep,
+    h2_keep,
+    aset_all,
+    grad,
     h1_all,
     q_out,
     k_out,
@@ -151,9 +212,12 @@
     s_recv,
     g_send,
     g_recv,
+    f_send,
+    f_recv,
     p_send,
     p_recv,
     l_sem,
+    k_sem,
 ):
     z, p, c = here()
     dp = z * PLANE + p
@@ -175,6 +239,7 @@
 
     px, py = flipped(p, 1), flipped(p, 2)
     sent = []
+    grad[...] = out_grad[...].astype(BF)
 
     def send(*args):
         sent.append(push(*args))
@@ -237,9 +302,12 @@
             line(s, k)
     for copy in local:
         copy.start()
-    send(grad, grad_all.at[0, c], g_send.at[0, 1], g_recv.at[0, 1], pair)
-    for k in others:
-        send(grad, grad_all.at[k, c], g_send.at[k, 0], g_recv.at[k, 0], at(flipped(z, k), p))
+    push(grad, grad_all.at[0, c], f_send.at[z], f_recv.at[z], pair)
+    spread = line_spread(
+        quarters, z, grad, lambda zz, src: grad_all.at[moved(zz, src, quarters), c],
+        g_send, g_recv, f_send, f_recv, lambda zz: at(zz, p), pair,
+    )
+    spread.begin()
     fan(1, 0)
 
     local[0].wait()
@@ -266,6 +334,15 @@
     for k in range(quarters):
         rest(0, k)
     landed(h1_all.at[1 - c], p_recv.at[0])
+    kept = []
+
+    def keep(src, dst):
+        copy = pltpu.make_async_copy(src, dst, k_sem.at[len(kept)])
+        copy.start()
+        kept.append(copy)
+
+    keep(aset_all, aset_out)
+    keep(h1_all, h1_keep)
 
     def project(n):
         cols = slice(n * TILE, (n + 1) * TILE)
@@ -299,6 +376,8 @@
         halves[1, :, cols] = out[rows:]
 
     def swap():
+        for src, dst in ((q_out, q_keep), (k_out, k_keep), (v_out, v_keep), (o_out, o_keep)):
+            keep(src, dst)
         pair_out[...] = halves[1 - c].astype(BF)
         send(pair_out, pair_in, p_send.at[1], p_recv.at[1], pair)
 
@@ -307,7 +386,9 @@
         residual = hidden[...] + halves[c] + pair_in[...].astype(F32)
         r1_out[...] = residual
         gain = line_of(vec_sum[...], wide, wide)
+        keep(r1_out, r1_keep)
         h2_out[...] = (residual * lax.rsqrt(wide_mean(residual * residual) + NORM_EPS) * gain).astype(BF)
+        keep(h2_out, h2_keep)
 
     work = [functools.partial(project, n) for n in range(qkv_width // TILE)]
     work += [functools.partial(attend, head) for head in range(group_heads)]
@@ -316,40 +397,49 @@
     moves += [functools.partial(relay, s, 0) for s in (2, 3)]
     for k in others:
         moves += [functools.partial(fan, 2, k), functools.partial(relay, 1, k)]
+    moves.append(functools.partial(spread.pass_on, 1))
     for k in others:
         moves += [functools.partial(fan, 3, k), functools.partial(relay, 2, k)]
+    moves.append(functools.partial(spread.pass_on, 2))
     moves += [functools.partial(relay, 3, k) for k in others]
     for i in range(max(len(work), len(moves))):
         if i < len(moves):
             moves[i]()
         if i < len(work):
             work[i]()
-    for k in others:
-        slot = grad_all.at[k, c]
-        landed(slot, g_recv.at[k, 0])
-        send(slot, slot, g_send.at[k, 1], g_recv.at[k, 1], pair)
-    for k in range(quarters):
-        landed(grad_all.at[k, 1 - c], g_recv.at[k, 1])
+    spread.pass_on(quarters - 1)
+    for src in range(quarters):
+        landed(grad_all.at[moved(z, src, quarters), 1 - c], f_recv.at[src])
+    spread.end()
     for s in (1, 2, 3):
         for k in range(quarters):
             rest(s, k)
-    for copy in local[2:]:
+    for copy in local[2:] + kept:
         copy.wait()
     for copy in sent:
         copy.wait_send()
 
 
-def gather_all(aset, vec, gate, up, down, grad, hidden, cosine, sine_tab, mask_bias, quarters, part_cols):
+def gather_all(aset, vec, gate, up, down, out_grad, hidden, cosine, sine_tab, mask_bias, quarters, part_cols):
     shards = quarters * PLANE
-    depth, query_width = aset.shape[0], aset.shape[1]
+    depth = aset.shape[0]
     head_dim = cosine.shape[1]
     query_width = (aset.shape[1] - 2 * head_dim) // 2
     rows, width = hidden.shape
     dma = pltpu.SemaphoreType.DMA
-    hbm = pl.BlockSpec(memory_space=pl.ANY)
+    hbm = pl.BlockSpec(memory_space=pltpu.HBM)
     vmem = pl.BlockSpec(memory_space=pltpu.VMEM)
     shape = jax.ShapeDtypeStruct
     part = shape((shards, depth, part_cols), BF)
+    kept = (
+        ((2, rows, width), BF),
+        ((2 * rows, query_width), BF),
+        ((2 * rows, head_dim), BF),
+        ((2 * rows, head_dim), BF),
+        ((2 * rows, query_width), BF),
+        ((rows, width), F32),
+        ((rows, width), BF),
+    )
     return pl.pallas_call(
         functools.partial(gather_kernel, quarters, part_cols),
         out_shape=(
@@ -358,18 +448,14 @@
             part,
             part,
             part,
-            shape((quarters, 2) + grad.shape, BF),
-            shape((2, rows, width), BF),
-            shape((2 * rows, query_width), BF),
-            shape((2 * rows, head_dim), BF),
-            shape((2 * rows, head_dim), BF),
-            shape((2 * rows, query_width), BF),
-            shape((rows, width), F32),
-            shape((rows, width), BF),
-        ),
-        in_specs=[hbm] * 6 + [vmem] * 4,
-        out_specs=[vmem] * 2 + [hbm] * 4 + [vmem] * 7,
-        scratch_shapes=[
+            shape((quarters, 2, rows, width), BF),
+        )
+        + tuple(shape(*entry) for entry in kept),
+        in_specs=[hbm] * 5 + [vmem] * 5,
+        out_specs=[hbm, vmem] + [hbm] * 11,
+        scratch_shapes=[pltpu.VMEM((shards,) + aset.shape, BF), pltpu.VMEM((rows, width), BF)]
+        + [pltpu.VMEM(*entry) for entry in kept]
+        + [
             pltpu.VMEM((shards,) + vec.shape, BF),
             pltpu.VMEM((2, rows, width), F32),
             pltpu.VMEM((rows, width), BF),
@@ -380,16 +466,19 @@
             dma((3, quarters, 4)),
             dma((shards - 1,)),
             dma((shards - 1,)),
-            dma((quarters, 2)),
-            dma((quarters, 2)),
+            dma((quarters + 2,)),
+            dma((quarters,)),
+            dma((quarters,)),
+            dma((quarters,)),
             dma((2,)),
             dma((2,)),
             dma((6,)),
+            dma((8,)),
         ],
         compiler_params=pltpu.CompilerParams(
-            collective_id=0, has_side_effects=True, vmem_limit_bytes=40 * 2**20
+            collective_id=0, has_side_effects=True, vmem_limit_bytes=48 * 2**20
         ),
-    )(aset, vec, gate, up, down, grad, hidden, cosine, sine_tab, mask_bias)
+    )(aset, vec, gate, up, down, out_grad, hidden, cosine, sine_tab, mask_bias)
 
 
 def mlp_kernel(
@@ -446,9 +535,12 @@
     for copy in loads:
         copy.start()
     greet([spot(flipped(z, k), p, c) for k in range(1, quarters)] + [pair])
-    push(own, half(0, c), hp_send.at[0], hp_recv.at[0], pair)
-    for k in range(1, quarters):
-        push(own, half(k, c), h_send.at[k], h_recv.at[k], spot(flipped(z, k), p, c))
+    push(own, half(0, c), hp_send.at[z], hp_recv.at[z], pair)
+    spread = line_spread(
+        quarters, z, own, lambda zz, src: half(moved(zz, src, quarters), c),
+        h_send, h_recv, hp_send, hp_recv, lambda zz: spot(zz, p, c), pair,
+    )
+    spread.begin()
     if padded > part_cols:
         for i in range(3):
             w_all[i, :, part_cols:] = jnp.zeros((width, padded - part_cols), w_all.dtype)
@@ -470,13 +562,20 @@
         def _():
             push(other, d_line.at[k], l_send.at[k], l_recv.at[k], spot(moved(z, k, quarters), p, c))
 
-    def block(k, carry):
-        @pl.when(k > 0)
+    edge = (z == 0) | (z == quarters - 1)
+
+    def offset(step):
+        return jnp.where(edge | (step == 0), step, quarters - step)
+
+    def block(step, carry):
+        k = offset(step)
+
+        @pl.when(step > 0)
         def _():
-            landed(half(k, c), h_recv.at[k])
-            push(half(k, c), half(k, c), hp_send.at[k], hp_recv.at[k], pair)
-
-        landed(half(k, 1 - c), hp_recv.at[k])
+            spread.pass_on(step)
+
+        src = moved(z, k, quarters)
+        landed(half(k, 1 - c), hp_recv.at[src])
 
         def units(n, carry):
             cols = pl.ds(pl.multiple_of(n * TILE, TILE), TILE)
@@ -495,11 +594,11 @@
             d_up[k, :, cols] = (da * sg).astype(BF)
             return carry
 
-        lax.fori_loop(0, tiles, units, 0)
-
-        @pl.when(k > 0)
+        lax.fori_loop(0, tiles, units, 0, unroll=True)
+
+        @pl.when(step > 0)
         def _():
-            finish(k - 1)
+            finish(offset(step - 1))
 
         def model(n, carry):
             cols = pl.ds(pl.multiple_of(n * TILE, TILE), TILE)
@@ -523,20 +622,17 @@
         return carry
 
     lax.fori_loop(0, quarters, block, 0)
-    finish(quarters - 1)
+    finish(offset(quarters - 1))
 
     outs = (gate_out, up_out, down_out)
 
     def weight(n, carry):
         cols = pl.ds(pl.multiple_of(n * TILE, TILE), TILE)
         for i, (left, right) in enumerate(((h_all, d_gate), (h_all, d_up), (g_all, act))):
-            total = None
-            for k in range(quarters):
-                term = lax.dot_general(
-                    left[k, :, cols], right[k], (((0,), (0,)), ((), ())),
-                    preferred_element_type=F32,
-                )
-                total = term if total is None else total + term
+            total = dot_first(
+                left[:, :, cols].reshape(quarters * 2 * rows, TILE),
+                right[...].reshape(quarters * 2 * rows, padded),
+            )
             w_all[i, cols, :] = total.astype(BF)
             pltpu.make_async_copy(
                 w_all.at[i, cols, pl.ds(0, part_cols)], outs[i].at[cols, :], out_sem.at[1 + i, n]
@@ -553,13 +649,12 @@
         for i in range(3):
             tile = w_all.at[i, pl.ds(n * TILE, TILE), pl.ds(0, part_cols)]
             pltpu.make_async_copy(tile, outs[i].at[pl.ds(n * TILE, TILE), :], out_sem.at[1 + i, n]).wait()
+    spread.end()
     for k in range(quarters):
         pltpu.make_async_copy(y_slot.at[k], y_out.at[k], out_sem.at[0, k]).wait()
-        landed(half(k, c), hp_send.at[k])
         landed(y_part.at[k, 1 - c], y_send.at[k])
         landed(d_part.at[k, 1 - c], d_send.at[k])
         if k:
-            landed(own, h_send.at[k])
             landed(d_slot.at[k], l_send.at[k])
 
 
@@ -570,7 +665,7 @@
     padded = -(-part_cols // TILE) * TILE
     rows = own.shape[0]
     dma = pltpu.SemaphoreType.DMA
-    hbm = pl.BlockSpec(memory_space=pl.ANY)
+    hbm = pl.BlockSpec(memory_space=pltpu.HBM)
     vmem = pl.BlockSpec(memory_space=pltpu.VMEM)
     grad_w = jax.ShapeDtypeStruct((width, part_cols), bf)
     steps = max(quarters, width // TILE)
@@ -598,7 +693,8 @@
             pltpu.VMEM((quarters, rows, width), bf),
             pltpu.VMEM((quarters, rows, width), bf),
         ]
-        + [dma((quarters,))] * 10
+        + [dma((quarters + 2,))]
+        + [dma((quarters,))] * 9
         + [dma((5,)), dma((4, steps))],
         compiler_params=pltpu.CompilerParams(
             collective_id=2, has_side_effects=True, vmem_limit_bytes=60 * 2**20
@@ -606,68 +702,77 @@
     )(own, grads, gate, up, down)
 
 
-AHEAD = 1
+AHEAD = 2
 LAG = 1
-
-
-def reduce_kernel(
-    quarters,
-    gate,
-    up,
-    down,
-    y_half,
-    d_sum,
-    r1,
-    out_grad,
-    hidden,
-    h1_all,
-    q_in,
-    k_in,
-    v_in,
-    o_in,
-    aset_all,
-    vec_sum,
-    cosine,
-    sine_tab,
-    mask_bias,
-    small_sum,
-    attn_sum,
-    block_out,
-    grad_in,
-    gate_out,
-    up_out,
-    down_out,
-    small,
-    small_all,
-    staged,
-    attn_slots,
-    mlp_slots,
-    mlp_own,
-    attn_line,
-    y_line,
-    attn_grads,
-    da_all,
-    dr1,
-    do_all,
-    dqkv,
-    dk_sum,
-    dv_sum,
-    halves,
-    pair_out,
-    pair_in,
-    t_send,
-    t_recv,
-    z_send,
-    z_recv,
-    s_send,
-    s_recv,
-    y_send,
-    y_recv,
-    p_send,
-    p_recv,
-    l_sem,
-    own_sem,
-):
+PIECES = 2
+LINE_STEPS = (4, 9)
+
+
+INPUTS = 15
+
+
+def reduce_kernel(quarters, gate, up, down, *refs):
+    given, refs = (refs[:INPUTS], refs[INPUTS:])
+    (small_sum, attn_sum, block_out, grad_in, gate_out, up_out, down_out), refs = (refs[:7], refs[7:])
+    (
+        small,
+        small_all,
+        staged,
+        attn_slots,
+        mlp_slots,
+        mlp_own,
+        attn_line,
+        y_line,
+        attn_grads,
+        da_all,
+        dr1,
+        do_all,
+        dqkv,
+        dk_sum,
+        dv_sum,
+        halves,
+        pair_out,
+        pair_in,
+    ), refs = (refs[:18], refs[18:])
+    taken, refs = (refs[:INPUTS], refs[INPUTS:])
+    (
+        y_half,
+        d_sum,
+        r1,
+        out_grad,
+        vec_sum,
+        cosine,
+        sine_tab,
+        mask_bias,
+        aset_all,
+        q_in,
+        k_in,
+        v_in,
+        hidden,
+        h1_all,
+        o_in,
+    ) = taken
+    (
+        t_send,
+        t_recv,
+        z_send,
+        z_recv,
+        s_send,
+        s_recv,
+        y_send,
+        y_recv,
+        p_send,
+        p_recv,
+        l_sem,
+        own_sem,
+        in_sem,
+    ) = refs
+    loads = [pltpu.make_async_copy(src, dst, in_sem.at[i]) for i, (src, dst) in enumerate(zip(given, taken))]
+
+    def need(count):
+        while len(loads) > INPUTS - count:
+            loads.pop(0).wait()
+
     z, p, c = here()
     dp = z * PLANE + p
     pair = spot(z, p, 1 - c)
@@ -691,8 +796,8 @@
     for s, k in units:
         for i, kp in enumerate((0, 2 - k % 2)):
             pltpu.make_async_copy(source(s, k, kp), mlp_own.at[s - 1, k, i], own_sem.at[s - 1, k, i]).start()
-    first_y = pltpu.make_async_copy(y_half.at[0], y_line.at[0], l_sem.at[0])
-    first_y.start()
+    for copy in loads:
+        copy.start()
     masks = [(kz, kp) for kz in range(quarters) for kp in range(PLANE) if kz or kp]
     greet([spot(flipped(z, kz), flipped(p, kp), c) for kz, kp in masks] + [pair])
     sent = []
@@ -748,7 +853,45 @@
         for i in range(value.shape[1] // LANE):
             small[start + i : start + i + 1, :] = value[:, i * LANE : (i + 1) * LANE]
 
+    def line_terms(step):
+        for way, side in enumerate((1, -1)):
+            here_z = step if way == 0 else quarters - 1 - step
+            targets = range(quarters - 1, here_z, -1) if way == 0 else range(here_z)
+
+            @pl.when(z == here_z)
+            def _():
+                for target in targets:
+                    slot, mine = (y_line.at[way, target], y_half.at[here_z ^ target])
+                    if step:
+                        landed(slot, y_recv.at[way, target])
+                        slot[...] = (slot[...].astype(F32) + mine[...].astype(F32)).astype(BF)
+                    push(
+                        slot if step else mine, y_line.at[way, target], y_send.at[way, target],
+                        y_recv.at[way, target], spot(here_z + side, p, c),
+                    )
+
+    def line_total():
+        total = r1[...] + y_half[0].astype(F32)
+        block_out[...] = total
+        for way, first_z in ((0, 0), (1, quarters - 1)):
+
+            @pl.when(z != first_z)
+            def _():
+                landed(y_line.at[way, z], y_recv.at[way, z])
+                block_out[...] += y_line[way, z].astype(F32)
+
+    def line_end():
+        for at in range(quarters):
+
+            @pl.when(z == at)
+            def _():
+                for target in range(quarters):
+                    if target != at:
+                        way = 0 if target > at else 1
+                        landed(y_half.at[0], y_send.at[way, target])
+
     def norm_back():
+        need(5)
         residual, dh2 = (r1[...], d_sum[...])
         rho = lax.rsqrt(wide_mean(residual * residual) + NORM_EPS)
         n = residual * rho
@@ -761,6 +904,7 @@
 
     def heads_back(n):
         if n == 0:
+            need(INPUTS)
             landed(da_all.at[1 - c], p_recv.at[0])
         cols = slice(n * TILE, (n + 1) * TILE)
         weight = aset_all[:, :, qkv_width + n * TILE : qkv_width + (n + 1) * TILE]
@@ -830,8 +974,8 @@
     work += [functools.partial(weights_back, i) for i in range(shards // 4)] + [leave]
 
     mlp_count = len(units)
-    for k in others:
-        send(y_half.at[k], y_line.at[k], y_send.at[k], y_recv.at[k], spot(flipped(z, k), p, c))
+    need(1)
+    line_terms(0)
     units += [(0, k) for k in ks]
     for i in range(-AHEAD, len(units) + LAG):
         if i + AHEAD == mlp_count:
@@ -843,7 +987,9 @@
             relay(*units[i])
         if 0 <= i - LAG:
             last(*units[i - LAG])
-        for _ in range(2):
+        if i in LINE_STEPS:
+            line_terms(LINE_STEPS.index(i) + 1)
+        for _ in range(PIECES):
             if work:
                 work.pop(0)()
     for n, (kz, kp) in enumerate(masks):
@@ -854,12 +1000,7 @@
     staged[...] = total
     small_sum[c] = total
     send(staged, small_sum.at[c], s_send.at[len(masks)], s_recv.at[len(masks)], pair)
-    first_y.wait()
-    total = r1[...] + y_line[0].astype(F32)
-    for k in others:
-        landed(y_line.at[k], y_recv.at[k])
-        total = total + y_line[k].astype(F32)
-    block_out[...] = total
+    line_total()
     landed(small_sum.at[1 - c], s_recv.at[len(masks)])
     total = attn_slots[0, 1].astype(F32)
     for k in others:
@@ -869,24 +1010,26 @@
     for s in (1, 2, 3):
         for k in others:
             landed(outs[s].at[flipped(z, k)], z_recv.at[s, k])
+    line_end()
     for copy in local:
         copy.wait()
     for copy in sent:
         copy.wait_send()
 
 
-def reduce_all(quarters, mlp_grads, y_half, d_sum, r1, out_grad, hidden, h1_all, heads, aset_all, vec_sum, tables):
+def reduce_all(quarters, mlp_grads, inputs):
     shards = quarters * PLANE
     dma = pltpu.SemaphoreType.DMA
     depth, part_cols = mlp_grads[0].shape[1:]
+    y_half, _, r1, _, vec_sum, cosine, _, _, aset_all, q_in = inputs[:10]
     rows, width = r1.shape
-    tokens, query_width = heads[0].shape
-    head_dim = heads[1].shape[1]
+    tokens, query_width = q_in.shape
+    head_dim = cosine.shape[1]
     qkv_width = query_width + 2 * head_dim
     attn_shape = aset_all.shape[1:]
     vec_shape = vec_sum.shape
     vmem = pl.BlockSpec(memory_space=pltpu.VMEM)
-    hbm = pl.BlockSpec(memory_space=pl.ANY)
+    hbm = pl.BlockSpec(memory_space=pltpu.HBM)
     shape = jax.ShapeDtypeStruct
     quarter_out = shape((quarters, depth, part_cols), BF)
     return pl.pallas_call(
@@ -900,7 +1043,7 @@
             quarter_out,
             quarter_out,
         ),
-        in_specs=[hbm] * 4 + [vmem] * 14,
+        in_specs=[hbm] * (3 + INPUTS),
         out_specs=[vmem] * 4 + [hbm] * 3,
         scratch_shapes=[
             pltpu.VMEM(vec_shape, F32),
@@ -910,7 +1053,7 @@
             pltpu.VMEM((3, quarters, 3, depth, part_cols), BF),
             pltpu.VMEM((3, quarters, 2, depth, part_cols), BF),
             pltpu.VMEM((quarters,) + attn_shape, BF),
-            pltpu.VMEM((quarters, rows, width), BF),
+            pltpu.VMEM((2, quarters, rows, width), BF),
             pltpu.VMEM((shards,) + attn_shape, BF),
             pltpu.VMEM((2, rows, width), BF),
             pltpu.VMEM((rows, width), F32),
@@ -921,23 +1064,27 @@
             pltpu.VMEM((2, rows, width), F32),
             pltpu.VMEM((rows, width), BF),
             pltpu.VMEM((rows, width), BF),
+        ]
+        + [pltpu.VMEM(x.shape, x.dtype) for x in inputs]
+        + [
             dma((4, quarters, 3)),
             dma((4, quarters, 3)),
             dma((4, quarters)),
             dma((4, quarters)),
             dma((shards,)),
             dma((shards,)),
-            dma((quarters,)),
-            dma((quarters,)),
+            dma((2, quarters)),
+            dma((2, quarters)),
             dma((2,)),
             dma((2,)),
             dma((4,)),
             dma((3, quarters, 2)),
+            dma((INPUTS,)),
         ],
         compiler_params=pltpu.CompilerParams(
-            collective_id=1, has_side_effects=True, vmem_limit_bytes=60 * 2**20
+            collective_id=1, has_side_effects=True, vmem_limit_bytes=62 * 2**20
         ),
-    )(*mlp_grads, y_half, d_sum, r1, out_grad, hidden, h1_all, *heads, aset_all, vec_sum, *tables)
+    )(*mlp_grads, *inputs)
 
 
 def local(
@@ -985,8 +1132,8 @@
     shard = lax.axis_index("z") * PLANE + lax.axis_index("p")
 
     def placed(part):
-        whole = jnp.zeros((part.shape[0] * shards,), part.dtype)
-        return lax.dynamic_update_slice(whole, part, (shard * part.shape[0],)).reshape(-1, LANE)
+        mine = jnp.arange(shards, dtype=jnp.int32)[:, None] == shard
+        return jnp.where(mine, part[None, :], 0).astype(BF).reshape(-1, LANE)
 
     vec = jnp.concatenate(
         [placed(x) for x in (norm_attn, norm_mlp, b_query[0], b_key[0], b_value[0])], 0
@@ -997,7 +1144,7 @@
         w_gate,
         w_up,
         w_down.T,
-        out_grad.astype(BF),
+        out_grad,
         hidden_in,
         *tables,
         quarters,
@@ -1012,16 +1159,7 @@
     small_total, attn_part, block_out, grad_in, *quarter_grads = reduce_all(
         quarters,
         [g.reshape(shards, depth, part_width) for g in mlp_grads],
-        y_half,
-        dh2,
-        residual,
-        out_grad,
-        hidden_in,
-        h1_all,
-        heads,
-        aset_all,
-        vec_sum,
-        tables,
+        (y_half, dh2, residual, out_grad, vec_sum, *tables, aset_all, *heads[:3], hidden_in, h1_all, heads[3]),
     )
 
     def whole_rows(parts):

time: 480 us -> 447 us (0.931)
  Pallas kernels: 443 us -> 413 us
  local copies, waits for them, and re-layouts: 22.3 us -> 13.9 us
    pallas_call x1, Pallas kernels: 181 us -> 159 us  [reduce_all(): pl.pallas_call(functools.partial(reduce_kernel, quarters), out_shape=(sha...]
    pallas_call x1, Pallas kernels: 115 us -> 107 us  [mlp_all(): pl.pallas_call(functools.partial(mlp_kernel, quarters, hidden), out_shape...]
    unnamed x45 -> x37, local copies, waits for them, and re-layouts: 12.7 us -> 7.92 us
where the time goes in v5:
time: 447 us; the launch traced here: 442 us
  Pallas kernels  413 us (92%)
  local copies, waits for them, and re-layouts  13.9 us (3%)
  other arithmetic  13.8 us (3%)
    pallas_call x1, Pallas kernels, reduce_all(): pl.pallas_call(functools.partial(reduce_kernel, quarters), out_shape=(sha...  159 us
    pallas_call x1, Pallas kernels, gather_all(): pl.pallas_call(functools.partial(gather_kernel, quarters, part_cols), out...  147 us
    pallas_call x1, Pallas kernels, mlp_all(): pl.pallas_call(functools.partial(mlp_kernel, quarters, hidden), out_shape...  107 us

profile of v5, /device:TPU:0, one launch (start us, length us, event | category | flops | bytes accessed | tf_op | source)
XLA Modules:
  0.0 441.8 jit_solution(1558793191803782863)
XLA Ops:
  0.6 0.0 copy-start.4
  0.7 0.0 copy-start.3
  0.7 1.4 slice_reduce_fusion.1
  2.1 1.3 reduce_sum.50
  3.4 2.0 pad_add_fusion
  5.4 0.7 convert_reduce_fusion
  6.2 0.7 broadcast_select_fusion.2
  6.9 0.1 select_n.59
  7.0 0.8 broadcast_select_fusion.3
  7.7 0.1 select_n.57
  7.8 0.1 select_n.55
  7.9 0.7 broadcast_select_fusion
  8.7 0.1 select_n.63
  8.8 0.1 select_n.61
  8.9 0.2 concatenate.22.vec
  9.0 0.0 copy-start.5
  9.0 1.1 pad_maximum_fusion.aset
  10.2 0.8 fusion.2
  10.9 0.2 pad_maximum_fusion.1
  11.1 0.0 copy-start.1
  11.1 0.0 copy-start.2
  11.1 0.1 fusion.1.mask_bias.refs_7_
  11.3 0.0 copy-done.4
  11.3 0.0 copy-done.3
  11.3 0.0 copy-done.5
  11.3 0.0 copy-start
  11.3 147.2 %shard_map.254 = (bf16[16,96,1792]{2,1,0:T(8,128)(2,1)}, f32[32,128]{1,0:T(8,128)S(1)}, bf16[16,96,1152]{2,1,0:T(8,128)(2,1)}, bf16[16,96,1152]{2,1,0:T(8,128)(2...) custom-call(bf16[96,1792]{1,0:T(8,128)(2,1)S(1)} %pad_maximum_fusion, ...), custom_call_target="tpu_custom_call" | custom-call | tf_op jit(solution)/shard_map/pallas_call | solution.py:443
  158.5 0.0 copy-done.1
  158.6 0.0 copy-done.2
  158.6 0.0 copy-done
  158.6 0.0 copy-start.6
  158.6 0.8 copy-done.6
  159.4 0.0 copy-start.7
  159.4 0.8 copy-done.7
  160.2 0.0 copy-start.8
  160.2 0.8 copy-done.8
  161.0 0.6 copy-done.9
  161.7 0.6 copy-done.10
  162.3 106.9 %shard_map.255 = (bf16[4,192,1536]{2,1,0:T(8,128)(2,1)}, f32[192,1536]{1,0:T(8,128)}, bf16[1536,1152]{1,0:T(8,128)(2,1)}, bf16[1536,1152]{1,0:T(8,128)(2,1)}, bf16[1536,1152]{1,0:T(8,128)(2,1)}) custom-call(bf16[192,1536]{1,0:T(8,128)(2,1)} %copy-done.8, bf16[4,384,1536]{2,1,0:T(8,128)(2,1)} %bitcast.50, bf16[1536,1152]{1,0:T(8,128)(2,1)} %bitcast.51, ...), custom_call_target="tpu_custom_call" | custom-call | tf_op jit(solution)/shard_map/pallas_call | solution.py:672
  269.2 0.0 copy-done.11
  269.2 159.0 %shard_map.256 = (f32[2,32,128]{2,1,0:T(8,128)}, f32[96,1792]{1,0:T(8,128)}, f32[192,1536]{1,0:T(8,128)}, f32[192,1536]{1,0:T(8,128)}, bf16[4,96,1152]{2,1,0:T(8...) custom-call(bf16[16,96,1152]{2,1,0:T(8,128)(2,1)} %bitcast.54, bf16[16,96,1152]{2,1,0:T(8,128)(2,1)} %bitcast.55, ...), custom_call_target="tpu_custom_call" | custom-call | tf_op jit(solution)/shard_map/pallas_call | solution.py:1035
  428.3 0.0 copy-start.16
  428.3 0.9 copy.31
  429.1 0.6 fusion.4
  429.7 0.6 slice.121
  430.3 0.6 fusion.5
  430.9 1.5 fusion.3
  432.4 1.9 slice_bitcast_fusion
  434.3 0.0 copy-done.16
  434.3 0.1 slice_bitcast_fusion.12
  434.4 0.0 copy-start.15
  434.4 1.3 maximum_convert_fusion
  435.7 0.1 copy-done.15
  435.8 0.1 slice_bitcast_fusion.8
  435.9 0.0 copy-start.14
  435.9 1.3 maximum_convert_fusion.1
  437.2 0.1 copy-done.14
  437.3 0.1 slice_bitcast_fusion.4
  437.4 0.0 copy-start.13
  437.4 1.3 convert_bitcast_fusion
  438.7 0.4 copy-done.13
  439.1 1.0 copy.34
  440.1 0.7 copy-done.12
  440.8 1.0 copy.35
  (11 shorter events, 0.1 us)
Async XLA Ops:
  0.6 10.6 %copy-start.4 = (bf16[96,4480]{1,0:T(8,128)(2,1)S(1)}, bf16[96,4480]{1,0:T(8,128)(2,1)}, u32[]{:S(2)}) copy-start(bf16[96,4480]{1,0:T(8,128)(2,1)} %up.1) | copy-start | bytes 2580484
  0.7 10.6 %copy-start.3 = (bf16[96,4480]{1,0:T(8,128)(2,1)S(1)}, bf16[96,4480]{1,0:T(8,128)(2,1)}, u32[]{:S(2)}) copy-start(bf16[96,4480]{1,0:T(8,128)(2,1)} %gate.1) | copy-start | bytes 2580484
  9.0 2.2 copy-start.5
  11.1 147.4 %copy-start.1 = (f32[384,128]{1,0:T(8,128)}, f32[384,128]{1,0:T(8,128)S(1)}, u32[]{:S(2)}) copy-start(f32[384,128]{1,0:T(8,128)S(1)} %get-tuple-element.93.cosine.refs_5_) | copy-start | bytes 589828
  11.1 147.4 %copy-start.2 = (f32[384,128]{1,0:T(8,128)}, f32[384,128]{1,0:T(8,128)S(1)}, u32[]{:S(2)}) copy-start(f32[384,128]{1,0:T(8,128)S(1)} %get-tuple-element.94.sine_tab.refs_6_) | copy-start | bytes 589828
  11.3 147.3 %copy-start = (f32[384,384]{1,0:T(8,128)}, f32[384,384]{1,0:T(8,128)S(1)}, u32[]{:S(2)}) copy-start(f32[384,384]{1,0:T(8,128)S(1)} %fusion.1.mask_bias.refs_7_) | copy-start | bytes 1769476
  158.6 0.8 copy-start.6
  159.4 0.8 copy-start.7
  160.2 0.8 copy-start.8
  161.0 0.6 copy-start.9
  161.7 0.6 copy-start.10
  162.3 106.9 %copy-start.11 = (f32[32,128]{1,0:T(8,128)}, f32[32,128]{1,0:T(8,128)S(1)}, u32[]{:S(2)}) copy-start(f32[32,128]{1,0:T(8,128)S(1)} %get-tuple-element.50.refs_4_) | copy-start | bytes 49156
  428.3 6.0 %copy-start.16 = (bf16[4,96,1152]{2,1,0:T(8,128)(2,1)S(1)}, bf16[4,96,1152]{2,1,0:T(8,128)(2,1)}, u32[]{:S(2)}) copy-start(bf16[4,96,1152]{2,1,0:T(8,128)(2,1)} %get-tuple-element.61) | copy-start | bytes 2654212
  434.4 1.4 copy-start.15
  435.9 1.4 copy-start.14
  437.4 1.7 copy-start.13
  439.1 1.7 copy-start.12
